TPU v7x, 128 devices: a whole 4x4x4 slice. The times are simulated.
128 devices in a mesh: mem: 32 (over z, y, core), tp: 4 (over x).
Axes of the slice: x: 4, y: 4, z: 4, core: 2. Of those that a mesh axis runs over, the one named last changes fastest.
Arguments:
- hidden_states: bfloat16 [8192, 2048], P('mem', 'tp'), may hold values from -6 to 6
- entry_rescale_coefficients: bfloat16 [2048], replicated, may hold values from 0.099609375 to 1.8984375
- probe_projection_matrix: bfloat16 [2048, 2048], P(None, 'tp'), may hold values from -0.125 to 0.125
- address_projection_matrix: bfloat16 [2048, 2048], P(None, 'tp'), may hold values from -0.125 to 0.125
- content_projection_matrix: bfloat16 [2048, 2048], P(None, 'tp'), may hold values from -0.125 to 0.125
- final_projection_matrix: bfloat16 [2048, 2048], P('tp'), may hold values from -0.125 to 0.125
- archive_address_vectors: bfloat16 [131072, 2048], P('mem', 'tp'), may hold values from -6 to 6
- archive_content_vectors: bfloat16 [131072, 2048], P('mem', 'tp'), may hold values from -6 to 6
- reader_sharpness: float32 [16], P('tp'), may hold values from 16 to 48
- reader_mixing_bias: float32 [16], P('tp'), may hold values from 0.5 to 2
- retrieval_assignments: int32 [64, 8], replicated, may hold values from 0 to 255, as said below
- document_labels: int32 [8192], replicated, may hold values from 0 to 63, never falling along the last dimension, each value on 1 to 512 neighbouring positions
Outputs:
- layer_out: bfloat16 [8192, 2048], P(('mem', 'tp'))
Inputs may be any that keep to these rules, and one draw needn't show every extreme that they name: `retrieval_assignments`: the 8 ids of each query block differ. Block m is held by index m // 8 of mem. Of the 16 ids of the query blocks on one index of mem, at most 1 name blocks held by one index of mem, and in every draw some index of mem is named exactly 1 times by the query blocks of every index.
All inputs are finite; a program needn't handle non-finite values.
Results may differ from a plain program's by a relative error of at most 0.015.
Values may be sent and summed in bfloat16 or wider, within the bound.
No kernel may reach another device: no remote copies, remote signals or barrier semaphores. Data moves between devices by JAX's collectives and lax.ppermute only.
A program may use at most 128 MiB of HBM per device.

v0:
```python
import jax
import jax.numpy as jnp
from jax import lax
from jax.sharding import PartitionSpec as P

QB = 128
MB = 512
LOCAL = 256


def from_behind(value, axis, by):
    count = lax.axis_size(axis)
    pairs = [(i, i + by) for i in range(count) if 0 <= i + by < count]
    return lax.ppermute(value, axis, pairs)


def as_sent(value):

    def short(part):
        return part.astype(jnp.bfloat16) if part.dtype == jnp.float32 else part

    return jax.tree.map(short, value)


def unit_heads(matrix, reader_number):
    row_count = matrix.shape[0]
    shaped = matrix.astype(jnp.float32).reshape(row_count, reader_number, -1)
    dot_product_multiplier = lax.rsqrt(jnp.mean(shaped * shaped, axis=-1, keepdims=True) + 1e-06)
    return (shaped * dot_product_multiplier).astype(jnp.bfloat16)


def block_attention(query_items, block_ids, memory_keys, memory_values, dot_product_multiplier):
    item_count, reader_number, block_rows, reader_dimension = query_items.shape
    slot_count = block_ids.shape[1]
    pair_total = item_count * slot_count
    group_size = 1
    for divisor in range(1, 9):
        if pair_total % divisor == 0:
            group_size = divisor
    turn_count = pair_total // group_size
    id_groups = block_ids.reshape(turn_count, group_size)

    def one_group(item):
        turn, picked = item
        query_list = []
        key_list = []
        value_list = []
        for member in range(group_size):
            which = jnp.maximum(picked[member], 0)
            source_item = (turn * group_size + member) // slot_count
            query_list.append(lax.dynamic_index_in_dim(query_items, source_item, 0, keepdims=False))
            key_list.append(lax.dynamic_index_in_dim(memory_keys, which, 0, keepdims=False))
            value_list.append(lax.dynamic_index_in_dim(memory_values, which, 0, keepdims=False))
        query_rows = jnp.stack(query_list)
        key_rows = jnp.stack(key_list)
        value_rows = jnp.stack(value_list)
        present = (picked >= 0).astype(jnp.float32)
        scores = (
            jnp.einsum("ghqd,ghmd->ghqm", query_rows, key_rows, preferred_element_type=jnp.float32)
            * dot_product_multiplier[None, :, None, None]
        )
        weights = jnp.exp(scores) * present[:, None, None, None]
        totals = jnp.sum(weights, axis=-1)
        numer = jnp.einsum(
            "ghqm,ghmd->ghqd",
            weights.astype(jnp.bfloat16),
            value_rows,
            preferred_element_type=jnp.float32,
        )
        absent = 1.0 - present
        part_out = (numer / (totals + absent[:, None, None])[..., None]).astype(jnp.bfloat16)
        return (part_out, totals.astype(jnp.bfloat16))

    part_out, part_den = lax.map(one_group, (jnp.arange(turn_count, dtype=jnp.int32), id_groups))
    return (
        part_out.reshape(item_count, slot_count, reader_number, block_rows, reader_dimension),
        part_den.reshape(item_count, slot_count, reader_number, block_rows),
    )


def merge_partials(part_out, part_den, assign):
    weights = assign[:, :, None, None] * part_den.astype(jnp.float32)[:, None, :, :]
    totals = jnp.sum(weights, axis=0)
    numer = jnp.einsum("sbhq,shqd->bhqd", weights, part_out.astype(jnp.float32))
    merged = numer / totals[..., None]
    return jnp.transpose(merged, (0, 2, 1, 3))


def body(
    hidden_states,
    entry_rescale_coefficients,
    probe_projection_matrix,
    address_projection_matrix,
    content_projection_matrix,
    final_projection_matrix,
    archive_address_vectors,
    archive_content_vectors,
    reader_sharpness,
    reader_mixing_bias,
    retrieval_assignments,
    document_labels,
):
    reader_number = reader_sharpness.shape[0]
    feature_width = probe_projection_matrix.shape[1]
    reader_dimension = feature_width // reader_number
    gathered = lax.all_gather(hidden_states, "tp", axis=1, tiled=True)
    row_count = gathered.shape[0]
    widened = gathered.astype(jnp.float32)
    normed = (
        widened
        * lax.rsqrt(jnp.mean(widened * widened, axis=-1, keepdims=True) + 1e-05)
        * entry_rescale_coefficients.astype(jnp.float32)
    ).astype(jnp.bfloat16)
    queries = unit_heads(
        jnp.dot(normed, probe_projection_matrix, preferred_element_type=jnp.float32), reader_number
    )
    local_keys = unit_heads(
        jnp.dot(normed, address_projection_matrix, preferred_element_type=jnp.float32),
        reader_number,
    )
    local_values = (
        jnp.dot(normed, content_projection_matrix, preferred_element_type=jnp.float32)
        .astype(jnp.bfloat16)
        .reshape(row_count, reader_number, reader_dimension)
    )
    dot_product_multiplier = reader_sharpness / reader_dimension
    before_keys, before_values = from_behind((local_keys, local_values), "mem", 1)
    my_index = lax.axis_index("mem")
    first_row = my_index * row_count
    segment_own = lax.dynamic_slice_in_dim(document_labels, first_row, row_count, 0)
    segment_before = lax.dynamic_slice_in_dim(
        document_labels, jnp.maximum(first_row - row_count, 0), row_count, 0
    )
    segment_before = jnp.where(my_index > 0, segment_before, -1)
    segment_keys = jnp.concatenate([segment_before, segment_own], axis=0)
    query_place = jnp.arange(row_count, dtype=jnp.int32) + row_count
    key_place = jnp.arange(2 * row_count, dtype=jnp.int32)
    allowed = (
        (key_place[None, :] <= query_place[:, None])
        & (query_place[:, None] - key_place[None, :] < LOCAL)
        & (segment_own[:, None] == segment_keys[None, :])
    )
    window_keys = jnp.concatenate([before_keys, local_keys], axis=0)
    window_values = jnp.concatenate([before_values, local_values], axis=0)
    scores = (
        jnp.einsum("qhd,khd->hqk", queries, window_keys, preferred_element_type=jnp.float32)
        * dot_product_multiplier[:, None, None]
    )
    weights = jnp.exp(scores) * allowed[None].astype(jnp.float32)
    totals = jnp.sum(weights, axis=-1)
    numer = jnp.einsum(
        "hqk,khd->qhd",
        weights.astype(jnp.bfloat16),
        window_values,
        preferred_element_type=jnp.float32,
    )
    local_out = numer / jnp.transpose(totals)[:, :, None]
    memory_keys = jnp.transpose(
        unit_heads(archive_address_vectors, reader_number).reshape(
            -1, MB, reader_number, reader_dimension
        ),
        (0, 2, 1, 3),
    )
    memory_values = jnp.transpose(
        archive_content_vectors.reshape(-1, MB, reader_number, reader_dimension), (0, 2, 1, 3)
    )
    blocks_here = memory_keys.shape[0]
    topk_count = retrieval_assignments.shape[1]
    source_count = lax.axis_size("mem")
    own_blocks = row_count // QB
    capacity = 2 * own_blocks * topk_count // source_count
    query_blocks = jnp.transpose(
        queries.reshape(own_blocks, QB, reader_number, reader_dimension), (0, 2, 1, 3)
    )
    slot_range = jnp.arange(capacity, dtype=jnp.int32)
    everyone = lax.all_gather(query_blocks, "mem", axis=0, tiled=True)
    mine_all = retrieval_assignments // blocks_here == my_index
    order_all = jnp.cumsum(mine_all.astype(jnp.int32), axis=1) - 1
    matched = mine_all[:, None, :] & (order_all[:, None, :] == slot_range[None, :, None])
    located = jnp.any(matched, axis=2)
    picked = jnp.sum(
        jnp.where(matched, (retrieval_assignments % blocks_here)[:, None, :], 0), axis=2
    )
    block_ids = jnp.where(located, picked, -1)
    part_out, part_den = block_attention(
        everyone, block_ids, memory_keys, memory_values, dot_product_multiplier
    )
    part_out = part_out.reshape(
        source_count, own_blocks * capacity, reader_number, QB, reader_dimension
    )
    part_den = part_den.reshape(source_count, own_blocks * capacity, reader_number, QB)
    assign = jnp.tile(
        jnp.repeat(jnp.eye(own_blocks, dtype=jnp.float32), capacity, axis=0), (source_count, 1)
    )
    back_out, back_den = (
        lax.all_to_all(as_sent(part_out), "mem", split_axis=0, concat_axis=0, tiled=True).astype(
            part_out.dtype
        ),
        lax.all_to_all(as_sent(part_den), "mem", split_axis=0, concat_axis=0, tiled=True).astype(
            part_den.dtype
        ),
    )
    memory_out = merge_partials(
        back_out.reshape(-1, reader_number, QB, reader_dimension),
        back_den.reshape(-1, reader_number, QB),
        assign,
    )
    memory_out = memory_out.reshape(row_count, reader_number, reader_dimension)
    gate_value = jax.nn.sigmoid(reader_mixing_bias)[None, :, None]
    mixed = (
        (gate_value * memory_out + (1.0 - gate_value) * local_out)
        .astype(jnp.bfloat16)
        .reshape(row_count, feature_width)
    )
    summed = lax.psum_scatter(
        jnp.dot(mixed, final_projection_matrix, preferred_element_type=jnp.float32).astype(
            jnp.bfloat16
        ),
        "tp",
        scatter_dimension=0,
        tiled=True,
    )
    return summed


def solution(mesh):
    placed = (
        P("mem", "tp"),
        P(),
        P(None, "tp"),
        P(None, "tp"),
        P(None, "tp"),
        P("tp", None),
        P("mem", "tp"),
        P("mem", "tp"),
        P("tp"),
        P("tp"),
        P(),
        P(),
    )
    return jax.shard_map(
        body, mesh=mesh, in_specs=placed, out_specs=P(("mem", "tp"), None), check_vma=False
    )
```

profile of v0, /device:TPU:0, one launch (start us, length us, event | category | flops | bytes accessed | tf_op | source)
XLA Modules:
  0.0 542.2 jit_solution(10444962819517664487)
XLA Ops:
  8.0 27.5 %all-gather.3.cloned.1.call-done = bf16[256,2048]{1,0:T(8,128)(2,1)} async-done(((bf16[256,512]{1,0:T(8,128)(2,1)}), bf16[256,2048]{1,0:T(8,128)(2,1)}) %all-gather.3.cloned.1.call-update) | async-done | bytes 1048592 | tf_op jit(solution)/shard_map/all_gather | solution.py:106
  35.5 1.5 fusion.10
  37.0 2.7 fusion.51
  40.7 1.4 reshape.277
  43.7 8.4 %reshape.288 = f32[8,512,4,128]{3,2,1,0:T(4,128)} reshape(bf16[4096,512]{1,0:T(8,128)(2,1)} %param.20) | data formatting | bytes 12582912 | tf_op jit(solution)/shard_map/reshape | solution.py:27
  52.1 8.1 %copy.87 = f32[8,512,4,128]{1,0,3,2:T(8,128)} copy(f32[8,512,4,128]{3,2,1,0:T(4,128)} %reshape.288) | data formatting | bytes 16777216 | tf_op jit(solution)/shard_map/reshape | solution.py:27
  60.2 6.6 %convert_multiply_fusion.2 = f32[4096,512]{1,0:T(8,128)} fusion(bf16[4096,512]{1,0:T(8,128)(2,1)} %param.20), kind=kLoop, calls=%fused_computation.49 | loop fusion | flops 4194304 | bytes 12582912 | tf_op jit(solution)/shard_map/mul | solution.py:28
  66.8 10.1 %mul.184 = f32[4096,4,128]{2,1,0:T(4,128)} reshape(f32[4096,512]{1,0:T(8,128)} %convert_multiply_fusion.2) | data formatting | bytes 16777216 | tf_op jit(solution)/shard_map/mul | solution.py:28
  76.9 9.9 %reduce_sum.82 = f32[4096,4]{1,0:T(8,128)} reduce(f32[4096,4,128]{2,1,0:T(4,128)} %mul.184, f32[]{:T(128)} %constant.368.clone.1), dimensions={2}, to_apply=%region_5.6 | reduce | flops 2080768 | bytes 8454148 | tf_op jit(solution)/shard_map/reduce_sum | solution.py:28
  86.8 3.2 add_rsqrt_fusion
  90.0 2.4 copy.94
  92.4 6.7 %fusion.9 = bf16[8,4,512,128]{2,0,3,1:T(8,128)(2,1)} fusion(f32[8,512,4,128]{1,0,3,2:T(8,128)} %copy.87, f32[8,512,4]{1,0,2:T(8,128)S(1)} %bitcast.111), kind=kLoop, calls=%fused_computation.39 | loop fusion | flops 4194304 | bytes 12648448 | tf_op jit(solution)/shard_map/transpose | solution.py:158
  99.2 7.9 %copy.74 = bf16[8,4,512,128]{3,2,1,0:T(8,128)(2,1)} copy(bf16[8,4,512,128]{2,0,3,1:T(8,128)(2,1)} %fusion.9) | data formatting | bytes 8388608 | tf_op jit(solution)/shard_map/while | solution.py:74
  107.1 6.9 %reshape.289 = bf16[8,512,4,128]{3,2,1,0:T(4,128)(2,1)} reshape(bf16[4096,512]{1,0:T(8,128)(2,1)} %param.21) | data formatting | bytes 8388608 | tf_op jit(solution)/shard_map/reshape | solution.py:165
  114.0 5.2 copy.107
  119.2 235.6 %while.17 = (s32[]{:T(128)}, bf16[8,8,4,128,128]{4,3,2,1,0:T(8,128)(2,1)}, bf16[8,8,4,128]{3,2,1,0:T(4,128)(2,1)}, s32[8]{0:T(128)S(1)}, bf16[64,4,128,128]{3,2,...) while((s32[]{:T(128)}, ...), condition=%wide.region_8.9_spmd, body=%wide.region_6.8_spmd.sunk | while | flops 1087377408 | bytes 63005876 | solution.py:74
  143.5 1.7 fusion.80
  145.3 2.9 bitcast_dynamic-update-slice_fusion.4
  173.0 1.7 fusion.80
  174.8 2.8 bitcast_dynamic-update-slice_fusion.4
  202.4 1.7 fusion.80
  204.2 2.8 bitcast_dynamic-update-slice_fusion.4
  231.8 1.7 fusion.80
  233.6 2.8 bitcast_dynamic-update-slice_fusion.4
  261.3 1.7 fusion.80
  263.1 2.8 bitcast_dynamic-update-slice_fusion.4
  290.7 1.7 fusion.80
  292.5 2.8 bitcast_dynamic-update-slice_fusion.4
  320.1 1.7 fusion.80
  322.0 2.8 bitcast_dynamic-update-slice_fusion.4
  349.6 1.7 fusion.80
  351.4 2.8 bitcast_dynamic-update-slice_fusion.4
  354.8 7.3 %all-to-all-start.1 = ((bf16[32,2,4,128]{3,2,1,0:T(4,128)(2,1)}), bf16[32,2,4,128]{3,2,1,0:T(4,128)(2,1)S(1)}, u32[]{:S(2)}, u32[]{:S(2)}) async-start(bf16[32,2,4,128]{3,2,1,0:T(4,128)(2,1)} %bitcast.19), calls=%async_computation.1 | async-start | bytes 131072 | tf_op jit(solution)/shard_map/all_to_all | solution.py:199
  362.2 16.3 %copy.76 = bf16[32,2,4,128,128]{4,1,3,2,0:T(2,128)(2,1)} copy(bf16[32,2,4,128,128]{4,3,2,1,0:T(8,128)(2,1)} %bitcast.108) | data formatting | bytes 16777216 | tf_op jit(solution)/shard_map/reshape;reshape | solution.py:188
  379.1 7.3 %all-to-all-start = ((bf16[32,2,4,128,128]{4,1,3,2,0:T(2,128)(2,1)}), bf16[32,2,4,128,128]{4,1,3,2,0:T(2,128)(2,1)}, u32[]{:S(2)}, u32[]{:S(2)}) async-start(bf16[32,2,4,128,128]{4,1,3,2,0:T(2,128)(2,1)} %copy.76), calls=%async_computation | async-start | bytes 16777216 | tf_op jit(solution)/shard_map/all_to_all | solution.py:196
  389.1 3.1 fusion.48
  393.9 1.3 fusion.24
  395.2 2.8 collective-permute-start.1
  398.1 3.4 convolution_convert_fusion.1
  401.5 1.8 copy.90
  403.2 3.7 collective-permute-start
  407.3 2.8 fusion.13
  410.9 81.4 %all-to-all-done = bf16[32,2,4,128,128]{4,1,3,2,0:T(2,128)(2,1)} async-done(((bf16[32,2,4,128,128]{4,1,3,2,0:T(2,128)(2,1)}), bf16[32,2,4,128,128]{4,1,3,2,0:T(2,128)(2,1)}, u32[]{:S(2)}, u32[]{:S(2)}) %all-to-all-start) | async-done | bytes 8388640 | tf_op jit(solution)/shard_map/all_to_all | solution.py:196
  492.3 10.2 %copy.77 = bf16[32,2,4,128,128]{4,1,0,3,2:T(2,128)(2,1)S(1)} copy(bf16[32,2,4,128,128]{4,1,3,2,0:T(2,128)(2,1)} %all-to-all-done) | data formatting | bytes 16777216 | tf_op jit(solution)/shard_map/all_to_all | solution.py:196
  502.6 2.3 fusion.22
  505.9 2.4 fusion.18
  508.3 1.7 convolution_convert_fusion
  510.0 25.7 %reduce-scatter.2.cloned.1.call-done = bf16[64,2048]{1,0:T(8,128)(2,1)} async-done(((bf16[256,2048]{1,0:T(8,128)(2,1)}), bf16[64,2048]{1,0:T(8,128)(2,1)}) %reduce-scatter.2.cloned.1.call-update) | async-done | bytes 262160 | tf_op jit(solution)/shard_map/reduce_scatter | solution.py:215
  (324 shorter events, 163.0 us)
Async XLA Ops:
  6.5 501.8 %copy-start = (bf16[512,2048]{1,0:T(8,128)(2,1)S(1)}, bf16[512,2048]{1,0:T(8,128)(2,1)}, u32[]{:S(2)}) copy-start(bf16[512,2048]{1,0:T(8,128)(2,1)} %param.19) | copy-start | bytes 6291460
  6.5 28.9 %all-gather.3.cloned.1.call-start = ((), (), s32[]{:S(2)}) async-start(), calls=%async_computation.3 | async-start | bytes 1310720 | tf_op jit(solution)/shard_map/all_gather | solution.py:106
  7.3 112.0 %all-gather.5.cloned.1.call-start = ((), (), s32[]{:S(2)}) async-start(), calls=%async_computation.4 | async-start | bytes 8650752 | tf_op jit(solution)/shard_map/all_gather | solution.py:176
  37.0 352.1 %copy-start.11 = (f32[256]{0:T(256)}, f32[256]{0:T(256)S(1)}, u32[]{:S(2)}) copy-start(f32[256]{0:T(256)S(1)} %add_rsqrt_fusion.3) | copy-start | bytes 3076
  37.0 6.5 %copy-start.10 = (s32[64,8]{0,1:T(8,128)S(1)}, s32[64,8]{0,1:T(8,128)}, u32[]{:S(2)}) copy-start(s32[64,8]{0,1:T(8,128)} %param.24) | copy-start | bytes 6148
  39.7 0.8 copy-start.4
  40.7 11.4 %copy-start.2 = (f32[256,4,128]{2,1,0:T(4,128)}, f32[256,4,128]{2,1,0:T(4,128)S(1)}, u32[]{:S(2)}) copy-start(f32[256,4,128]{2,1,0:T(4,128)S(1)} %reshape.278) | copy-start | bytes 1572868
  114.0 5.2 copy-start.12
  127.1 14.6 %copy-start.1 = (bf16[8,4,512,128]{3,2,1,0:T(8,128)(2,1)S(1)}, bf16[8,4,512,128]{3,2,1,0:T(8,128)(2,1)}, u32[]{:S(2)}) copy-start(bf16[8,4,512,128]{3,2,1,0:T(8,128)(2,1)} %get-tuple-element.459) | copy-start | bytes 12582916 | tf_op jit(solution)/shard_map/while
  156.6 14.6 %copy-start.1 = (bf16[8,4,512,128]{3,2,1,0:T(8,128)(2,1)S(1)}, bf16[8,4,512,128]{3,2,1,0:T(8,128)(2,1)}, u32[]{:S(2)}) copy-start(bf16[8,4,512,128]{3,2,1,0:T(8,128)(2,1)} %get-tuple-element.459) | copy-start | bytes 12582916 | tf_op jit(solution)/shard_map/while
  186.0 14.6 %copy-start.1 = (bf16[8,4,512,128]{3,2,1,0:T(8,128)(2,1)S(1)}, bf16[8,4,512,128]{3,2,1,0:T(8,128)(2,1)}, u32[]{:S(2)}) copy-start(bf16[8,4,512,128]{3,2,1,0:T(8,128)(2,1)} %get-tuple-element.459) | copy-start | bytes 12582916 | tf_op jit(solution)/shard_map/while
  215.4 14.6 %copy-start.1 = (bf16[8,4,512,128]{3,2,1,0:T(8,128)(2,1)S(1)}, bf16[8,4,512,128]{3,2,1,0:T(8,128)(2,1)}, u32[]{:S(2)}) copy-start(bf16[8,4,512,128]{3,2,1,0:T(8,128)(2,1)} %get-tuple-element.459) | copy-start | bytes 12582916 | tf_op jit(solution)/shard_map/while
  244.9 14.6 %copy-start.1 = (bf16[8,4,512,128]{3,2,1,0:T(8,128)(2,1)S(1)}, bf16[8,4,512,128]{3,2,1,0:T(8,128)(2,1)}, u32[]{:S(2)}) copy-start(bf16[8,4,512,128]{3,2,1,0:T(8,128)(2,1)} %get-tuple-element.459) | copy-start | bytes 12582916 | tf_op jit(solution)/shard_map/while
  274.3 14.6 %copy-start.1 = (bf16[8,4,512,128]{3,2,1,0:T(8,128)(2,1)S(1)}, bf16[8,4,512,128]{3,2,1,0:T(8,128)(2,1)}, u32[]{:S(2)}) copy-start(bf16[8,4,512,128]{3,2,1,0:T(8,128)(2,1)} %get-tuple-element.459) | copy-start | bytes 12582916 | tf_op jit(solution)/shard_map/while
  303.8 14.6 %copy-start.1 = (bf16[8,4,512,128]{3,2,1,0:T(8,128)(2,1)S(1)}, bf16[8,4,512,128]{3,2,1,0:T(8,128)(2,1)}, u32[]{:S(2)}) copy-start(bf16[8,4,512,128]{3,2,1,0:T(8,128)(2,1)} %get-tuple-element.459) | copy-start | bytes 12582916 | tf_op jit(solution)/shard_map/while
  333.2 14.6 %copy-start.1 = (bf16[8,4,512,128]{3,2,1,0:T(8,128)(2,1)S(1)}, bf16[8,4,512,128]{3,2,1,0:T(8,128)(2,1)}, u32[]{:S(2)}) copy-start(bf16[8,4,512,128]{3,2,1,0:T(8,128)(2,1)} %get-tuple-element.459) | copy-start | bytes 12582916 | tf_op jit(solution)/shard_map/while
  354.8 23.6 %all-to-all-start.1 = ((bf16[32,2,4,128]{3,2,1,0:T(4,128)(2,1)}), bf16[32,2,4,128]{3,2,1,0:T(4,128)(2,1)S(1)}, u32[]{:S(2)}, u32[]{:S(2)}) async-start(bf16[32,2,4,128]{3,2,1,0:T(4,128)(2,1)} %bitcast.19), calls=%async_computation.1 | async-start | bytes 131072 | tf_op jit(solution)/shard_map/all_to_all | solution.py:199
  378.5 9.1 %copy-start.13 = (f32[4]{0:T(128)S(1)}, f32[4]{0:T(128)}, u32[]{:S(2)}) copy-start(f32[4]{0:T(128)} %param.23) | copy-start | bytes 52
  378.5 10.6 %copy-start.6 = (bf16[256,2048]{1,0:T(8,128)(2,1)S(1)}, bf16[256,2048]{1,0:T(8,128)(2,1)}, u32[]{:S(2)}) copy-start(bf16[256,2048]{1,0:T(8,128)(2,1)} %all-gather.3.cloned.1.call-done) | copy-start | bytes 3145732
  378.5 0.6 copy-start.7
  379.1 113.2 %all-to-all-start = ((bf16[32,2,4,128,128]{4,1,3,2,0:T(2,128)(2,1)}), bf16[32,2,4,128,128]{4,1,3,2,0:T(2,128)(2,1)}, u32[]{:S(2)}, u32[]{:S(2)}) async-start(bf16[32,2,4,128,128]{4,1,3,2,0:T(2,128)(2,1)} %copy.76), calls=%async_computation | async-start | bytes 16777216 | tf_op jit(solution)/shard_map/all_to_all | solution.py:196
  386.5 149.2 %reduce-scatter.2.cloned.1.call-start = ((), (), s32[]{:S(2)}) async-start(), calls=%async_computation.5 | async-start | bytes 1310720 | tf_op jit(solution)/shard_map/reduce_scatter | solution.py:215
  392.2 14.7 %copy-start.3 = (f32[256,4,128]{2,1,0:T(4,128)S(1)}, f32[256,4,128]{2,1,0:T(4,128)}, u32[]{:S(2)}) copy-start(f32[256,4,128]{2,1,0:T(4,128)} %copy-done.2) | copy-start | bytes 1572868
  393.8 13.4 %copy-start.5 = (f32[256,512]{1,0:T(8,128)S(1)}, f32[256,512]{1,0:T(8,128)}, u32[]{:S(2)}) copy-start(f32[256,512]{1,0:T(8,128)} %fusion.35) | copy-start | bytes 1572868
  395.2 12.0 %collective-permute-start.1 = (bf16[256,4,128]{2,0,1:T(8,128)(2,1)S(1)}, bf16[256,4,128]{2,0,1:T(8,128)(2,1)}, u32[]{:S(2)}, u32[]{:S(2)}) collective-permute-start(bf16[256,4,128]{2,0,1:T(8,128)(2,1)S(1)} %fusion.24), channel_id=1, source_target_pairs={{0,4},{4,8},{8,12},{12,16},{16,20},{20,24},{24,28},{28,32},{32,36}... | collective-permute-start | bytes 786440 | tf_op jit(solution)/shard_map/ppermute | solution.py:14
  403.2 6.9 %copy-start.8 = (bf16[32,2,4,128]{3,2,1,0:T(4,128)(2,1)S(1)}, bf16[32,2,4,128]{3,2,1,0:T(4,128)(2,1)}, u32[]{:S(2)}) copy-start(bf16[32,2,4,128]{3,2,1,0:T(4,128)(2,1)} %copy-done.7) | copy-start | bytes 196612
  403.2 102.7 %collective-permute-start = (bf16[256,4,128]{0,2,1:T(8,128)(2,1)}, bf16[256,4,128]{0,2,1:T(8,128)(2,1)}, u32[]{:S(2)}, u32[]{:S(2)}) collective-permute-start(bf16[256,4,128]{0,2,1:T(8,128)(2,1)} %bitcast.113), channel_id=1, source_target_pairs={{0,4},{4,8},{8,12},{12,16},{16,20},{20,24},{24,28},{28,32},{32,36}... | collective-permute-start | bytes 786440 | tf_op jit(solution)/shard_map/ppermute | solution.py:14
  502.5 3.4 copy-start.9
  502.5 3.4 copy-start.14
  502.6 3.4 copy-start.15
Sparse Core Ops, SparseCore 0:
  9.0 26.3 all-gather.2
  43.6 53.3 all-gather.4
  510.2 25.5 reduce-scatter.1
where the time goes:
time: 548 us; the launch traced here: 542 us
  local copies, waits for them, and re-layouts  230 us (42%)
  waiting for transfers between devices  135 us (25%)
  matrix products  54.9 us (10%)
  loops' own time  47.3 us (9%)
  other arithmetic  40.6 us (7%)
  starting transfers between devices  21.2 us (4%)
  between operations  13.4 us (2%)
    while x184, local copies, waits for them, and re-layouts  118 us
    all_to_all x1, waiting for transfers between devices, body(): lax.all_to_all(as_sent(part_out), 'mem', split_axis=0, concat_axis=0, til...  81.4 us
    another operation x1, loops' own time, block_attention(): lax.map(one_group, (jnp.arange(turn_count, dtype=jnp.int32), id_groups))  47.3 us
    all_gather x1, waiting for transfers between devices, body(): gathered = lax.all_gather(hidden_states, 'tp', axis=1, tiled=True)  27.5 us
    reduce_scatter x1, waiting for transfers between devices, body(): lax.psum_scatter(jnp.dot(mixed, final_projection_matrix, preferred_elemen...  25.7 us
    dot_general x8, matrix products, one_group(): jnp.einsum('ghqm,ghmd->ghqd', weights.astype(jnp.bfloat16), value_rows, p...  22.6 us
    reshape x5, local copies, waits for them, and re-layouts, unit_heads(): shaped = matrix.astype(jnp.float32).reshape(row_count, reader_number, -1)  19.3 us
    another operation x1, local copies, waits for them, and re-layouts, body(): part_out.reshape(source_count, own_blocks * capacity, reader_number, QB,...  16.3 us
  transfers between devices with their start and end apart: 7, of which 3 were waited for; matrix products, arithmetic and copies ran while one was open for 23% of the time, Pallas kernels for 0%

commit v1 on v0

v1 whole, which is shorter than its diff:
```python
import functools

import jax
import jax.numpy as jnp
from jax import lax
from jax.experimental import pallas as pl
from jax.experimental.pallas import tpu as pltpu
from jax.sharding import PartitionSpec as P

QB = 128
MB = 512
LOCAL = 256
HD = 128
LOG2E = 1.4426950408889634
NT = (((1,), (1,)), ((), ()))
VMEM = pl.BlockSpec(memory_space=pltpu.VMEM)
SMEM = pl.BlockSpec(memory_space=pltpu.SMEM)
F32 = jnp.float32
BF16 = jnp.bfloat16


def params(mib):
    return pltpu.CompilerParams(vmem_limit_bytes=mib * 2**20)


def cost(flops, nbytes, trans=0):
    return pl.CostEstimate(flops=flops, bytes_accessed=nbytes, transcendentals=trans)


def unit_into(ref, rows, value):
    for h in range(value.shape[1] // HD):
        part = value[:, h * HD : (h + 1) * HD]
        scale = lax.rsqrt(jnp.mean(part * part, axis=-1, keepdims=True) + 1e-06)
        ref[rows, h * HD : (h + 1) * HD] = (part * scale).astype(BF16)


def query_kernel(order, x0, x1, x2, x3, gain, weight, normed, queries):
    pieces = [x[...].astype(F32) for x in (x0, x1, x2, x3)]
    total = sum(jnp.sum(p * p, axis=-1, keepdims=True) for p in pieces)
    scale = lax.rsqrt(total / (4 * pieces[0].shape[1]) + 1e-05)
    result = None
    for p, piece in enumerate(pieces):
        value = (piece * scale * gain[order[p]].astype(F32)).astype(BF16)
        normed[p] = value
        term = jnp.dot(value, weight[order[p]], preferred_element_type=F32)
        result = term if result is None else result + term
    unit_into(queries, slice(None), result)


def kv_kernel(order, normed, key_weight, value_weight, kv):
    for side, weight in enumerate((key_weight, value_weight)):
        result = None
        for p in range(4):
            term = jnp.dot(normed[p], weight[order[p]], preferred_element_type=F32)
            result = term if result is None else result + term
        if side == 0:
            unit_into(kv.at[0], slice(None), result)
        else:
            kv[1] = result.astype(BF16)


def key_unit_kernel(raw, keys):
    unit_into(keys, slice(None), raw[...].astype(F32))


def local_kernel(sharp, seg_own, seg_keys, queries, kv, before, out):
    rows = queries.shape[0]
    place = lax.broadcasted_iota(jnp.int32, (rows, rows), 0)
    other = lax.broadcasted_iota(jnp.int32, (rows, rows), 1)
    same_before = seg_own[...] == seg_keys[:, :rows]
    same_own = seg_own[...] == seg_keys[:, rows:]
    allow_before = (other > place) & same_before
    allow_own = (other <= place) & same_own
    for h in range(queries.shape[1] // HD):
        cols = slice(h * HD, (h + 1) * HD)
        scale = sharp[h] * (LOG2E / HD)
        q = queries[:, cols]
        numer = None
        total = None
        for keep, src in ((allow_before, before), (allow_own, kv)):
            s = lax.dot_general(q, src[0, :, cols], NT, preferred_element_type=F32)
            w = jnp.where(keep, jnp.exp2(s * scale), 0.0)
            t = jnp.sum(w, axis=-1, keepdims=True)
            n = jnp.dot(w.astype(BF16), src[1, :, cols], preferred_element_type=F32)
            numer = n if numer is None else numer + n
            total = t if total is None else total + t
        out[:, cols] = numer / total


def memory_kernel(meta, sharp, q1, q2, k_own, v_own, k_sib, v_sib, o1, o2):
    i = pl.program_id(0)
    eye = lax.broadcasted_iota(jnp.int32, (QB, QB), 0) == lax.broadcasted_iota(
        jnp.int32, (QB, QB), 1
    )
    tile_row = lax.broadcasted_iota(jnp.int32, (16, HD), 0)

    def work(q_ref, o_ref):
        o_ref[...] = jnp.zeros_like(o_ref)

        def slot(j, k_ref, v_ref):
            half = meta[i, 4 + j]
            rows = pl.ds(pl.multiple_of(half * QB, QB), QB)
            for h in range(q_ref.shape[2] // HD):
                cols = slice(h * HD, (h + 1) * HD)
                scale = sharp[h] * (LOG2E / HD)
                s = lax.dot_general(
                    q_ref[0, rows, cols], k_ref[:, cols], NT, preferred_element_type=F32
                )
                w = jnp.exp2(s * scale)
                den = jnp.sum(w, axis=-1, keepdims=True)
                num = jnp.dot(w.astype(BF16), v_ref[:, cols], preferred_element_type=F32)
                line = jnp.sum(jnp.where(eye, den, 0.0), axis=0, keepdims=True)
                dens = jnp.where(tile_row == half, line, 0.0)
                if j == 1:
                    num = num + o_ref[0, rows, cols].astype(F32)
                    dens = dens + o_ref[0, 2 * QB :, cols].astype(F32)
                o_ref[0, rows, cols] = num.astype(BF16)
                o_ref[0, 2 * QB :, cols] = dens.astype(BF16)

        pl.when(meta[i, 2] > 0)(lambda: slot(0, k_own, v_own))
        pl.when(meta[i, 3] > 0)(lambda: slot(1, k_sib, v_sib))

    pl.when(i < 2)(lambda: work(q1, o1))
    pl.when(i >= 2)(lambda: work(q2, o2))


def memory_attention(meta, sharp, q1, q2, k_own, v_own, k_sib, v_sib):
    width = q1.shape[2]
    first = lambda i, meta: (jnp.minimum(i, 1), 0, 0)
    second = lambda i, meta: (jnp.maximum(i - 2, 0), 0, 0)
    own = lambda i, meta: (meta[i, 0], 0)
    sib = lambda i, meta: (meta[i, 1], 0)
    block = lambda m: pl.BlockSpec((MB, width), m)
    part = lambda m: pl.BlockSpec((1, 2 * QB, width), m)
    done = lambda m: pl.BlockSpec((1, 2 * QB + 16, width), m)
    shape = jax.ShapeDtypeStruct((2, 2 * QB + 16, width), BF16)
    return pl.pallas_call(
        memory_kernel,
        grid_spec=pltpu.PrefetchScalarGridSpec(
            num_scalar_prefetch=1,
            grid=(4,),
            in_specs=[
                SMEM,
                part(first),
                part(second),
                block(own),
                block(own),
                block(sib),
                block(sib),
            ],
            out_specs=[done(first), done(second)],
        ),
        out_shape=[shape, shape],
        compiler_params=params(24),
        cost_estimate=cost(8 * 134_000_000, 8 * 2**20, 8 * QB * MB * 4),
        name="memory_attention",
    )(meta, sharp, q1, q2, k_own, v_own, k_sib, v_sib)


def output_kernel(order, bias, w, x1, x2, x3, local, weight, c0, c1, c2, c3, mixed):
    total = [a[0].astype(F32) if a.ndim == 3 else a[...].astype(F32) for a in (w, x1, x2, x3)]
    total = total[0] + total[1] + total[2] + total[3]
    dens = total[2 * QB :, :]
    for h in range(total.shape[1] // HD):
        cols = slice(h * HD, (h + 1) * HD)
        gate = jax.nn.sigmoid(jnp.full((1, HD), bias[h], F32))
        turned = jnp.transpose(
            jnp.concatenate([dens[:, cols], jnp.zeros((HD - 16, HD), F32)], axis=0)
        )
        for b in range(2):
            rows = slice(b * QB, (b + 1) * QB)
            mem = total[rows, cols] / turned[:, b : b + 1]
            mixed[rows, cols] = (gate * mem + (1.0 - gate) * local[rows, cols]).astype(BF16)
    for j, c in enumerate((c0, c1, c2, c3)):
        rows = pl.ds(pl.multiple_of(order[j] * 64, 64), 64)
        c[...] = jnp.dot(mixed[rows, :], weight[...], preferred_element_type=F32).astype(c.dtype)


def mem_pairs(move):
    out = []
    for z in range(4):
        for y in range(4):
            for c in range(2):
                tz, ty, tc = move(z, y, c)
                out.append((z * 8 + y * 2 + c, (tz % 4) * 8 + (ty % 4) * 2 + tc))
    return out


def first_axis(value, by):
    pairs = mem_pairs(lambda z, y, c: (z + by, y, c) if c == 0 else (z, y + by, c))
    return lax.ppermute(value, "mem", pairs)


def second_axis(value, by):
    pairs = mem_pairs(lambda z, y, c: (z, y + by, c) if c == 0 else (z + by, y, c))
    return lax.ppermute(value, "mem", pairs)


def other_core(value):
    return lax.ppermute(value, "mem", mem_pairs(lambda z, y, c: (z, y, 1 - c)))


def along_tp(value, by):
    return lax.ppermute(value, "tp", [(i, (i + by) % 4) for i in range(4)])


def make_meta(assign, index, blocks_here):
    z, y, c = index // 8, (index // 2) % 4, index % 2
    shifts = jnp.array([0, -1, 1, 2], jnp.int32)
    second = jnp.array([0, -1, 1, 2], jnp.int32)[:, None]
    first = shifts[None, :]
    sz = jnp.where(c == 0, z + first, z + second) % 4
    sy = jnp.where(c == 0, y + second, y + first) % 4
    source = sz * 8 + sy * 2 + c
    ids = jnp.take(assign.reshape(-1, 16), source.reshape(-1), axis=0)
    holder = jnp.stack([index, index + 1 - 2 * c])
    hit = (ids // blocks_here)[:, None, :] == holder[None, :, None]
    here = jnp.any(hit, axis=-1).astype(jnp.int32).reshape(4, 4, 2)
    block = jnp.sum(jnp.where(hit, (ids % blocks_here)[:, None, :], 0), axis=-1).reshape(4, 4, 2)
    place = jnp.arange(16, dtype=jnp.int32)[None, None, :] // 8
    half = jnp.sum(jnp.where(hit, place, 0), axis=-1).reshape(4, 4, 2)
    fetch = [block[:, 0]]
    for i in range(1, 4):
        fetch.append(jnp.where(here[:, i] > 0, block[:, i], fetch[-1]))
    return jnp.concatenate([jnp.stack(fetch, axis=1), here, half], axis=-1)


def add(a, b):
    return (a.astype(F32) + b.astype(F32)).astype(BF16)


def add3(a, b, c):
    return (a.astype(F32) + b.astype(F32) + c.astype(F32)).astype(BF16)


def body(
    hidden_states,
    entry_rescale_coefficients,
    probe_projection_matrix,
    address_projection_matrix,
    content_projection_matrix,
    final_projection_matrix,
    archive_address_vectors,
    archive_content_vectors,
    reader_sharpness,
    reader_mixing_bias,
    retrieval_assignments,
    document_labels,
):
    rows, piece = hidden_states.shape
    width = probe_projection_matrix.shape[1]
    index = lax.axis_index("mem")
    me = lax.axis_index("tp")
    order = (me + jnp.array([0, -1, 1, 2], jnp.int32)) % 4

    x1 = along_tp(hidden_states, 1)
    x2 = along_tp(hidden_states, -1)
    x3 = along_tp(hidden_states, 2)

    v_own = archive_content_vectors
    v_sib = other_core(v_own)
    k_own = pl.pallas_call(
        key_unit_kernel,
        grid=(8,),
        in_specs=[pl.BlockSpec((MB, width), lambda i: (i, 0))],
        out_specs=pl.BlockSpec((MB, width), lambda i: (i, 0)),
        out_shape=jax.ShapeDtypeStruct(archive_address_vectors.shape, BF16),
        compiler_params=params(16),
        cost_estimate=cost(10 * 2**20, 8 * 2**20),
        name="key_unit",
    )(archive_address_vectors)
    k_sib = other_core(k_own)

    meta = make_meta(retrieval_assignments, index, archive_address_vectors.shape[0] // MB)

    normed, queries = pl.pallas_call(
        query_kernel,
        in_specs=[SMEM] + [VMEM] * 6,
        out_specs=[VMEM, VMEM],
        out_shape=[
            jax.ShapeDtypeStruct((4, rows, piece), BF16),
            jax.ShapeDtypeStruct((rows, width), BF16),
        ],
        compiler_params=params(24),
        cost_estimate=cost(2 * rows * 4 * piece * width, 4 * 2**20),
        name="norm_query",
    )(
        order,
        hidden_states,
        x1,
        x2,
        x3,
        entry_rescale_coefficients.reshape(4, 1, piece),
        probe_projection_matrix.reshape(4, piece, width),
    )

    a1 = first_axis(queries, 1)
    a2 = first_axis(queries, -1)
    a3 = first_axis(queries, 2)
    kv = pl.pallas_call(
        kv_kernel,
        in_specs=[SMEM] + [VMEM] * 3,
        out_specs=VMEM,
        out_shape=jax.ShapeDtypeStruct((2, rows, width), BF16),
        compiler_params=params(24),
        cost_estimate=cost(4 * rows * 4 * piece * width, 6 * 2**20),
        name="local_kv",
    )(
        order,
        normed,
        address_projection_matrix.reshape(4, piece, width),
        content_projection_matrix.reshape(4, piece, width),
    )
    m1 = jnp.stack([queries, a1])
    m2 = jnp.stack([a2, a3])
    b1p = second_axis(m1, 1)
    b1m = second_axis(m1, -1)
    b2p = second_axis(m2, 1)
    b2m = second_axis(m2, -1)
    c1 = second_axis(b1p, 1)
    c2 = second_axis(b2m, -1)

    count = lax.axis_size("mem")
    before = lax.ppermute(kv, "mem", [(i, i + 1) for i in range(count - 1)])
    first_row = index * rows
    seg_own = lax.dynamic_slice_in_dim(document_labels, first_row, rows, 0)
    seg_before = lax.dynamic_slice_in_dim(
        document_labels, jnp.maximum(first_row - rows, 0), rows, 0
    )
    seg_before = jnp.where(index > 0, seg_before, -1)
    seg_keys = jnp.concatenate([seg_before, seg_own], axis=0)
    local_out = pl.pallas_call(
        local_kernel,
        in_specs=[SMEM] + [VMEM] * 5,
        out_specs=VMEM,
        out_shape=jax.ShapeDtypeStruct((rows, width), F32),
        compiler_params=params(24),
        cost_estimate=cost(2**28, 2 * 2**20, 2**19),
        name="local_attention",
    )(reader_sharpness, seg_own[:, None], seg_keys[None, :], queries, kv, before)

    attend = lambda g, q1, q2: memory_attention(
        meta[g], reader_sharpness, q1, q2, k_own, v_own, k_sib, v_sib
    )
    z1, z2 = attend(0, m1, m2)
    n1, n2 = attend(1, b1p, b2p)
    p1, p2 = attend(2, b1m, b2m)
    f1, f2 = attend(3, c1, c2)

    t1 = second_axis(f1, 1)
    t2 = second_axis(f2, -1)
    u2 = second_axis(p2, 1)
    v1 = second_axis(n1, -1)
    u1 = second_axis(add(p1, t1), 1)
    v2 = second_axis(add(n2, t2), -1)
    w1 = add3(z1, u1, v1)
    w2 = add3(z2, u2, v2)
    r1 = first_axis(w1[1], -1)
    r2 = first_axis(w2[0], 1)
    r3 = first_axis(w2[1], 2)

    chunk = jax.ShapeDtypeStruct((rows // 4, 4 * piece), BF16)
    c0, d1, d2, d3 = pl.pallas_call(
        output_kernel,
        in_specs=[SMEM, SMEM] + [VMEM] * 6,
        out_specs=[VMEM] * 4,
        out_shape=[chunk] * 4,
        scratch_shapes=[pltpu.VMEM((rows, width), BF16)],
        compiler_params=params(32),
        cost_estimate=cost(2 * rows * width * 4 * piece, 5 * 2**20),
        name="merge_output",
    )(order, reader_mixing_bias, w1[0], r1, r2, r3, local_out, final_projection_matrix)
    e1 = along_tp(d1, -1)
    e2 = along_tp(d2, 1)
    e3 = along_tp(d3, 2)
    total = c0.astype(F32) + e1.astype(F32) + e2.astype(F32) + e3.astype(F32)
    return total.astype(BF16)


def solution(mesh):
    placed = (
        P("mem", "tp"),
        P(),
        P(None, "tp"),
        P(None, "tp"),
        P(None, "tp"),
        P("tp", None),
        P("mem", "tp"),
        P("mem", "tp"),
        P("tp"),
        P("tp"),
        P(),
        P(),
    )
    return jax.shard_map(
        body, mesh=mesh, in_specs=placed, out_specs=P(("mem", "tp"), None), check_vma=False
    )
```

time: 548 us -> 156 us (0.28)
  local copies, waits for them, and re-layouts: 230 us -> 18 us
  waiting for transfers between devices: 135 us -> 41.1 us
  matrix products: 54.9 us -> 0 us
  loops' own time: 47.3 us -> 0 us
  Pallas kernels: 0 us -> 42.7 us
  other arithmetic: 40.6 us -> 7.71 us
  starting transfers between devices: 21.2 us -> 45.2 us
  between operations: 13.4 us -> 0.27 us
    while x185 -> x0, local copies, waits for them, and re-layouts: 126 us -> none
    all_to_all x2 -> x0, waiting for transfers between devices: 81.5 us -> none  [the longest x1 81.4 us: body(): lax.all_to_all(as_sent(part_out), 'mem', split_axis=0, concat_axis=0, til...]
    dot_general x23 -> x0, matrix products: 54.9 us -> none  [the longest x8 22.6 us: one_group(): jnp.einsum('ghqm,ghmd->ghqd', weights.astype(jnp.bfloat16), value_rows, p...]
    another operation x1 -> x0, loops' own time: 47.3 us -> none  [block_attention(): lax.map(one_group, (jnp.arange(turn_count, dtype=jnp.int32), id_groups))]
    pallas_call x0 -> x9, Pallas kernels: none -> 42.7 us  [the longest x4 29 us: memory_attention(): pl.pallas_call(memory_kernel, grid_spec=pltpu.PrefetchScalarGridSpec(num_...]
    ppermute x2 -> x27, waiting for transfers between devices: 0.01 us -> 41.1 us  [the longest x6 23.6 us: along_tp(): return lax.ppermute(value, 'tp', [(i, (i + by) % 4) for i in range(4)])]
    ppermute x2 -> x27, starting transfers between devices: 6.48 us -> 45.2 us  [the longest x12 20.5 us: second_axis(): return lax.ppermute(value, 'mem', pairs)]
    another operation x19 -> x0, local copies, waits for them, and re-layouts: 34.5 us -> none  [the longest x1 16.3 us: body(): part_out.reshape(source_count, own_blocks * capacity, reader_number, QB,...]
  transfers between devices with their start and end apart: 7 -> 27, of which waited for: 3 -> 11; matrix products, arithmetic and copies ran while one was open for 23% -> 7% of each run, Pallas kernels for 0% -> 22%
where the time goes in v1:
time: 156 us; the launch traced here: 155 us
  starting transfers between devices  45.2 us (29%)
  Pallas kernels  42.7 us (27%)
  waiting for transfers between devices  41.1 us (26%)
  local copies, waits for them, and re-layouts  18 us (12%)
  other arithmetic  7.71 us (5%)
    pallas_call x4, Pallas kernels, memory_attention(): pl.pallas_call(memory_kernel, grid_spec=pltpu.PrefetchScalarGridSpec(num_...  29 us
    ppermute x6, waiting for transfers between devices, along_tp(): return lax.ppermute(value, 'tp', [(i, (i + by) % 4) for i in range(4)])  23.6 us
    ppermute x12, starting transfers between devices, second_axis(): return lax.ppermute(value, 'mem', pairs)  20.5 us
    ppermute x6, starting transfers between devices, first_axis(): return lax.ppermute(value, 'mem', pairs)  14.7 us
    unnamed x57, local copies, waits for them, and re-layouts  14.7 us
    ppermute x12, waiting for transfers between devices, second_axis(): return lax.ppermute(value, 'mem', pairs)  10.8 us
    ppermute x6, starting transfers between devices, along_tp(): return lax.ppermute(value, 'tp', [(i, (i + by) % 4) for i in range(4)])  7.23 us
    ppermute x6, waiting for transfers between devices, first_axis(): return lax.ppermute(value, 'mem', pairs)  6.63 us
  transfers between devices with their start and end apart: 27, of which 11 were waited for; matrix products, arithmetic and copies ran while one was open for 7% of the time, Pallas kernels for 22%

profile of v1, /device:TPU:0, one launch (start us, length us, event | category | flops | bytes accessed | tf_op | source)
XLA Modules:
  0.0 154.9 jit_solution(9008371477949900088)
XLA Ops:
  0.0 2.2 %copy-done = bf16[4096,512]{1,0:T(8,128)(2,1)S(1)} copy-done((bf16[4096,512]{1,0:T(8,128)(2,1)S(1)}, bf16[4096,512]{1,0:T(8,128)(2,1)}, u32[]{:S(2)}) %copy-start) | copy-done | bytes 4194328
  2.2 5.0 %key_unit.1.k_own = bf16[4096,512]{1,0:T(8,128)(2,1)} custom-call(bf16[4096,512]{1,0:T(8,128)(2,1)S(1)} %copy-done), custom_call_target="tpu_custom_call" | custom-call | flops 10485760 | bytes 8388608 | tf_op jit(solution)/shard_map/key_unit/pallas_call | solution.py:262
  7.7 2.8 %collective-permute-start.1 = (bf16[256,512]{1,0:T(8,128)(2,1)S(1)}, bf16[256,512]{1,0:T(8,128)(2,1)S(1)}, u32[]{:S(2)}, u32[]{:S(2)}) collective-permute-start(bf16[256,512]{1,0:T(8,128)(2,1)S(1)} %copy-done.13), channel_id=1, source_target_pairs={{0,3},{1,0},{2,1},{3,2},{4,7},{5,4},{6,5},{7,6},{8,11},{9,8},{10,9... | collective-permute-start | bytes 786440 | tf_op jit(solution)/shard_map/ppermute | solution.py:204
  10.6 2.3 %collective-permute-start.2 = (bf16[256,512]{1,0:T(8,128)(2,1)S(1)}, bf16[256,512]{1,0:T(8,128)(2,1)S(1)}, u32[]{:S(2)}, u32[]{:S(2)}) collective-permute-start(bf16[256,512]{1,0:T(8,128)(2,1)S(1)} %copy-done.13), channel_id=1, source_target_pairs={{0,2},{1,3},{2,0},{3,1},{4,6},{5,7},{6,4},{7,5},{8,10},{9,11},{10,... | collective-permute-start | bytes 786440 | tf_op jit(solution)/shard_map/ppermute | solution.py:204
  13.3 8.6 %collective-permute-done.1.x2 = bf16[256,512]{1,0:T(8,128)(2,1)S(1)} collective-permute-done((bf16[256,512]{1,0:T(8,128)(2,1)S(1)}, bf16[256,512]{1,0:T(8,128)(2,1)S(1)}, u32[]{:S(2)}, u32[]{:S(2)}) %collective-permute-start.1) | collective-permute-done | bytes 262176 | tf_op jit(solution)/shard_map/ppermute | solution.py:204
  22.6 2.7 %collective-permute-done.x1 = bf16[256,512]{1,0:T(8,128)(2,1)S(1)} collective-permute-done((bf16[256,512]{1,0:T(8,128)(2,1)S(1)}, bf16[256,512]{1,0:T(8,128)(2,1)S(1)}, u32[]{:S(2)}, u32[]{:S(2)}) %collective-permute-start) | collective-permute-done | bytes 262176 | tf_op jit(solution)/shard_map/ppermute | solution.py:204
  26.8 0.9 copy-done.14
  27.7 0.9 copy-done.16
  28.7 0.9 copy-done.18
  29.6 0.9 copy-done.20
  30.6 1.7 %norm_query.1 = (bf16[4,256,512]{2,1,0:T(8,128)(2,1)S(1)}, bf16[256,512]{1,0:T(8,128)(2,1)S(1)}) custom-call(s32[4]{0:T(128)S(1)} %get-tuple-element.52.order, bf16[256,512]{1,0:T(8,128)(2,1)S(1)} %copy-done.14, bf16[256,512]{1,0:T(8,128)(2,1)S(1)} %copy-done.18, bf16[256,512]{1,0:T(8,128)(2,1)S(1)} %copy-done.16, bf16[256,512]{1,0:T(8,128)(2,1)S(1)} %copy-done.20, ...), custom_call_target="tpu_custom_call" | custom-call | flops 536870912 | bytes 4194304 | tf_op jit(solution)/shard_map/norm_query/pallas_call | solution.py:276
  32.2 1.0 copy-done.7
  33.2 1.9 %collective-permute-start.3 = (bf16[256,512]{1,0:T(8,128)(2,1)S(1)}, bf16[256,512]{1,0:T(8,128)(2,1)S(1)}, u32[]{:S(2)}, u32[]{:S(2)}) collective-permute-start(bf16[256,512]{1,0:T(8,128)(2,1)S(1)} %get-tuple-element.19.queries), channel_id=1, source_target_pairs={{0,32},{4,12},{8,40},{12,20},{16,48},{20,28},{24,56},{28,4},{32,64... | collective-permute-start | bytes 786440 | tf_op jit(solution)/shard_map/ppermute | solution.py:191
  35.1 3.7 %collective-permute-start.5 = (bf16[256,512]{1,0:T(8,128)(2,1)S(1)}, bf16[256,512]{1,0:T(8,128)(2,1)S(1)}, u32[]{:S(2)}, u32[]{:S(2)}) collective-permute-start(bf16[256,512]{1,0:T(8,128)(2,1)S(1)} %get-tuple-element.19.queries), channel_id=1, source_target_pairs={{0,64},{4,20},{8,72},{12,28},{16,80},{20,4},{24,88},{28,12},{32,96... | collective-permute-start | bytes 786440 | tf_op jit(solution)/shard_map/ppermute | solution.py:191
  38.8 1.0 collective-permute-start.4
  40.6 1.0 collective-permute-done.3
  41.6 2.5 %collective-permute-start.10 = (bf16[2,256,512]{2,1,0:T(8,128)(2,1)S(1)}, bf16[2,256,512]{2,1,0:T(8,128)(2,1)S(1)}, u32[]{:S(2)}, u32[]{:S(2)}) collective-permute-start(bf16[2,256,512]{2,1,0:T(8,128)(2,1)S(1)} %pad_maximum_fusion.q1), channel_id=1, source_target_pairs={{0,8},{4,36},{8,16},{12,44},{16,24},{20,52},{24,0},{28,60},{32,40}... | collective-permute-start | bytes 1572872 | tf_op jit(solution)/shard_map/ppermute | solution.py:196
  44.2 4.4 %collective-permute-done.5 = bf16[256,512]{1,0:T(8,128)(2,1)S(1)} collective-permute-done((bf16[256,512]{1,0:T(8,128)(2,1)S(1)}, bf16[256,512]{1,0:T(8,128)(2,1)S(1)}, u32[]{:S(2)}, u32[]{:S(2)}) %collective-permute-start.5) | collective-permute-done | bytes 262176 | tf_op jit(solution)/shard_map/ppermute | solution.py:191
  48.6 4.4 %collective-permute-start.9 = (bf16[2,256,512]{2,1,0:T(8,128)(2,1)S(1)}, bf16[2,256,512]{2,1,0:T(8,128)(2,1)S(1)}, u32[]{:S(2)}, u32[]{:S(2)}) collective-permute-start(bf16[2,256,512]{2,1,0:T(8,128)(2,1)S(1)} %pad_maximum_fusion.1.q2), channel_id=1, source_target_pairs={{0,24},{4,100},{8,0},{12,108},{16,8},{20,116},{24,16},{28,124},{32... | collective-permute-start | bytes 1572872 | tf_op jit(solution)/shard_map/ppermute | solution.py:196
  53.7 5.9 %collective-permute-done.9.q2 = bf16[2,256,512]{2,1,0:T(8,128)(2,1)S(1)} collective-permute-done((bf16[2,256,512]{2,1,0:T(8,128)(2,1)S(1)}, bf16[2,256,512]{2,1,0:T(8,128)(2,1)S(1)}, u32[]{:S(2)}, u32[]{:S(2)}) %collective-permute-start.9) | collective-permute-done | bytes 524320 | tf_op jit(solution)/shard_map/ppermute | solution.py:196
  59.7 3.7 %collective-permute-start.12 = (bf16[2,256,512]{2,1,0:T(8,128)(2,1)S(1)}, bf16[2,256,512]{2,1,0:T(8,128)(2,1)}, u32[]{:S(2)}, u32[]{:S(2)}) collective-permute-start(bf16[2,256,512]{2,1,0:T(8,128)(2,1)S(1)} %collective-permute-done.9.q2), channel_id=1, source_target_pairs={{0,24},{4,100},{8,0},{12,108},{16,8},{20,116},{24,16},{28,124},{32... | collective-permute-start | bytes 1572872 | tf_op jit(solution)/shard_map/ppermute | solution.py:196
  64.1 1.5 collective-permute-start.15
  65.7 4.4 %collective-permute-done.12.q2 = bf16[2,256,512]{2,1,0:T(8,128)(2,1)} collective-permute-done((bf16[2,256,512]{2,1,0:T(8,128)(2,1)S(1)}, bf16[2,256,512]{2,1,0:T(8,128)(2,1)}, u32[]{:S(2)}, u32[]{:S(2)}) %collective-permute-start.12) | collective-permute-done | bytes 524320 | tf_op jit(solution)/shard_map/ppermute | solution.py:196
  70.1 9.2 %memory_attention.6 = (bf16[2,272,512]{2,1,0:T(8,128)(2,1)}, bf16[2,272,512]{2,1,0:T(8,128)(2,1)}) custom-call(s32[4,6]{1,0:T(4,128)S(1)} %bitcast.38, f32[4]{0:T(128)S(1)} %copy-done.21, bf16[2,256,512]{2,1,0:T(8,128)(2,1)S(1)} %collective-permute-done.11.q1, bf16[2,256,512]{2,1,0:T(8,128)(2,1)} %collective-permute-done.12.q2, ...), custom_call_target="tpu_custom_call" | custom-call | flops 1072000000 | bytes 8388608 | tf_op jit(solution)/shard_map/memory_attention/pallas_call | solution.py:137
  80.3 6.2 %memory_attention.5 = (bf16[2,272,512]{2,1,0:T(8,128)(2,1)S(1)}, bf16[2,272,512]{2,1,0:T(8,128)(2,1)}) custom-call(s32[4,6]{1,0:T(4,128)S(1)} %bitcast.39, f32[4]{0:T(128)S(1)} %copy-done.21, bf16[2,256,512]{2,1,0:T(8,128)(2,1)} %collective-permute-done.8.q1, bf16[2,256,512]{2,1,0:T(8,128)(2,1)S(1)} %collective-permute-done.9.q2, ...), custom_call_target="tpu_custom_call" | custom-call | flops 1072000000 | bytes 8388608 | tf_op jit(solution)/shard_map/memory_attention/pallas_call | solution.py:137
  87.3 1.3 collective-permute-start.18
  89.4 1.0 copy-done.12
  90.5 7.4 %memory_attention.7 = (bf16[2,272,512]{2,1,0:T(8,128)(2,1)S(1)}, bf16[2,272,512]{2,1,0:T(8,128)(2,1)S(1)}) custom-call(s32[4,6]{1,0:T(4,128)S(1)} %bitcast.37, f32[4]{0:T(128)S(1)} %copy-done.21, bf16[2,256,512]{2,1,0:T(8,128)(2,1)S(1)} %collective-permute-done.10.q1, bf16[2,256,512]{2,1,0:T(8,128)(2,1)S(1)} %copy-done.12, bf16[4096,512]{1,0:T(8,128)(2,1)} %key_unit.1.k_own, ...), custom_call_target="tpu_custom_call" | custom-call | flops 1072000000 | bytes 8388608 | tf_op jit(solution)/shard_map/memory_attention/pallas_call | solution.py:137
  97.9 2.2 %add_convert_fusion.1 = bf16[2,272,512]{2,1,0:T(8,128)(2,1)} fusion(bf16[2,272,512]{2,1,0:T(8,128)(2,1)} %collective-permute-done.19, bf16[2,272,512]{2,1,0:T(8,128)(2,1)S(1)} %get-tuple-element.26), kind=kLoop, calls=%fused_computation.2 | loop fusion | flops 1114112 | bytes 1671168 | tf_op jit(solution)/shard_map/convert_element_type | solution.py:229
  100.1 4.1 %collective-permute-start.20 = (bf16[2,272,512]{2,1,0:T(8,128)(2,1)}, bf16[2,272,512]{2,1,0:T(8,128)(2,1)}, u32[]{:S(2)}, u32[]{:S(2)}) collective-permute-start(bf16[2,272,512]{2,1,0:T(8,128)(2,1)} %add_convert_fusion.1), channel_id=1, source_target_pairs={{0,24},{4,100},{8,0},{12,108},{16,8},{20,116},{24,16},{28,124},{32... | collective-permute-start | bytes 1671176 | tf_op jit(solution)/shard_map/ppermute | solution.py:196
  104.3 1.6 %copy-done.2 = bf16[2048,512]{1,0:T(8,128)(2,1)S(1)} copy-done((bf16[2048,512]{1,0:T(8,128)(2,1)S(1)}, bf16[2048,512]{1,0:T(8,128)(2,1)}, u32[]{:S(2)}) %copy-start.2) | copy-done | bytes 2097176
  105.9 1.2 copy-done.8
  107.2 1.8 %local_kv.1.kv = bf16[2,256,512]{2,1,0:T(8,128)(2,1)S(1)} custom-call(s32[4]{0:T(128)S(1)} %get-tuple-element.52.order, bf16[4,256,512]{2,1,0:T(8,128)(2,1)S(1)} %copy-done.8, bf16[4,512,512]{2,1,0:T(8,128)(2,1)S(1)} %bitcast.31, bf16[4,512,512]{2,1,0:T(8,128)(2,1)S(1)} %bitcast.32), custom_call_target="tpu_custom_call" | custom-call | flops 1073741824 | bytes 6291456 | tf_op jit(solution)/shard_map/local_kv/pallas_call | solution.py:300
  109.0 2.2 %collective-permute-start.23 = (bf16[2,256,512]{2,1,0:T(8,128)(2,1)S(1)}, bf16[2,256,512]{2,1,0:T(8,128)(2,1)}, u32[]{:S(2)}, u32[]{:S(2)}) collective-permute-start(bf16[2,256,512]{2,1,0:T(8,128)(2,1)S(1)} %local_kv.1.kv), channel_id=1, source_target_pairs={{0,4},{4,8},{8,12},{12,16},{16,20},{20,24},{24,28},{28,32},{32,36}... | collective-permute-start | bytes 1572872 | tf_op jit(solution)/shard_map/ppermute | solution.py:324
  111.2 1.2 add_convert_fusion.3
  112.4 2.1 %collective-permute-start.14 = (bf16[2,272,512]{2,1,0:T(8,128)(2,1)S(1)}, bf16[2,272,512]{2,1,0:T(8,128)(2,1)S(1)}, u32[]{:S(2)}, u32[]{:S(2)}) collective-permute-start(bf16[2,272,512]{2,1,0:T(8,128)(2,1)S(1)} %add_convert_fusion.3), channel_id=1, source_target_pairs={{0,8},{4,36},{8,16},{12,44},{16,24},{20,52},{24,0},{28,60},{32,40}... | collective-permute-start | bytes 1671176 | tf_op jit(solution)/shard_map/ppermute | solution.py:196
  114.5 6.2 %memory_attention.4 = (bf16[2,272,512]{2,1,0:T(8,128)(2,1)S(1)}, bf16[2,272,512]{2,1,0:T(8,128)(2,1)S(1)}) custom-call(s32[4,6]{1,0:T(4,128)S(1)} %bitcast.36, f32[4]{0:T(128)S(1)} %copy-done.21, bf16[2,256,512]{2,1,0:T(8,128)(2,1)S(1)} %pad_maximum_fusion.q1, bf16[2,256,512]{2,1,0:T(8,128)(2,1)S(1)} %copy-done.4, bf16[4096,512]{1,0:T(8,128)(2,1)} %key_unit.1.k_own, ...), custom_call_target="tpu_custom_call" | custom-call | flops 1072000000 | bytes 8388608 | tf_op jit(solution)/shard_map/memory_attention/pallas_call | solution.py:137
  120.8 1.4 add_convert_fusion
  122.2 0.9 slice_bitcast_fusion
  123.1 4.9 %collective-permute-start.22 = (bf16[272,512]{1,0:T(8,128)(2,1)}, bf16[272,512]{1,0:T(8,128)(2,1)}, u32[]{:S(2)}, u32[]{:S(2)}) collective-permute-start(bf16[272,512]{1,0:T(8,128)(2,1)} %get-tuple-element.38), channel_id=1, source_target_pairs={{0,64},{4,20},{8,72},{12,28},{16,80},{20,4},{24,88},{28,12},{32,96... | collective-permute-start | bytes 835592 | tf_op jit(solution)/shard_map/ppermute | solution.py:191
  128.9 3.2 %collective-permute-start.17 = (bf16[272,512]{1,0:T(8,128)(2,1)}, bf16[272,512]{1,0:T(8,128)(2,1)}, u32[]{:S(2)}, u32[]{:S(2)}) collective-permute-start(bf16[272,512]{1,0:T(8,128)(2,1)} %get-tuple-element.40), channel_id=1, source_target_pairs={{0,96},{4,28},{8,104},{12,4},{16,112},{20,12},{24,120},{28,20},{32... | collective-permute-start | bytes 835592 | tf_op jit(solution)/shard_map/ppermute | solution.py:191
  132.2 0.8 dynamic-slice_select_fusion
  133.2 2.1 %local_attention.1.local = f32[256,512]{1,0:T(8,128)S(1)} custom-call(f32[4]{0:T(128)S(1)} %copy-done.21, s32[256,1]{1,0:T(8,128)S(1)} %copy.34.seg_own, s32[1,512]{1,0:T(1,128)S(1)} %bitcast.35, bf16[256,512]{1,0:T(8,128)(2,1)S(1)} %get-tuple-element.19.queries, bf16[2,256,512]{2,1,0:T(8,128)(2,1)S(1)} %local_kv.1.kv, ...), custom_call_target="tpu_custom_call" | custom-call | flops 268435456 | bytes 2097152 | tf_op jit(solution)/shard_map/local_attention/pallas_call | solution.py:332
  136.6 3.1 %merge_output.1 = (bf16[64,2048]{1,0:T(8,128)(2,1)S(1)}, bf16[64,2048]{1,0:T(8,128)(2,1)S(1)}, bf16[64,2048]{1,0:T(8,128)(2,1)S(1)}, bf16[64,2048]{1,0:T(8,128)(2,1)S(1)}) custom-call(s32[4]{0:T(128)S(1)} %get-tuple-element.52.order, f32[4]{0:T(128)S(1)} %copy-done.22, bf16[272,512]{1,0:T(8,128)(2,1)S(1)} %get-tuple-element.41.w, ...), custom_call_target="tpu_custom_call" | custom-call | flops 536870912 | bytes 5242880 | tf_op jit(solution)/shard_map/merge_output/pallas_call | solution.py:363
  140.0 1.8 %collective-permute-start.25 = (bf16[64,2048]{1,0:T(8,128)(2,1)S(1)}, bf16[64,2048]{1,0:T(8,128)(2,1)S(1)}, u32[]{:S(2)}, u32[]{:S(2)}) collective-permute-start(bf16[64,2048]{1,0:T(8,128)(2,1)S(1)} %get-tuple-element.31), channel_id=1, source_target_pairs={{0,1},{1,2},{2,3},{3,0},{4,5},{5,6},{6,7},{7,4},{8,9},{9,10},{10,1... | collective-permute-start | bytes 786440 | tf_op jit(solution)/shard_map/ppermute | solution.py:204
  141.7 7.2 %collective-permute-done.24 = bf16[64,2048]{1,0:T(8,128)(2,1)S(1)} collective-permute-done((bf16[64,2048]{1,0:T(8,128)(2,1)S(1)}, bf16[64,2048]{1,0:T(8,128)(2,1)S(1)}, u32[]{:S(2)}, u32[]{:S(2)}) %collective-permute-start.24) | collective-permute-done | bytes 262176 | tf_op jit(solution)/shard_map/ppermute | solution.py:204
  149.0 5.1 %collective-permute-done.25 = bf16[64,2048]{1,0:T(8,128)(2,1)S(1)} collective-permute-done((bf16[64,2048]{1,0:T(8,128)(2,1)S(1)}, bf16[64,2048]{1,0:T(8,128)(2,1)S(1)}, u32[]{:S(2)}, u32[]{:S(2)}) %collective-permute-start.25) | collective-permute-done | bytes 262176 | tf_op jit(solution)/shard_map/ppermute | solution.py:204
  154.0 0.8 add_convert_fusion.4
  (112 shorter events, 11.0 us)
Async XLA Ops:
  0.0 12.9 %copy-start.27 = (s32[4]{0:T(128)S(1)}, s32[4]{0:T(128)}, u32[]{:S(2)}) copy-start(s32[4]{0:T(128)} %constant.142.clone) | copy-start | bytes 52
  0.0 2.2 %copy-start = (bf16[4096,512]{1,0:T(8,128)(2,1)S(1)}, bf16[4096,512]{1,0:T(8,128)(2,1)}, u32[]{:S(2)}) copy-start(bf16[4096,512]{1,0:T(8,128)(2,1)} %raw.1) | copy-start | bytes 12582916
  2.2 5.5 %copy-start.13 = (bf16[256,512]{1,0:T(8,128)(2,1)S(1)}, bf16[256,512]{1,0:T(8,128)(2,1)}, u32[]{:S(2)}) copy-start(bf16[256,512]{1,0:T(8,128)(2,1)} %x0.1) | copy-start | bytes 786436
  2.2 11.1 %copy-start.25 = (bf16[2048]{0:T(1024)(128)(2,1)S(1)}, bf16[2048]{0:T(1024)(128)(2,1)}, u32[]{:S(2)}) copy-start(bf16[2048]{0:T(1024)(128)(2,1)} %param.16) | copy-start | bytes 12292
  2.2 24.5 %copy-start.5 = (bf16[2048,512]{1,0:T(8,128)(2,1)S(1)}, bf16[2048,512]{1,0:T(8,128)(2,1)}, u32[]{:S(2)}) copy-start(bf16[2048,512]{1,0:T(8,128)(2,1)} %param.17) | copy-start | bytes 6291460
  7.2 62.8 %collective-permute-start.6 = (bf16[4096,512]{1,0:T(8,128)(2,1)}, bf16[4096,512]{1,0:T(8,128)(2,1)}, u32[]{:S(2)}, u32[]{:S(2)}) collective-permute-start(bf16[4096,512]{1,0:T(8,128)(2,1)} %key_unit.1.k_own), channel_id=1, source_target_pairs={{0,4},{4,0},{8,12},{12,8},{16,20},{20,16},{24,28},{28,24},{32,36},... | collective-permute-start | bytes 12582920 | tf_op jit(solution)/shard_map/ppermute | solution.py:200
  7.2 62.8 %collective-permute-start.7 = (bf16[4096,512]{1,0:T(8,128)(2,1)}, bf16[4096,512]{1,0:T(8,128)(2,1)}, u32[]{:S(2)}, u32[]{:S(2)}) collective-permute-start(bf16[4096,512]{1,0:T(8,128)(2,1)} %v_own.7), channel_id=1, source_target_pairs={{0,4},{4,0},{8,12},{12,8},{16,20},{20,16},{24,28},{28,24},{32,36},... | collective-permute-start | bytes 12582920 | tf_op jit(solution)/shard_map/ppermute | solution.py:200
  7.7 14.2 %collective-permute-start.1 = (bf16[256,512]{1,0:T(8,128)(2,1)S(1)}, bf16[256,512]{1,0:T(8,128)(2,1)S(1)}, u32[]{:S(2)}, u32[]{:S(2)}) collective-permute-start(bf16[256,512]{1,0:T(8,128)(2,1)S(1)} %copy-done.13), channel_id=1, source_target_pairs={{0,3},{1,0},{2,1},{3,2},{4,7},{5,4},{6,5},{7,6},{8,11},{9,8},{10,9... | collective-permute-start | bytes 786440 | tf_op jit(solution)/shard_map/ppermute | solution.py:204
  10.6 14.8 %collective-permute-start = (bf16[256,512]{1,0:T(8,128)(2,1)S(1)}, bf16[256,512]{1,0:T(8,128)(2,1)S(1)}, u32[]{:S(2)}, u32[]{:S(2)}) collective-permute-start(bf16[256,512]{1,0:T(8,128)(2,1)S(1)} %copy-done.13), channel_id=1, source_target_pairs={{0,1},{1,2},{2,3},{3,0},{4,5},{5,6},{6,7},{7,4},{8,9},{9,10},{10,1... | collective-permute-start | bytes 786440 | tf_op jit(solution)/shard_map/ppermute | solution.py:204
  10.6 15.5 %collective-permute-start.2 = (bf16[256,512]{1,0:T(8,128)(2,1)S(1)}, bf16[256,512]{1,0:T(8,128)(2,1)S(1)}, u32[]{:S(2)}, u32[]{:S(2)}) collective-permute-start(bf16[256,512]{1,0:T(8,128)(2,1)S(1)} %copy-done.13), channel_id=1, source_target_pairs={{0,2},{1,3},{2,0},{3,1},{4,6},{5,7},{6,4},{7,5},{8,10},{9,11},{10,... | collective-permute-start | bytes 786440 | tf_op jit(solution)/shard_map/ppermute | solution.py:204
  26.8 1.0 copy-start.14
  27.7 0.9 copy-start.16
  30.6 9.2 %copy-start.26 = (s32[64,8]{0,1:T(8,128)S(1)}, s32[64,8]{0,1:T(8,128)}, u32[]{:S(2)}) copy-start(s32[64,8]{0,1:T(8,128)} %param.25) | copy-start | bytes 6148
  32.2 1.0 copy-start.7
  33.2 8.4 %collective-permute-start.3 = (bf16[256,512]{1,0:T(8,128)(2,1)S(1)}, bf16[256,512]{1,0:T(8,128)(2,1)S(1)}, u32[]{:S(2)}, u32[]{:S(2)}) collective-permute-start(bf16[256,512]{1,0:T(8,128)(2,1)S(1)} %get-tuple-element.19.queries), channel_id=1, source_target_pairs={{0,32},{4,12},{8,40},{12,20},{16,48},{20,28},{24,56},{28,4},{32,64... | collective-permute-start | bytes 786440 | tf_op jit(solution)/shard_map/ppermute | solution.py:191
  35.1 13.4 %collective-permute-start.5 = (bf16[256,512]{1,0:T(8,128)(2,1)S(1)}, bf16[256,512]{1,0:T(8,128)(2,1)S(1)}, u32[]{:S(2)}, u32[]{:S(2)}) collective-permute-start(bf16[256,512]{1,0:T(8,128)(2,1)S(1)} %get-tuple-element.19.queries), channel_id=1, source_target_pairs={{0,64},{4,20},{8,72},{12,28},{16,80},{20,4},{24,88},{28,12},{32,96... | collective-permute-start | bytes 786440 | tf_op jit(solution)/shard_map/ppermute | solution.py:191
  38.8 9.8 %collective-permute-start.4 = (bf16[256,512]{1,0:T(8,128)(2,1)S(1)}, bf16[256,512]{1,0:T(8,128)(2,1)S(1)}, u32[]{:S(2)}, u32[]{:S(2)}) collective-permute-start(bf16[256,512]{1,0:T(8,128)(2,1)S(1)} %get-tuple-element.19.queries), channel_id=1, source_target_pairs={{0,96},{4,28},{8,104},{12,4},{16,112},{20,12},{24,120},{28,20},{32... | collective-permute-start | bytes 786440 | tf_op jit(solution)/shard_map/ppermute | solution.py:191
  41.6 28.5 %copy-start.21 = (f32[4]{0:T(128)S(1)}, f32[4]{0:T(128)}, u32[]{:S(2)}) copy-start(f32[4]{0:T(128)} %sharp.9) | copy-start | bytes 52
  41.6 12.1 %collective-permute-start.10 = (bf16[2,256,512]{2,1,0:T(8,128)(2,1)S(1)}, bf16[2,256,512]{2,1,0:T(8,128)(2,1)S(1)}, u32[]{:S(2)}, u32[]{:S(2)}) collective-permute-start(bf16[2,256,512]{2,1,0:T(8,128)(2,1)S(1)} %pad_maximum_fusion.q1), channel_id=1, source_target_pairs={{0,8},{4,36},{8,16},{12,44},{16,24},{20,52},{24,0},{28,60},{32,40}... | collective-permute-start | bytes 1572872 | tf_op jit(solution)/shard_map/ppermute | solution.py:196
  48.6 30.7 %copy-start.3 = (bf16[2,256,512]{2,1,0:T(8,128)(2,1)}, bf16[2,256,512]{2,1,0:T(8,128)(2,1)S(1)}, u32[]{:S(2)}) copy-start(bf16[2,256,512]{2,1,0:T(8,128)(2,1)S(1)} %pad_maximum_fusion.1.q2) | copy-start | bytes 1572868
  48.6 11.1 %collective-permute-start.9 = (bf16[2,256,512]{2,1,0:T(8,128)(2,1)S(1)}, bf16[2,256,512]{2,1,0:T(8,128)(2,1)S(1)}, u32[]{:S(2)}, u32[]{:S(2)}) collective-permute-start(bf16[2,256,512]{2,1,0:T(8,128)(2,1)S(1)} %pad_maximum_fusion.1.q2), channel_id=1, source_target_pairs={{0,24},{4,100},{8,0},{12,108},{16,8},{20,116},{24,16},{28,124},{32... | collective-permute-start | bytes 1572872 | tf_op jit(solution)/shard_map/ppermute | solution.py:196
  53.7 10.4 %collective-permute-start.11 = (bf16[2,256,512]{2,1,0:T(8,128)(2,1)S(1)}, bf16[2,256,512]{2,1,0:T(8,128)(2,1)S(1)}, u32[]{:S(2)}, u32[]{:S(2)}) collective-permute-start(bf16[2,256,512]{2,1,0:T(8,128)(2,1)S(1)} %collective-permute-done.10.q1), channel_id=1, source_target_pairs={{0,8},{4,36},{8,16},{12,44},{16,24},{20,52},{24,0},{28,60},{32,40}... | collective-permute-start | bytes 1572872 | tf_op jit(solution)/shard_map/ppermute | solution.py:196
  59.7 10.4 %collective-permute-start.12 = (bf16[2,256,512]{2,1,0:T(8,128)(2,1)S(1)}, bf16[2,256,512]{2,1,0:T(8,128)(2,1)}, u32[]{:S(2)}, u32[]{:S(2)}) collective-permute-start(bf16[2,256,512]{2,1,0:T(8,128)(2,1)S(1)} %collective-permute-done.9.q2), channel_id=1, source_target_pairs={{0,24},{4,100},{8,0},{12,108},{16,8},{20,116},{24,16},{28,124},{32... | collective-permute-start | bytes 1572872 | tf_op jit(solution)/shard_map/ppermute | solution.py:196
  63.5 16.8 %collective-permute-start.8 = (bf16[2,256,512]{2,1,0:T(8,128)(2,1)S(1)}, bf16[2,256,512]{2,1,0:T(8,128)(2,1)}, u32[]{:S(2)}, u32[]{:S(2)}) collective-permute-start(bf16[2,256,512]{2,1,0:T(8,128)(2,1)S(1)} %pad_maximum_fusion.q1), channel_id=1, source_target_pairs={{0,24},{4,100},{8,0},{12,108},{16,8},{20,116},{24,16},{28,124},{32... | collective-permute-start | bytes 1572872 | tf_op jit(solution)/shard_map/ppermute | solution.py:196
  64.1 24.5 %collective-permute-start.15 = (bf16[2,256,512]{2,1,0:T(8,128)(2,1)S(1)}, bf16[2,256,512]{2,1,0:T(8,128)(2,1)S(1)}, u32[]{:S(2)}, u32[]{:S(2)}) collective-permute-start(bf16[2,256,512]{2,1,0:T(8,128)(2,1)S(1)} %pad_maximum_fusion.1.q2), channel_id=1, source_target_pairs={{0,8},{4,36},{8,16},{12,44},{16,24},{20,52},{24,0},{28,60},{32,40}... | collective-permute-start | bytes 1572872 | tf_op jit(solution)/shard_map/ppermute | solution.py:196
  79.3 18.6 %collective-permute-start.19 = (bf16[2,272,512]{2,1,0:T(8,128)(2,1)}, bf16[2,272,512]{2,1,0:T(8,128)(2,1)}, u32[]{:S(2)}, u32[]{:S(2)}) collective-permute-start(bf16[2,272,512]{2,1,0:T(8,128)(2,1)} %get-tuple-element.27), channel_id=1, source_target_pairs={{0,24},{4,100},{8,0},{12,108},{16,8},{20,116},{24,16},{28,124},{32... | collective-permute-start | bytes 1671176 | tf_op jit(solution)/shard_map/ppermute | solution.py:196
  87.3 33.4 %collective-permute-start.18 = (bf16[2,272,512]{2,1,0:T(8,128)(2,1)}, bf16[2,272,512]{2,1,0:T(8,128)(2,1)}, u32[]{:S(2)}, u32[]{:S(2)}) collective-permute-start(bf16[2,272,512]{2,1,0:T(8,128)(2,1)} %get-tuple-element.25), channel_id=1, source_target_pairs={{0,8},{4,36},{8,16},{12,44},{16,24},{20,52},{24,0},{28,60},{32,40}... | collective-permute-start | bytes 1671176 | tf_op jit(solution)/shard_map/ppermute | solution.py:196
  88.6 22.6 %collective-permute-start.13 = (bf16[2,272,512]{2,1,0:T(8,128)(2,1)}, bf16[2,272,512]{2,1,0:T(8,128)(2,1)}, u32[]{:S(2)}, u32[]{:S(2)}) collective-permute-start(bf16[2,272,512]{2,1,0:T(8,128)(2,1)} %get-tuple-element.22), channel_id=1, source_target_pairs={{0,8},{4,36},{8,16},{12,44},{16,24},{20,52},{24,0},{28,60},{32,40}... | collective-permute-start | bytes 1671176 | tf_op jit(solution)/shard_map/ppermute | solution.py:196
  89.4 1.0 copy-start.12
  90.5 13.9 %copy-start.1 = (bf16[2048,512]{1,0:T(8,128)(2,1)S(1)}, bf16[2048,512]{1,0:T(8,128)(2,1)}, u32[]{:S(2)}) copy-start(bf16[2048,512]{1,0:T(8,128)(2,1)} %param.18) | copy-start | bytes 6291460
  97.9 6.4 %copy-start.23 = (bf16[2,272,512]{2,1,0:T(8,128)(2,1)}, bf16[2,272,512]{2,1,0:T(8,128)(2,1)S(1)}, u32[]{:S(2)}) copy-start(bf16[2,272,512]{2,1,0:T(8,128)(2,1)S(1)} %get-tuple-element.23) | copy-start | bytes 1671172
  100.1 20.6 %collective-permute-start.20 = (bf16[2,272,512]{2,1,0:T(8,128)(2,1)}, bf16[2,272,512]{2,1,0:T(8,128)(2,1)}, u32[]{:S(2)}, u32[]{:S(2)}) collective-permute-start(bf16[2,272,512]{2,1,0:T(8,128)(2,1)} %add_convert_fusion.1), channel_id=1, source_target_pairs={{0,24},{4,100},{8,0},{12,108},{16,8},{20,116},{24,16},{28,124},{32... | collective-permute-start | bytes 1671176 | tf_op jit(solution)/shard_map/ppermute | solution.py:196
  104.3 1.6 %copy-start.2 = (bf16[2048,512]{1,0:T(8,128)(2,1)S(1)}, bf16[2048,512]{1,0:T(8,128)(2,1)}, u32[]{:S(2)}) copy-start(bf16[2048,512]{1,0:T(8,128)(2,1)} %param.19) | copy-start | bytes 6291460
  105.9 1.2 copy-start.8
  107.2 4.1 %copy-start.24 = (bf16[2,272,512]{2,1,0:T(8,128)(2,1)S(1)}, bf16[2,272,512]{2,1,0:T(8,128)(2,1)}, u32[]{:S(2)}) copy-start(bf16[2,272,512]{2,1,0:T(8,128)(2,1)} %copy-done.23) | copy-start | bytes 1671172
  107.2 4.1 %copy-start.10 = (bf16[2,272,512]{2,1,0:T(8,128)(2,1)S(1)}, bf16[2,272,512]{2,1,0:T(8,128)(2,1)}, u32[]{:S(2)}) copy-start(bf16[2,272,512]{2,1,0:T(8,128)(2,1)} %copy-done.9) | copy-start | bytes 1671172
  109.0 5.5 %copy-start.4 = (bf16[2,256,512]{2,1,0:T(8,128)(2,1)S(1)}, bf16[2,256,512]{2,1,0:T(8,128)(2,1)}, u32[]{:S(2)}) copy-start(bf16[2,256,512]{2,1,0:T(8,128)(2,1)} %copy-done.3) | copy-start | bytes 1572868
  109.0 24.2 %collective-permute-start.23 = (bf16[2,256,512]{2,1,0:T(8,128)(2,1)S(1)}, bf16[2,256,512]{2,1,0:T(8,128)(2,1)}, u32[]{:S(2)}, u32[]{:S(2)}) collective-permute-start(bf16[2,256,512]{2,1,0:T(8,128)(2,1)S(1)} %local_kv.1.kv), channel_id=1, source_target_pairs={{0,4},{4,8},{8,12},{12,16},{16,20},{20,24},{24,28},{28,32},{32,36}... | collective-permute-start | bytes 1572872 | tf_op jit(solution)/shard_map/ppermute | solution.py:324
  111.2 16.7 %collective-permute-start.16 = (bf16[2,272,512]{2,1,0:T(8,128)(2,1)S(1)}, bf16[2,272,512]{2,1,0:T(8,128)(2,1)S(1)}, u32[]{:S(2)}, u32[]{:S(2)}) collective-permute-start(bf16[2,272,512]{2,1,0:T(8,128)(2,1)S(1)} %copy-done.24), channel_id=1, source_target_pairs={{0,24},{4,100},{8,0},{12,108},{16,8},{20,116},{24,16},{28,124},{32... | collective-permute-start | bytes 1671176 | tf_op jit(solution)/shard_map/ppermute | solution.py:196
  112.4 15.5 %collective-permute-start.14 = (bf16[2,272,512]{2,1,0:T(8,128)(2,1)S(1)}, bf16[2,272,512]{2,1,0:T(8,128)(2,1)S(1)}, u32[]{:S(2)}, u32[]{:S(2)}) collective-permute-start(bf16[2,272,512]{2,1,0:T(8,128)(2,1)S(1)} %add_convert_fusion.3), channel_id=1, source_target_pairs={{0,8},{4,36},{8,16},{12,44},{16,24},{20,52},{24,0},{28,60},{32,40}... | collective-permute-start | bytes 1671176 | tf_op jit(solution)/shard_map/ppermute | solution.py:196
  123.1 12.2 %collective-permute-start.22 = (bf16[272,512]{1,0:T(8,128)(2,1)}, bf16[272,512]{1,0:T(8,128)(2,1)}, u32[]{:S(2)}, u32[]{:S(2)}) collective-permute-start(bf16[272,512]{1,0:T(8,128)(2,1)} %get-tuple-element.38), channel_id=1, source_target_pairs={{0,64},{4,20},{8,72},{12,28},{16,80},{20,4},{24,88},{28,12},{32,96... | collective-permute-start | bytes 835592 | tf_op jit(solution)/shard_map/ppermute | solution.py:191
  128.0 8.1 %collective-permute-start.21 = (bf16[272,512]{1,0:T(8,128)(2,1)}, bf16[272,512]{1,0:T(8,128)(2,1)}, u32[]{:S(2)}, u32[]{:S(2)}) collective-permute-start(bf16[272,512]{1,0:T(8,128)(2,1)} %get-tuple-element.39), channel_id=1, source_target_pairs={{0,32},{4,12},{8,40},{12,20},{16,48},{20,28},{24,56},{28,4},{32,64... | collective-permute-start | bytes 835592 | tf_op jit(solution)/shard_map/ppermute | solution.py:191
  128.9 7.6 %copy-start.6 = (bf16[512,2048]{1,0:T(8,128)(2,1)S(1)}, bf16[512,2048]{1,0:T(8,128)(2,1)}, u32[]{:S(2)}) copy-start(bf16[512,2048]{1,0:T(8,128)(2,1)} %weight.1) | copy-start | bytes 6291460
  128.9 7.6 %copy-start.22 = (f32[4]{0:T(128)S(1)}, f32[4]{0:T(128)}, u32[]{:S(2)}) copy-start(f32[4]{0:T(128)} %bias.1) | copy-start | bytes 52
  128.9 7.6 %collective-permute-start.17 = (bf16[272,512]{1,0:T(8,128)(2,1)}, bf16[272,512]{1,0:T(8,128)(2,1)}, u32[]{:S(2)}, u32[]{:S(2)}) collective-permute-start(bf16[272,512]{1,0:T(8,128)(2,1)} %get-tuple-element.40), channel_id=1, source_target_pairs={{0,96},{4,28},{8,104},{12,4},{16,112},{20,12},{24,120},{28,20},{32... | collective-permute-start | bytes 835592 | tf_op jit(solution)/shard_map/ppermute | solution.py:191
  139.6 9.3 %collective-permute-start.24 = (bf16[64,2048]{1,0:T(8,128)(2,1)S(1)}, bf16[64,2048]{1,0:T(8,128)(2,1)S(1)}, u32[]{:S(2)}, u32[]{:S(2)}) collective-permute-start(bf16[64,2048]{1,0:T(8,128)(2,1)S(1)} %get-tuple-element.30), channel_id=1, source_target_pairs={{0,3},{1,0},{2,1},{3,2},{4,7},{5,4},{6,5},{7,6},{8,11},{9,8},{10,9... | collective-permute-start | bytes 786440 | tf_op jit(solution)/shard_map/ppermute | solution.py:204
  140.0 14.0 %collective-permute-start.25 = (bf16[64,2048]{1,0:T(8,128)(2,1)S(1)}, bf16[64,2048]{1,0:T(8,128)(2,1)S(1)}, u32[]{:S(2)}, u32[]{:S(2)}) collective-permute-start(bf16[64,2048]{1,0:T(8,128)(2,1)S(1)} %get-tuple-element.31), channel_id=1, source_target_pairs={{0,1},{1,2},{2,3},{3,0},{4,5},{5,6},{6,7},{7,4},{8,9},{9,10},{10,1... | collective-permute-start | bytes 786440 | tf_op jit(solution)/shard_map/ppermute | solution.py:204
  141.7 12.3 %collective-permute-start.26 = (bf16[64,2048]{1,0:T(8,128)(2,1)S(1)}, bf16[64,2048]{1,0:T(8,128)(2,1)S(1)}, u32[]{:S(2)}, u32[]{:S(2)}) collective-permute-start(bf16[64,2048]{1,0:T(8,128)(2,1)S(1)} %get-tuple-element.32), channel_id=1, source_target_pairs={{0,2},{1,3},{2,0},{3,1},{4,6},{5,7},{6,4},{7,5},{8,10},{9,11},{10,... | collective-permute-start | bytes 786440 | tf_op jit(solution)/shard_map/ppermute | solution.py:204
  (7 other events, 5.6 us)

commit v2 on v1

v2 whole, which is shorter than its diff:
```python
import functools

import jax
import jax.numpy as jnp
from jax import lax
from jax.experimental import pallas as pl
from jax.experimental.pallas import tpu as pltpu
from jax.sharding import PartitionSpec as P

QB = 128
MB = 512
LOCAL = 256
HD = 128
LOG2E = 1.4426950408889634
NT = (((1,), (1,)), ((), ()))
VMEM = pl.BlockSpec(memory_space=pltpu.VMEM)
SMEM = pl.BlockSpec(memory_space=pltpu.SMEM)
F32 = jnp.float32
BF16 = jnp.bfloat16


def params(mib=40):
    return pltpu.CompilerParams(vmem_limit_bytes=mib * 2**20)


def cost(us):
    return pl.CostEstimate(flops=1, bytes_accessed=int(us * 3.69e6), transcendentals=0)


def unit_into(ref, rows, value):
    for h in range(value.shape[1] // HD):
        part = value[:, h * HD : (h + 1) * HD]
        scale = lax.rsqrt(jnp.mean(part * part, axis=-1, keepdims=True) + 1e-06)
        ref[rows, h * HD : (h + 1) * HD] = (part * scale).astype(BF16)


def norm_pieces(order, pieces, gain):
    pieces = [x[...].astype(F32) for x in pieces]
    total = sum(jnp.sum(p * p, axis=-1, keepdims=True) for p in pieces)
    scale = lax.rsqrt(total / (4 * pieces[0].shape[1]) + 1e-05)
    return [
        (piece * scale * gain[order[p]].astype(F32)).astype(BF16)
        for p, piece in enumerate(pieces)
    ]


def project(order, normed, weight):
    result = None
    for p, value in enumerate(normed):
        term = jnp.dot(value, weight[order[p]], preferred_element_type=F32)
        result = term if result is None else result + term
    return result


def query_kernel(order, x0, x1, x2, x3, gain, weight, queries, x, w, x_sem, w_sem):
    loads = [
        pltpu.make_async_copy(part, x.at[p], x_sem.at[p]) for p, part in enumerate((x0, x1, x2, x3))
    ]
    fetches = [
        pltpu.make_async_copy(weight.at[order[p]], w.at[p], w_sem.at[p]) for p in range(4)
    ]
    for copy in loads + fetches:
        copy.start()
    for copy in loads:
        copy.wait()
    normed = norm_pieces(order, [x.at[p] for p in range(4)], gain)
    result = None
    for p, value in enumerate(normed):
        fetches[p].wait()
        term = jnp.dot(value, w[p], preferred_element_type=F32)
        result = term if result is None else result + term
    unit_into(queries, slice(None), result)


def kv_kernel(order, x0, x1, x2, x3, gain, key_weight, value_weight, kv):
    normed = norm_pieces(order, (x0, x1, x2, x3), gain)
    unit_into(kv.at[0], slice(None), project(order, normed, key_weight))
    kv[1] = project(order, normed, value_weight).astype(BF16)


def key_unit_kernel(raw, keys, x, sem):
    blocks = x.shape[0]
    loads = [
        pltpu.make_async_copy(raw.at[pl.ds(b * MB, MB)], x.at[b], sem.at[b]) for b in range(blocks)
    ]
    for load in loads:
        load.start()
    wide = 2 * HD
    place = lambda d: lax.broadcasted_iota(jnp.int32, (wide, wide), d) // HD
    ones = (place(0) == place(1)).astype(BF16)

    def step(b, _):
        pltpu.make_async_copy(raw.at[pl.ds(0, MB)], x.at[b], sem.at[b]).wait()
        rows = pl.ds(pl.multiple_of(b * MB, MB), MB)
        for c in range(x.shape[2] // wide):
            cols = slice(c * wide, (c + 1) * wide)
            part = x[b, :, cols].astype(F32)
            total = jnp.dot((part * part).astype(BF16), ones, preferred_element_type=F32)
            keys[rows, cols] = (part * lax.rsqrt(total * (1 / HD) + 1e-06)).astype(BF16)
        return 0

    lax.fori_loop(0, blocks, step, 0)


def key_unit(raw):
    blocks = raw.shape[0] // MB
    return pl.pallas_call(
        key_unit_kernel,
        in_specs=[pl.BlockSpec(memory_space=pl.ANY)],
        out_specs=VMEM,
        out_shape=jax.ShapeDtypeStruct(raw.shape, BF16),
        scratch_shapes=[
            pltpu.VMEM((blocks, MB, raw.shape[1]), BF16),
            pltpu.SemaphoreType.DMA((blocks,)),
        ],
        compiler_params=params(),
        cost_estimate=cost(6),
        name="key_unit",
    )(raw)


def local_kernel(index, sharp, labels, queries, kv, before, out):
    rows = queries.shape[0]
    place = lax.broadcasted_iota(jnp.int32, (rows, rows), 0)
    other = lax.broadcasted_iota(jnp.int32, (rows, rows), 1)
    line = lambda r: labels[pl.ds(r, 1), :].astype(F32)
    here = 2 * index[0]
    own = [line(here), line(here + 1)]
    past = [line(jnp.maximum(here - 2, 0)), line(jnp.maximum(here - 1, 0))]
    queried = jnp.concatenate(
        [jnp.transpose(jnp.broadcast_to(o, (QB, QB)))[:, :1] for o in own], axis=0
    )
    same_before = (queried == jnp.concatenate(past, axis=1)) & (index[0] > 0)
    same_own = queried == jnp.concatenate(own, axis=1)
    allow_before = (other > place) & same_before
    allow_own = (other <= place) & same_own
    for h in range(queries.shape[1] // HD):
        cols = slice(h * HD, (h + 1) * HD)
        scale = sharp[h] * (LOG2E / HD)
        q = queries[:, cols]
        numer = None
        total = None
        for keep, src in ((allow_before, before), (allow_own, kv)):
            s = lax.dot_general(q, src[0, :, cols], NT, preferred_element_type=F32)
            w = jnp.where(keep, jnp.exp2(s * scale), 0.0)
            t = jnp.sum(w, axis=-1, keepdims=True)
            n = jnp.dot(w.astype(BF16), src[1, :, cols], preferred_element_type=F32)
            numer = n if numer is None else numer + n
            total = t if total is None else total + t
        out[:, cols] = numer / total


def memory_kernel(first, meta, sharp, *refs):
    n = (len(refs) - 8) // 2
    parts, sources = refs[:n], (refs[n : n + 2], refs[n + 2 : n + 4])
    outs, (q, o, in_sem, out_sem) = refs[n + 4 : 2 * n + 4], refs[2 * n + 4 :]
    heads = q.shape[2] // HD
    loads = [
        pltpu.make_async_copy(parts[i // 2].at[i % 2], q.at[i], in_sem.at[i]) for i in range(2 * n)
    ]
    stores = [
        pltpu.make_async_copy(o.at[i], outs[i // 2].at[i % 2], out_sem.at[i]) for i in range(2 * n)
    ]
    for load in loads:
        load.start()
    eye = lax.broadcasted_iota(jnp.int32, (QB, QB), 0) == lax.broadcasted_iota(
        jnp.int32, (QB, QB), 1
    )
    tile_row = lax.broadcasted_iota(jnp.int32, (16, HD), 0)
    cols = [slice(h * HD, (h + 1) * HD) for h in range(heads)]
    o[...] = jnp.zeros_like(o)
    for load in loads:
        load.wait()

    def group(g, _):
        for j, (k, v) in enumerate(sources):
            base = ((first + g) * 2 + j) * 13

            def step(p, _, j=j, k=k, v=v, base=base):
                i = meta[base + 1 + p * 3] + 4 * g
                half = meta[base + 2 + p * 3]
                b = meta[base + 3 + p * 3]
                rows = pl.ds(pl.multiple_of(half * QB, QB), QB)
                span = pl.ds(pl.multiple_of(b * MB, MB), MB)
                scores = [
                    lax.dot_general(q[i, rows, c], k[span, c], NT, preferred_element_type=F32)
                    for c in cols
                ]
                weights = [jnp.exp2(s * (sharp[h] * (LOG2E / HD))) for h, s in enumerate(scores)]
                numers = [
                    jnp.dot(w.astype(BF16), v[span, c], preferred_element_type=F32)
                    for w, c in zip(weights, cols)
                ]
                lines = [
                    jnp.sum(
                        jnp.where(eye, jnp.sum(w, axis=-1, keepdims=True), 0.0),
                        axis=0,
                        keepdims=True,
                    )
                    for w in weights
                ]
                for num, line, c in zip(numers, lines, cols):
                    den = jnp.where(tile_row == half, line, 0.0)
                    if j == 1:
                        num = num + o[i, rows, c].astype(F32)
                        den = den + o[i, 2 * QB :, c].astype(F32)
                    o[i, rows, c] = num.astype(BF16)
                    o[i, 2 * QB :, c] = den.astype(BF16)
                return 0

            lax.fori_loop(0, meta[base], step, 0)
        return 0

    lax.fori_loop(0, n // 2, group, 0)
    for store in stores:
        store.start()
    for store in stores:
        store.wait()


def memory_attention(first, meta, sharp, parts, resident):
    width = parts[0].shape[2]
    n = len(parts)
    shape = jax.ShapeDtypeStruct((2, 2 * QB + 16, width), BF16)
    far = pl.BlockSpec(memory_space=pl.ANY)
    return pl.pallas_call(
        functools.partial(memory_kernel, first),
        in_specs=[SMEM, SMEM] + [far] * n + [VMEM] * 4,
        out_specs=[far] * n,
        out_shape=[shape] * n,
        scratch_shapes=[
            pltpu.VMEM((2 * n, 2 * QB, width), BF16),
            pltpu.VMEM((2 * n, 2 * QB + 16, width), BF16),
            pltpu.SemaphoreType.DMA((2 * n,)),
            pltpu.SemaphoreType.DMA((2 * n,)),
        ],
        compiler_params=params(),
        cost_estimate=cost(3 * n),
        name="memory_attention",
    )(meta, sharp, *parts, *resident)


def output_kernel(
    order, bias, z, u, v, x1, x2, x3, local, weight, c0, c1, c2, c3, mixed, w, w_sem
):
    fetch = pltpu.make_async_copy(weight, w, w_sem)
    fetch.start()
    total = z[0].astype(F32) + u[0].astype(F32) + v[0].astype(F32)
    total = total + x1[...].astype(F32) + x2[...].astype(F32) + x3[...].astype(F32)
    dens = total[2 * QB :, :]
    for h in range(total.shape[1] // HD):
        cols = slice(h * HD, (h + 1) * HD)
        gate = jax.nn.sigmoid(jnp.full((1, HD), bias[h], F32))
        turned = jnp.transpose(
            jnp.concatenate([dens[:, cols], jnp.zeros((HD - 16, HD), F32)], axis=0)
        )
        for b in range(2):
            rows = slice(b * QB, (b + 1) * QB)
            mem = total[rows, cols] / turned[:, b : b + 1]
            mixed[rows, cols] = (gate * mem + (1.0 - gate) * local[rows, cols]).astype(BF16)
    fetch.wait()
    for j, c in enumerate((c0, c1, c2, c3)):
        n = c.shape[0]
        rows = pl.ds(pl.multiple_of(order[j] * n, n), n)
        c[...] = jnp.dot(mixed[rows, :], w[...], preferred_element_type=F32).astype(c.dtype)


def mem_pairs(move):
    out = []
    for z in range(4):
        for y in range(4):
            for c in range(2):
                tz, ty, tc = move(z, y, c)
                out.append((z * 8 + y * 2 + c, (tz % 4) * 8 + (ty % 4) * 2 + tc))
    return out


def first_axis(value, by):
    pairs = mem_pairs(lambda z, y, c: (z + by, y, c) if c == 0 else (z, y + by, c))
    return lax.ppermute(value, "mem", pairs)


def second_axis(value, by):
    pairs = mem_pairs(lambda z, y, c: (z, y + by, c) if c == 0 else (z + by, y, c))
    return lax.ppermute(value, "mem", pairs)


def other_core(value):
    return lax.ppermute(value, "mem", mem_pairs(lambda z, y, c: (z, y, 1 - c)))


def along_tp(value, by):
    return lax.ppermute(value, "tp", [(i, (i + by) % 4) for i in range(4)])


def make_meta(assign, index, blocks_here):
    z, y, c = index // 8, (index // 2) % 4, index % 2
    shifts = jnp.array([0, -1, 1, 2], jnp.int32)
    second = jnp.array([0, -1, 1, 2], jnp.int32)[:, None]
    first = shifts[None, :]
    sz = jnp.where(c == 0, z + first, z + second) % 4
    sy = jnp.where(c == 0, y + second, y + first) % 4
    source = sz * 8 + sy * 2 + c
    ids = jnp.take(assign.reshape(-1, 16), source.reshape(-1), axis=0)
    holder = jnp.stack([index, index + 1 - 2 * c])
    hit = (ids // blocks_here)[:, None, :] == holder[None, :, None]
    here = jnp.any(hit, axis=-1).astype(jnp.int32).reshape(4, 4, 2)
    block = jnp.sum(jnp.where(hit, (ids % blocks_here)[:, None, :], 0), axis=-1).reshape(4, 4, 2)
    place = jnp.arange(16, dtype=jnp.int32)[None, None, :] // 8
    half = jnp.sum(jnp.where(hit, place, 0), axis=-1).reshape(4, 4, 2)
    slot = jnp.arange(4, dtype=jnp.int32)
    earlier = slot[:, None] > slot[None, :]
    rank = jnp.sum(jnp.where(earlier[None, :, :, None], here[:, None], 0), axis=2)
    chosen = (here[..., None] > 0) & (rank[..., None] == slot)
    fields = jnp.stack([jnp.broadcast_to(slot[None, :, None], here.shape), half, block], axis=-1)
    table = jnp.sum(jnp.where(chosen[..., None], fields[:, :, :, None, :], 0), axis=1)
    count = jnp.sum(here, axis=1)[..., None]
    return jnp.concatenate([count, table.reshape(4, 2, 12)], axis=-1).reshape(-1)


def add(a, b):
    return (a.astype(F32) + b.astype(F32)).astype(BF16)


def add3(a, b, c):
    return (a.astype(F32) + b.astype(F32) + c.astype(F32)).astype(BF16)


def ordered(first, *later):
    return lax.optimization_barrier((first,) + later)[1:]


FAR = pl.BlockSpec(memory_space=pl.ANY)


def call(us, kernel, name, scalars, arrays, shapes, far=(), scratch=()):
    whole = lambda a: pl.BlockSpec(a.shape, lambda i, n=len(a.shape): (0,) * n)
    specs = [SMEM] * len(scalars)
    values = list(scalars)
    for n, a in enumerate(arrays):
        if isinstance(a, tuple):
            a = a[0]
            specs.append(pl.BlockSpec((1,) + a.shape[1:], lambda i, n=a.ndim: (0,) * n))
        else:
            specs.append(FAR if n in far else whole(a))
        values.append(a)
    return pl.pallas_call(
        kernel,
        grid=(1,),
        in_specs=specs,
        out_specs=[whole(s) for s in shapes],
        out_shape=[jax.ShapeDtypeStruct(s.shape, s.dtype) for s in shapes],
        scratch_shapes=list(scratch),
        compiler_params=params(),
        cost_estimate=cost(us),
        name=name,
    )(*values)


def body(
    hidden_states,
    entry_rescale_coefficients,
    probe_projection_matrix,
    address_projection_matrix,
    content_projection_matrix,
    final_projection_matrix,
    archive_address_vectors,
    archive_content_vectors,
    reader_sharpness,
    reader_mixing_bias,
    retrieval_assignments,
    document_labels,
):
    rows, piece = hidden_states.shape
    width = probe_projection_matrix.shape[1]
    index = lax.axis_index("mem")
    me = lax.axis_index("tp")
    order = (me + jnp.array([0, -1, 1, 2], jnp.int32)) % 4
    like = jax.ShapeDtypeStruct

    x1 = along_tp(hidden_states, 1)
    x2 = along_tp(hidden_states, -1)
    x3 = along_tp(hidden_states, 2)
    k_own = key_unit(archive_address_vectors)
    (x3,) = ordered(k_own, x3)
    meta = make_meta(retrieval_assignments, index, k_own.shape[0] // MB)
    gain = entry_rescale_coefficients.reshape(4, 1, piece)

    (queries,) = call(
        3,
        query_kernel,
        "norm_query",
        (order,),
        (hidden_states, x1, x2, x3, gain, probe_projection_matrix.reshape(4, piece, width)),
        (like((rows, width), BF16),),
        far=(0, 1, 2, 3, 5),
        scratch=[
            pltpu.VMEM((4, rows, piece), BF16),
            pltpu.VMEM((4, piece, width), BF16),
            pltpu.SemaphoreType.DMA((4,)),
            pltpu.SemaphoreType.DMA((4,)),
        ],
    )

    a1 = first_axis(queries, 1)
    a2 = first_axis(queries, -1)
    a3 = first_axis(queries, 2)
    m1 = jnp.stack([queries, a1])
    m2 = jnp.stack([a2, a3])
    b1p = second_axis(m1, 1)
    b2m = second_axis(m2, -1)
    b1m = second_axis(m1, -1)
    b2p = second_axis(m2, 1)
    x1, x2, x3 = ordered(queries, x1, x2, x3)
    k_own, v_own = ordered(queries, k_own, archive_content_vectors)
    k_sib = other_core(k_own)
    v_sib = other_core(v_own)
    (kv,) = call(
        5,
        kv_kernel,
        "local_kv",
        (order,),
        (
            hidden_states,
            x1,
            x2,
            x3,
            gain,
            address_projection_matrix.reshape(4, piece, width),
            content_projection_matrix.reshape(4, piece, width),
        ),
        (like((2, rows, width), BF16),),
    )
    resident = (k_own, v_own, k_sib, v_sib)
    attend = lambda first, *parts: memory_attention(
        first, meta, reader_sharpness, parts, resident
    )
    m1, m2 = ordered(kv, m1, m2)
    z1, z2 = attend(0, m1, m2)
    b1p, b2m, kv = ordered(z1, b1p, b2m, kv)
    c1 = second_axis(b1p, 1)
    c2 = second_axis(b2m, -1)
    n1, n2, p1, p2 = attend(1, b1p, b2p, b1m, b2m)
    u2 = second_axis(p2, 1)
    v1 = second_axis(n1, -1)
    c1, c2 = ordered(p1, c1, c2)
    f1, f2 = attend(3, c1, c2)

    t1 = second_axis(f1, 1)
    t2 = second_axis(f2, -1)
    count = lax.axis_size("mem")
    before = lax.ppermute(kv, "mem", [(i, i + 1) for i in range(count - 1)])
    kv, queries = ordered(f1, kv, queries)
    (local_out,) = call(
        3,
        local_kernel,
        "local_attention",
        (index[None], reader_sharpness),
        (document_labels.reshape(-1, QB), queries, kv, before),
        (like((rows, width), F32),),
    )
    u1 = second_axis(add(p1, t1), 1)
    v2 = second_axis(add(n2, t2), -1)
    r2 = first_axis(add3(z2[0], u2[0], v2[0]), 1)
    r3 = first_axis(add3(z2[1], u2[1], v2[1]), 2)
    r1 = first_axis(add3(z1[1], u1[1], v1[1]), -1)

    chunk = like((rows // 4, 4 * piece), BF16)
    e0, d1, d2, d3 = call(
        5,
        output_kernel,
        "merge_output",
        (order, reader_mixing_bias),
        ((z1,), (u1,), (v1,), r1, r2, r3, local_out, final_projection_matrix),
        (chunk,) * 4,
        far=(7,),
        scratch=[
            pltpu.VMEM((rows, width), BF16),
            pltpu.VMEM(final_projection_matrix.shape, BF16),
            pltpu.SemaphoreType.DMA,
        ],
    )
    e1 = along_tp(d2, 1)
    e2 = along_tp(d1, -1)
    e3 = along_tp(d3, 2)
    total = e0.astype(F32) + e1.astype(F32) + e2.astype(F32) + e3.astype(F32)
    return total.astype(BF16)


def solution(mesh):
    placed = (
        P("mem", "tp"),
        P(),
        P(None, "tp"),
        P(None, "tp"),
        P(None, "tp"),
        P("tp", None),
        P("mem", "tp"),
        P("mem", "tp"),
        P("tp"),
        P("tp"),
        P(),
        P(),
    )
    return jax.shard_map(
        body, mesh=mesh, in_specs=placed, out_specs=P(("mem", "tp"), None), check_vma=False
    )
```

time: 156 us -> 133 us (0.85)
  Pallas kernels: 42.7 us -> 34.8 us
  waiting for transfers between devices: 41.1 us -> 34.6 us
  other arithmetic: 7.71 us -> 3.82 us
  local copies, waits for them, and re-layouts: 18 us -> 15.6 us
    ppermute x6, waiting for transfers between devices: 23.6 us -> 13.2 us  [along_tp(): return lax.ppermute(value, 'tp', [(i, (i + by) % 4) for i in range(4)])]
    pallas_call x9 -> x8, Pallas kernels: 42.7 us -> 34.8 us  [the longest x3 22.9 us: memory_attention(): pl.pallas_call(functools.partial(memory_kernel, first), in_specs=[SMEM, S...]
    ppermute x6, starting transfers between devices: 7.23 us -> 10.5 us  [along_tp(): return lax.ppermute(value, 'tp', [(i, (i + by) % 4) for i in range(4)])]
    ppermute x12, starting transfers between devices: 20.5 us -> 17.3 us  [second_axis(): return lax.ppermute(value, 'mem', pairs)]
    convert_element_type x2, other arithmetic: 3.42 us -> 0.29 us  [add(): return (a.astype(F32) + b.astype(F32)).astype(BF16)]
    ppermute x12, waiting for transfers between devices: 10.8 us -> 13.3 us  [second_axis(): return lax.ppermute(value, 'mem', pairs)]
    squeeze x2 -> x0, local copies, waits for them, and re-layouts: 1.61 us -> none  [the longest x1 0.86 us: body(): r3 = first_axis(w2[1], 2)]
    unnamed x57 -> x45, local copies, waits for them, and re-layouts: 14.7 us -> 13.9 us
  transfers between devices with their start and end apart: 27 -> 27, of which waited for: 11 -> 12; matrix products, arithmetic and copies ran while one was open for 7% -> 4% of each run, Pallas kernels for 22% -> 17%
where the time goes in v2:
time: 133 us
  starting transfers between devices  43.7 us (33%)
  Pallas kernels  34.8 us (26%)
  waiting for transfers between devices  34.6 us (26%)
  local copies, waits for them, and re-layouts  15.6 us (12%)
  other arithmetic  3.82 us (3%)
    pallas_call x3, Pallas kernels, memory_attention(): pl.pallas_call(functools.partial(memory_kernel, first), in_specs=[SMEM, S...  22.9 us
    ppermute x12, starting transfers between devices, second_axis(): return lax.ppermute(value, 'mem', pairs)  17.3 us
    ppermute x6, starting transfers between devices, first_axis(): return lax.ppermute(value, 'mem', pairs)  14.1 us
    unnamed x45, local copies, waits for them, and re-layouts  13.9 us
    ppermute x12, waiting for transfers between devices, second_axis(): return lax.ppermute(value, 'mem', pairs)  13.3 us
    ppermute x6, waiting for transfers between devices, along_tp(): return lax.ppermute(value, 'tp', [(i, (i + by) % 4) for i in range(4)])  13.2 us
    ppermute x6, starting transfers between devices, along_tp(): return lax.ppermute(value, 'tp', [(i, (i + by) % 4) for i in range(4)])  10.5 us
    pallas_call x4, Pallas kernels, call(): pl.pallas_call(kernel, grid=(1,), in_specs=specs, out_specs=[whole(s) for...  8.75 us
  transfers between devices with their start and end apart: 27, of which 12 were waited for; matrix products, arithmetic and copies ran while one was open for 4% of the time, Pallas kernels for 17%

profile of v2, /device:TPU:0, one launch (start us, length us, event | category | flops | bytes accessed | tf_op | source)
XLA Modules:
  0.0 132.9 jit_solution(18124979609063959339)
XLA Ops:
  0.0 3.1 %collective-permute-start.2 = (bf16[256,512]{1,0:T(8,128)(2,1)}, bf16[256,512]{1,0:T(8,128)(2,1)S(1)}, u32[]{:S(2)}, u32[]{:S(2)}) collective-permute-start(bf16[256,512]{1,0:T(8,128)(2,1)} %x0.3), channel_id=1, source_target_pairs={{0,2},{1,3},{2,0},{3,1},{4,6},{5,7},{6,4},{7,5},{8,10},{9,11},{10,... | collective-permute-start | bytes 786440 | tf_op jit(solution)/shard_map/ppermute | solution.py:293
  3.7 2.6 %collective-permute-start.1 = (bf16[256,512]{1,0:T(8,128)(2,1)}, bf16[256,512]{1,0:T(8,128)(2,1)S(1)}, u32[]{:S(2)}, u32[]{:S(2)}) collective-permute-start(bf16[256,512]{1,0:T(8,128)(2,1)} %x0.3), channel_id=1, source_target_pairs={{0,3},{1,0},{2,1},{3,2},{4,7},{5,4},{6,5},{7,6},{8,11},{9,8},{10,9... | collective-permute-start | bytes 786440 | tf_op jit(solution)/shard_map/ppermute | solution.py:293
  6.3 2.2 %copy-done.3 = bf16[4096,512]{1,0:T(8,128)(2,1)S(1)} copy-done((bf16[4096,512]{1,0:T(8,128)(2,1)S(1)}, bf16[4096,512]{1,0:T(8,128)(2,1)}, u32[]{:S(2)}) %copy-start.3) | copy-done | bytes 4194328
  8.5 3.1 %key_unit.1.refs_2_.refs_4_ = bf16[4096,512]{1,0:T(8,128)(2,1)S(1)} custom-call(bf16[4096,512]{1,0:T(8,128)(2,1)S(1)} %copy-done.3), custom_call_target="tpu_custom_call" | custom-call | flops 1 | bytes 22140000 | tf_op jit(solution)/shard_map/key_unit/pallas_call | solution.py:107
  11.7 2.0 %copy-done = bf16[4096,512]{1,0:T(8,128)(2,1)} copy-done((bf16[4096,512]{1,0:T(8,128)(2,1)}, bf16[4096,512]{1,0:T(8,128)(2,1)S(1)}, u32[]{:S(2)}) %copy-start) | copy-done | bytes 4194328
  13.7 1.5 %collective-permute-done.x1 = bf16[256,512]{1,0:T(8,128)(2,1)S(1)} collective-permute-done((bf16[256,512]{1,0:T(8,128)(2,1)}, bf16[256,512]{1,0:T(8,128)(2,1)S(1)}, u32[]{:S(2)}, u32[]{:S(2)}) %collective-permute-start) | collective-permute-done | bytes 262176 | tf_op jit(solution)/shard_map/ppermute | solution.py:293
  15.6 2.3 %norm_query.1.queries = bf16[256,512]{1,0:T(8,128)(2,1)S(1)} custom-call(s32[4]{0:T(128)S(1)} %get-tuple-element.66.order, bf16[256,512]{1,0:T(8,128)(2,1)S(1)} %copy-done.8, bf16[256,512]{1,0:T(8,128)(2,1)S(1)} %collective-permute-done.x1, bf16[256,512]{1,0:T(8,128)(2,1)S(1)} %collective-permute-done.1.x2, bf16[256,512]{1,0:T(8,128)(2,1)S(1)} %collective-permute-done.2.x3, ...), custom_call_target="tpu_custom_call" | custom-call | flops 1 | bytes 11070000 | tf_op jit(solution)/shard_map/norm_query/pallas_call | solution.py:347
  18.6 0.7 copy-done.12
  22.1 4.0 %collective-permute-start.5 = (bf16[256,512]{1,0:T(8,128)(2,1)S(1)}, bf16[256,512]{1,0:T(8,128)(2,1)S(1)}, u32[]{:S(2)}, u32[]{:S(2)}) collective-permute-start(bf16[256,512]{1,0:T(8,128)(2,1)S(1)} %norm_query.1.queries), channel_id=1, source_target_pairs={{0,64},{4,20},{8,72},{12,28},{16,80},{20,4},{24,88},{28,12},{32,96... | collective-permute-start | bytes 786440 | tf_op jit(solution)/shard_map/ppermute | solution.py:280
  26.1 0.7 collective-permute-start.4
  27.2 1.3 collective-permute-start.3
  28.7 1.8 %collective-permute-done.5 = bf16[256,512]{1,0:T(8,128)(2,1)S(1)} collective-permute-done((bf16[256,512]{1,0:T(8,128)(2,1)S(1)}, bf16[256,512]{1,0:T(8,128)(2,1)S(1)}, u32[]{:S(2)}, u32[]{:S(2)}) %collective-permute-start.5) | collective-permute-done | bytes 262176 | tf_op jit(solution)/shard_map/ppermute | solution.py:280
  30.4 3.9 %collective-permute-done.4 = bf16[256,512]{1,0:T(8,128)(2,1)S(1)} collective-permute-done((bf16[256,512]{1,0:T(8,128)(2,1)S(1)}, bf16[256,512]{1,0:T(8,128)(2,1)S(1)}, u32[]{:S(2)}, u32[]{:S(2)}) %collective-permute-start.4) | collective-permute-done | bytes 262176 | tf_op jit(solution)/shard_map/ppermute | solution.py:280
  34.3 3.1 %collective-permute-start.9 = (bf16[2,256,512]{2,1,0:T(8,128)(2,1)S(1)}, bf16[2,256,512]{2,1,0:T(8,128)(2,1)}, u32[]{:S(2)}, u32[]{:S(2)}) collective-permute-start(bf16[2,256,512]{2,1,0:T(8,128)(2,1)S(1)} %pad_maximum_fusion.1.refs_1_), channel_id=1, source_target_pairs={{0,24},{4,100},{8,0},{12,108},{16,8},{20,116},{24,16},{28,124},{32... | collective-permute-start | bytes 1572872 | tf_op jit(solution)/shard_map/ppermute | solution.py:285
  37.4 1.0 pad_maximum_fusion.refs_0_
  39.5 1.6 %copy-done.6 = bf16[2048,512]{1,0:T(8,128)(2,1)S(1)} copy-done((bf16[2048,512]{1,0:T(8,128)(2,1)S(1)}, bf16[2048,512]{1,0:T(8,128)(2,1)}, u32[]{:S(2)}) %copy-start.6) | copy-done | bytes 2097176
  41.1 0.9 copy-done.9
  42.0 0.9 copy-done.11
  43.0 0.9 copy-done.13
  43.9 0.9 copy-done.15
  44.9 2.0 %local_kv.1.kv = bf16[2,256,512]{2,1,0:T(8,128)(2,1)S(1)} custom-call(s32[4]{0:T(128)S(1)} %get-tuple-element.66.order, bf16[256,512]{1,0:T(8,128)(2,1)S(1)} %copy-done.9, bf16[256,512]{1,0:T(8,128)(2,1)S(1)} %copy-done.13, bf16[256,512]{1,0:T(8,128)(2,1)S(1)} %copy-done.15, bf16[256,512]{1,0:T(8,128)(2,1)S(1)} %copy-done.11, ...), custom_call_target="tpu_custom_call" | custom-call | flops 1 | bytes 18450000 | tf_op jit(solution)/shard_map/local_kv/pallas_call | solution.py:347
  47.6 2.7 %collective-permute-start.11 = (bf16[2,256,512]{2,1,0:T(8,128)(2,1)S(1)}, bf16[2,256,512]{2,1,0:T(8,128)(2,1)S(1)}, u32[]{:S(2)}, u32[]{:S(2)}) collective-permute-start(bf16[2,256,512]{2,1,0:T(8,128)(2,1)S(1)} %pad_maximum_fusion.refs_0_), channel_id=1, source_target_pairs={{0,24},{4,100},{8,0},{12,108},{16,8},{20,116},{24,16},{28,124},{32... | collective-permute-start | bytes 1572872 | tf_op jit(solution)/shard_map/ppermute | solution.py:285
  50.3 2.2 %copy-done.2 = bf16[4096,512]{1,0:T(8,128)(2,1)S(1)} copy-done((bf16[4096,512]{1,0:T(8,128)(2,1)S(1)}, bf16[4096,512]{1,0:T(8,128)(2,1)}, u32[]{:S(2)}) %copy-start.2) | copy-done | bytes 4194328
  52.5 6.5 %memory_attention.3 = (bf16[2,272,512]{2,1,0:T(8,128)(2,1)S(1)}, bf16[2,272,512]{2,1,0:T(8,128)(2,1)S(1)}) custom-call(s32[104]{0:T(128)S(1)} %reshape.325.meta, f32[4]{0:T(128)S(1)} %copy-done.17, bf16[2,256,512]{2,1,0:T(8,128)(2,1)S(1)} %pad_maximum_fusion.refs_0_, bf16[2,256,512]{2,1,0:T(8,128)(2,1)S(1)} %pad_maximum_fusion.1.refs_1_, ...), custom_call_target="tpu_custom_call" | custom-call | flops 1 | bytes 22140000 | tf_op jit(solution)/shard_map/memory_attention/pallas_call | solution.py:226
  59.2 3.2 %collective-permute-start.13 = (bf16[2,256,512]{2,1,0:T(8,128)(2,1)}, bf16[2,256,512]{2,1,0:T(8,128)(2,1)S(1)}, u32[]{:S(2)}, u32[]{:S(2)}) collective-permute-start(bf16[2,256,512]{2,1,0:T(8,128)(2,1)} %collective-permute-done.9.refs_3_), channel_id=1, source_target_pairs={{0,24},{4,100},{8,0},{12,108},{16,8},{20,116},{24,16},{28,124},{32... | collective-permute-start | bytes 1572872 | tf_op jit(solution)/shard_map/ppermute | solution.py:285
  62.4 9.2 %memory_attention.4 = (bf16[2,272,512]{2,1,0:T(8,128)(2,1)S(1)}, bf16[2,272,512]{2,1,0:T(8,128)(2,1)S(1)}, bf16[2,272,512]{2,1,0:T(8,128)(2,1)S(1)}, bf16[2,272,512]{2,1,0:T(8,128)(2,1)S(1)}) custom-call(s32[104]{0:T(128)S(1)} %reshape.325.meta, f32[4]{0:T(128)S(1)} %copy-done.17, bf16[2,256,512]{2,1,0:T(8,128)(2,1)} %collective-permute-done.8.refs_0_, ...), custom_call_target="tpu_custom_call" | custom-call | flops 1 | bytes 44280000 | tf_op jit(solution)/shard_map/memory_attention/pallas_call | solution.py:226
  71.6 7.2 %memory_attention.5 = (bf16[2,272,512]{2,1,0:T(8,128)(2,1)S(1)}, bf16[2,272,512]{2,1,0:T(8,128)(2,1)S(1)}) custom-call(s32[104]{0:T(128)S(1)} %reshape.325.meta, f32[4]{0:T(128)S(1)} %copy-done.17, bf16[2,256,512]{2,1,0:T(8,128)(2,1)S(1)} %collective-permute-done.12.refs_0_, bf16[2,256,512]{2,1,0:T(8,128)(2,1)S(1)} %collective-permute-done.13.refs_1_, ...), custom_call_target="tpu_custom_call" | custom-call | flops 1 | bytes 22140000 | tf_op jit(solution)/shard_map/memory_attention/pallas_call | solution.py:226
  78.9 2.0 %collective-permute-start.14 = (bf16[2,272,512]{2,1,0:T(8,128)(2,1)S(1)}, bf16[2,272,512]{2,1,0:T(8,128)(2,1)S(1)}, u32[]{:S(2)}, u32[]{:S(2)}) collective-permute-start(bf16[2,272,512]{2,1,0:T(8,128)(2,1)S(1)} %get-tuple-element.46), channel_id=1, source_target_pairs={{0,8},{4,36},{8,16},{12,44},{16,24},{20,52},{24,0},{28,60},{32,40}... | collective-permute-start | bytes 1671176 | tf_op jit(solution)/shard_map/ppermute | solution.py:285
  80.9 3.2 %collective-permute-start.16 = (bf16[2,272,512]{2,1,0:T(8,128)(2,1)S(1)}, bf16[2,272,512]{2,1,0:T(8,128)(2,1)S(1)}, u32[]{:S(2)}, u32[]{:S(2)}) collective-permute-start(bf16[2,272,512]{2,1,0:T(8,128)(2,1)S(1)} %get-tuple-element.47), channel_id=1, source_target_pairs={{0,24},{4,100},{8,0},{12,108},{16,8},{20,116},{24,16},{28,124},{32... | collective-permute-start | bytes 1671176 | tf_op jit(solution)/shard_map/ppermute | solution.py:285
  84.1 4.3 %collective-permute-done.19 = bf16[2,272,512]{2,1,0:T(8,128)(2,1)S(1)} collective-permute-done((bf16[2,272,512]{2,1,0:T(8,128)(2,1)S(1)}, bf16[2,272,512]{2,1,0:T(8,128)(2,1)S(1)}, u32[]{:S(2)}, u32[]{:S(2)}) %collective-permute-start.19) | collective-permute-done | bytes 557088 | tf_op jit(solution)/shard_map/ppermute | solution.py:285
  88.6 1.3 collective-permute-start.20
  90.0 0.8 collective-permute-start.15
  90.9 1.3 collective-permute-start.23
  92.2 3.5 %collective-permute-done.18 = bf16[2,272,512]{2,1,0:T(8,128)(2,1)S(1)} collective-permute-done((bf16[2,272,512]{2,1,0:T(8,128)(2,1)S(1)}, bf16[2,272,512]{2,1,0:T(8,128)(2,1)S(1)}, u32[]{:S(2)}, u32[]{:S(2)}) %collective-permute-start.18) | collective-permute-done | bytes 557088 | tf_op jit(solution)/shard_map/ppermute | solution.py:285
  95.7 4.8 %collective-permute-done.20 = bf16[2,272,512]{2,1,0:T(8,128)(2,1)S(1)} collective-permute-done((bf16[2,272,512]{2,1,0:T(8,128)(2,1)S(1)}, bf16[2,272,512]{2,1,0:T(8,128)(2,1)S(1)}, u32[]{:S(2)}, u32[]{:S(2)}) %collective-permute-start.20) | collective-permute-done | bytes 557088 | tf_op jit(solution)/shard_map/ppermute | solution.py:285
  100.8 5.5 %collective-permute-start.22 = (bf16[272,512]{1,0:T(8,128)(2,1)S(1)}, bf16[272,512]{1,0:T(8,128)(2,1)S(1)}, u32[]{:S(2)}, u32[]{:S(2)}) collective-permute-start(bf16[272,512]{1,0:T(8,128)(2,1)S(1)} %get-tuple-element.61), channel_id=1, source_target_pairs={{0,64},{4,20},{8,72},{12,28},{16,80},{20,4},{24,88},{28,12},{32,96... | collective-permute-start | bytes 835592 | tf_op jit(solution)/shard_map/ppermute | solution.py:280
  106.3 0.7 collective-permute-done.15.u
  107.1 2.5 %collective-permute-start.17 = (bf16[272,512]{1,0:T(8,128)(2,1)S(1)}, bf16[272,512]{1,0:T(8,128)(2,1)S(1)}, u32[]{:S(2)}, u32[]{:S(2)}) collective-permute-start(bf16[272,512]{1,0:T(8,128)(2,1)S(1)} %fusion), channel_id=1, source_target_pairs={{0,96},{4,28},{8,104},{12,4},{16,112},{20,12},{24,120},{28,20},{32... | collective-permute-start | bytes 835592 | tf_op jit(solution)/shard_map/ppermute | solution.py:280
  109.7 1.7 %local_attention.1.local = f32[256,512]{1,0:T(8,128)S(1)} custom-call(s32[1]{0:T(128)} %bitcast.1.index, f32[4]{0:T(128)S(1)} %copy-done.17, s32[64,128]{1,0:T(8,128)S(1)} %bitcast.29, bf16[256,512]{1,0:T(8,128)(2,1)S(1)} %norm_query.1.queries, bf16[2,256,512]{2,1,0:T(8,128)(2,1)S(1)} %local_kv.1.kv, bf16[2,256,512]{2,1,0:T(8,128)(2,1)S(1)} %collective-permute-done.23.before), custom_call_target="tpu_custom_call" | custom-call | flops 1 | bytes 11070000 | tf_op jit(solution)/shard_map/local_attention/pallas_call | solution.py:347
  111.4 2.4 %collective-permute-done.22.x3 = bf16[272,512]{1,0:T(8,128)(2,1)S(1)} collective-permute-done((bf16[272,512]{1,0:T(8,128)(2,1)S(1)}, bf16[272,512]{1,0:T(8,128)(2,1)S(1)}, u32[]{:S(2)}, u32[]{:S(2)}) %collective-permute-start.22) | collective-permute-done | bytes 278560 | tf_op jit(solution)/shard_map/ppermute | solution.py:280
  113.8 2.7 %merge_output.1 = (bf16[64,2048]{1,0:T(8,128)(2,1)S(1)}, bf16[64,2048]{1,0:T(8,128)(2,1)S(1)}, bf16[64,2048]{1,0:T(8,128)(2,1)S(1)}, bf16[64,2048]{1,0:T(8,128)(2,1)S(1)}) custom-call(s32[4]{0:T(128)S(1)} %get-tuple-element.66.order, f32[4]{0:T(128)S(1)} %copy-done.18, bf16[2,272,512]{2,1,0:T(8,128)(2,1)S(1)} %get-tuple-element.40.z, ...), custom_call_target="tpu_custom_call" | custom-call | flops 1 | bytes 18450000 | tf_op jit(solution)/shard_map/merge_output/pallas_call | solution.py:347
  116.6 1.5 %collective-permute-start.24 = (bf16[64,2048]{1,0:T(8,128)(2,1)S(1)}, bf16[64,2048]{1,0:T(8,128)(2,1)S(1)}, u32[]{:S(2)}, u32[]{:S(2)}) collective-permute-start(bf16[64,2048]{1,0:T(8,128)(2,1)S(1)} %get-tuple-element.56), channel_id=1, source_target_pairs={{0,1},{1,2},{2,3},{3,0},{4,5},{5,6},{6,7},{7,4},{8,9},{9,10},{10,1... | collective-permute-start | bytes 786440 | tf_op jit(solution)/shard_map/ppermute | solution.py:293
  118.1 1.8 %collective-permute-start.25 = (bf16[64,2048]{1,0:T(8,128)(2,1)S(1)}, bf16[64,2048]{1,0:T(8,128)(2,1)S(1)}, u32[]{:S(2)}, u32[]{:S(2)}) collective-permute-start(bf16[64,2048]{1,0:T(8,128)(2,1)S(1)} %get-tuple-element.57), channel_id=1, source_target_pairs={{0,3},{1,0},{2,1},{3,2},{4,7},{5,4},{6,5},{7,6},{8,11},{9,8},{10,9... | collective-permute-start | bytes 786440 | tf_op jit(solution)/shard_map/ppermute | solution.py:293
  119.9 0.9 collective-permute-start.26
  120.7 5.5 %collective-permute-done.24 = bf16[64,2048]{1,0:T(8,128)(2,1)S(1)} collective-permute-done((bf16[64,2048]{1,0:T(8,128)(2,1)S(1)}, bf16[64,2048]{1,0:T(8,128)(2,1)S(1)}, u32[]{:S(2)}, u32[]{:S(2)}) %collective-permute-start.24) | collective-permute-done | bytes 262176 | tf_op jit(solution)/shard_map/ppermute | solution.py:293
  126.2 4.3 %collective-permute-done.25 = bf16[64,2048]{1,0:T(8,128)(2,1)S(1)} collective-permute-done((bf16[64,2048]{1,0:T(8,128)(2,1)S(1)}, bf16[64,2048]{1,0:T(8,128)(2,1)S(1)}, u32[]{:S(2)}, u32[]{:S(2)}) %collective-permute-start.25) | collective-permute-done | bytes 262176 | tf_op jit(solution)/shard_map/ppermute | solution.py:293
  130.5 1.6 %collective-permute-done.26 = bf16[64,2048]{1,0:T(8,128)(2,1)S(1)} collective-permute-done((bf16[64,2048]{1,0:T(8,128)(2,1)S(1)}, bf16[64,2048]{1,0:T(8,128)(2,1)S(1)}, u32[]{:S(2)}, u32[]{:S(2)}) %collective-permute-start.26) | collective-permute-done | bytes 262176 | tf_op jit(solution)/shard_map/ppermute | solution.py:293
  132.1 0.8 add_convert_fusion.5
  (103 shorter events, 7.7 us)
Async XLA Ops:
  0.0 13.7 %copy-start.21 = (s32[4]{0:T(128)S(1)}, s32[4]{0:T(128)}, u32[]{:S(2)}) copy-start(s32[4]{0:T(128)} %constant.134.clone) | copy-start | bytes 52
  0.0 13.7 %collective-permute-start.2 = (bf16[256,512]{1,0:T(8,128)(2,1)}, bf16[256,512]{1,0:T(8,128)(2,1)S(1)}, u32[]{:S(2)}, u32[]{:S(2)}) collective-permute-start(bf16[256,512]{1,0:T(8,128)(2,1)} %x0.3), channel_id=1, source_target_pairs={{0,2},{1,3},{2,0},{3,1},{4,6},{5,7},{6,4},{7,5},{8,10},{9,11},{10,... | collective-permute-start | bytes 786440 | tf_op jit(solution)/shard_map/ppermute | solution.py:293
  3.1 12.1 %collective-permute-start = (bf16[256,512]{1,0:T(8,128)(2,1)}, bf16[256,512]{1,0:T(8,128)(2,1)S(1)}, u32[]{:S(2)}, u32[]{:S(2)}) collective-permute-start(bf16[256,512]{1,0:T(8,128)(2,1)} %x0.3), channel_id=1, source_target_pairs={{0,1},{1,2},{2,3},{3,0},{4,5},{5,6},{6,7},{7,4},{8,9},{9,10},{10,1... | collective-permute-start | bytes 786440 | tf_op jit(solution)/shard_map/ppermute | solution.py:293
  3.7 11.9 %collective-permute-start.1 = (bf16[256,512]{1,0:T(8,128)(2,1)}, bf16[256,512]{1,0:T(8,128)(2,1)S(1)}, u32[]{:S(2)}, u32[]{:S(2)}) collective-permute-start(bf16[256,512]{1,0:T(8,128)(2,1)} %x0.3), channel_id=1, source_target_pairs={{0,3},{1,0},{2,1},{3,2},{4,7},{5,4},{6,5},{7,6},{8,11},{9,8},{10,9... | collective-permute-start | bytes 786440 | tf_op jit(solution)/shard_map/ppermute | solution.py:293
  6.3 2.2 %copy-start.3 = (bf16[4096,512]{1,0:T(8,128)(2,1)S(1)}, bf16[4096,512]{1,0:T(8,128)(2,1)}, u32[]{:S(2)}) copy-start(bf16[4096,512]{1,0:T(8,128)(2,1)} %raw.1) | copy-start | bytes 12582916
  8.5 5.1 %copy-start.19 = (bf16[2048]{0:T(1024)(128)(2,1)S(1)}, bf16[2048]{0:T(1024)(128)(2,1)}, u32[]{:S(2)}) copy-start(bf16[2048]{0:T(1024)(128)(2,1)} %param.16) | copy-start | bytes 12292
  8.5 7.1 %copy-start.4 = (bf16[2048,512]{1,0:T(8,128)(2,1)S(1)}, bf16[2048,512]{1,0:T(8,128)(2,1)}, u32[]{:S(2)}) copy-start(bf16[2048,512]{1,0:T(8,128)(2,1)} %param.17) | copy-start | bytes 6291460
  8.5 7.1 %copy-start.8 = (bf16[256,512]{1,0:T(8,128)(2,1)S(1)}, bf16[256,512]{1,0:T(8,128)(2,1)}, u32[]{:S(2)}) copy-start(bf16[256,512]{1,0:T(8,128)(2,1)} %x0.3) | copy-start | bytes 786436
  11.7 2.0 %copy-start = (bf16[4096,512]{1,0:T(8,128)(2,1)}, bf16[4096,512]{1,0:T(8,128)(2,1)S(1)}, u32[]{:S(2)}) copy-start(bf16[4096,512]{1,0:T(8,128)(2,1)S(1)} %key_unit.1.refs_2_.refs_4_) | copy-start | bytes 12582916
  13.6 7.2 %copy-start.20 = (s32[64,8]{0,1:T(8,128)S(1)}, s32[64,8]{0,1:T(8,128)}, u32[]{:S(2)}) copy-start(s32[64,8]{0,1:T(8,128)} %param.25) | copy-start | bytes 6148
  18.6 0.7 copy-start.12
  19.3 0.7 copy-start.14
  20.0 19.5 %copy-start.5 = (bf16[2048,512]{1,0:T(8,128)(2,1)S(1)}, bf16[2048,512]{1,0:T(8,128)(2,1)}, u32[]{:S(2)}) copy-start(bf16[2048,512]{1,0:T(8,128)(2,1)} %param.18) | copy-start | bytes 6291460
  20.0 27.6 %collective-permute-start.6 = (bf16[4096,512]{1,0:T(8,128)(2,1)}, bf16[4096,512]{1,0:T(8,128)(2,1)}, u32[]{:S(2)}, u32[]{:S(2)}) collective-permute-start(bf16[4096,512]{1,0:T(8,128)(2,1)} %copy-done), channel_id=1, source_target_pairs={{0,4},{4,0},{8,12},{12,8},{16,20},{20,16},{24,28},{28,24},{32,36},... | collective-permute-start | bytes 12582920 | tf_op jit(solution)/shard_map/ppermute | solution.py:289
  20.0 30.3 %collective-permute-start.7 = (bf16[4096,512]{1,0:T(8,128)(2,1)}, bf16[4096,512]{1,0:T(8,128)(2,1)}, u32[]{:S(2)}, u32[]{:S(2)}) collective-permute-start(bf16[4096,512]{1,0:T(8,128)(2,1)} %refs_3_.1), channel_id=1, source_target_pairs={{0,4},{4,0},{8,12},{12,8},{16,20},{20,16},{24,28},{28,24},{32,36},... | collective-permute-start | bytes 12582920 | tf_op jit(solution)/shard_map/ppermute | solution.py:289
  22.1 8.3 %collective-permute-start.5 = (bf16[256,512]{1,0:T(8,128)(2,1)S(1)}, bf16[256,512]{1,0:T(8,128)(2,1)S(1)}, u32[]{:S(2)}, u32[]{:S(2)}) collective-permute-start(bf16[256,512]{1,0:T(8,128)(2,1)S(1)} %norm_query.1.queries), channel_id=1, source_target_pairs={{0,64},{4,20},{8,72},{12,28},{16,80},{20,4},{24,88},{28,12},{32,96... | collective-permute-start | bytes 786440 | tf_op jit(solution)/shard_map/ppermute | solution.py:280
  26.1 8.2 %collective-permute-start.4 = (bf16[256,512]{1,0:T(8,128)(2,1)S(1)}, bf16[256,512]{1,0:T(8,128)(2,1)S(1)}, u32[]{:S(2)}, u32[]{:S(2)}) collective-permute-start(bf16[256,512]{1,0:T(8,128)(2,1)S(1)} %norm_query.1.queries), channel_id=1, source_target_pairs={{0,96},{4,28},{8,104},{12,4},{16,112},{20,12},{24,120},{28,20},{32... | collective-permute-start | bytes 786440 | tf_op jit(solution)/shard_map/ppermute | solution.py:280
  27.2 10.3 %collective-permute-start.3 = (bf16[256,512]{1,0:T(8,128)(2,1)S(1)}, bf16[256,512]{1,0:T(8,128)(2,1)}, u32[]{:S(2)}, u32[]{:S(2)}) collective-permute-start(bf16[256,512]{1,0:T(8,128)(2,1)S(1)} %norm_query.1.queries), channel_id=1, source_target_pairs={{0,32},{4,12},{8,40},{12,20},{16,48},{20,28},{24,56},{28,4},{32,64... | collective-permute-start | bytes 786440 | tf_op jit(solution)/shard_map/ppermute | solution.py:280
  34.3 24.7 %collective-permute-start.9 = (bf16[2,256,512]{2,1,0:T(8,128)(2,1)S(1)}, bf16[2,256,512]{2,1,0:T(8,128)(2,1)}, u32[]{:S(2)}, u32[]{:S(2)}) collective-permute-start(bf16[2,256,512]{2,1,0:T(8,128)(2,1)S(1)} %pad_maximum_fusion.1.refs_1_), channel_id=1, source_target_pairs={{0,24},{4,100},{8,0},{12,108},{16,8},{20,116},{24,16},{28,124},{32... | collective-permute-start | bytes 1572872 | tf_op jit(solution)/shard_map/ppermute | solution.py:285
  38.4 20.6 %collective-permute-start.8 = (bf16[2,256,512]{2,1,0:T(8,128)(2,1)S(1)}, bf16[2,256,512]{2,1,0:T(8,128)(2,1)}, u32[]{:S(2)}, u32[]{:S(2)}) collective-permute-start(bf16[2,256,512]{2,1,0:T(8,128)(2,1)S(1)} %pad_maximum_fusion.refs_0_), channel_id=1, source_target_pairs={{0,8},{4,36},{8,16},{12,44},{16,24},{20,52},{24,0},{28,60},{32,40}... | collective-permute-start | bytes 1572872 | tf_op jit(solution)/shard_map/ppermute | solution.py:285
  39.4 1.6 %copy-start.6 = (bf16[2048,512]{1,0:T(8,128)(2,1)S(1)}, bf16[2048,512]{1,0:T(8,128)(2,1)}, u32[]{:S(2)}) copy-start(bf16[2048,512]{1,0:T(8,128)(2,1)} %param.19) | copy-start | bytes 6291460
  41.0 0.9 copy-start.9
  42.0 0.9 copy-start.11
  42.9 0.9 copy-start.13
  43.9 0.9 copy-start.15
  44.9 5.4 %copy-start.1 = (bf16[4096,512]{1,0:T(8,128)(2,1)S(1)}, bf16[4096,512]{1,0:T(8,128)(2,1)}, u32[]{:S(2)}) copy-start(bf16[4096,512]{1,0:T(8,128)(2,1)} %copy-done) | copy-start | bytes 12582916
  44.9 5.4 %copy-start.17 = (f32[4]{0:T(128)S(1)}, f32[4]{0:T(128)}, u32[]{:S(2)}) copy-start(f32[4]{0:T(128)} %sharp.7) | copy-start | bytes 52
  46.9 15.5 %collective-permute-start.10 = (bf16[2,256,512]{2,1,0:T(8,128)(2,1)S(1)}, bf16[2,256,512]{2,1,0:T(8,128)(2,1)S(1)}, u32[]{:S(2)}, u32[]{:S(2)}) collective-permute-start(bf16[2,256,512]{2,1,0:T(8,128)(2,1)S(1)} %pad_maximum_fusion.1.refs_1_), channel_id=1, source_target_pairs={{0,8},{4,36},{8,16},{12,44},{16,24},{20,52},{24,0},{28,60},{32,40}... | collective-permute-start | bytes 1572872 | tf_op jit(solution)/shard_map/ppermute | solution.py:285
  47.6 14.8 %collective-permute-start.11 = (bf16[2,256,512]{2,1,0:T(8,128)(2,1)S(1)}, bf16[2,256,512]{2,1,0:T(8,128)(2,1)S(1)}, u32[]{:S(2)}, u32[]{:S(2)}) collective-permute-start(bf16[2,256,512]{2,1,0:T(8,128)(2,1)S(1)} %pad_maximum_fusion.refs_0_), channel_id=1, source_target_pairs={{0,24},{4,100},{8,0},{12,108},{16,8},{20,116},{24,16},{28,124},{32... | collective-permute-start | bytes 1572872 | tf_op jit(solution)/shard_map/ppermute | solution.py:285
  50.3 2.2 %copy-start.2 = (bf16[4096,512]{1,0:T(8,128)(2,1)S(1)}, bf16[4096,512]{1,0:T(8,128)(2,1)}, u32[]{:S(2)}) copy-start(bf16[4096,512]{1,0:T(8,128)(2,1)} %refs_3_.1) | copy-start | bytes 12582916
  59.1 12.5 %collective-permute-start.12 = (bf16[2,256,512]{2,1,0:T(8,128)(2,1)}, bf16[2,256,512]{2,1,0:T(8,128)(2,1)S(1)}, u32[]{:S(2)}, u32[]{:S(2)}) collective-permute-start(bf16[2,256,512]{2,1,0:T(8,128)(2,1)} %collective-permute-done.8.refs_0_), channel_id=1, source_target_pairs={{0,8},{4,36},{8,16},{12,44},{16,24},{20,52},{24,0},{28,60},{32,40}... | collective-permute-start | bytes 1572872 | tf_op jit(solution)/shard_map/ppermute | solution.py:285
  59.2 12.4 %collective-permute-start.13 = (bf16[2,256,512]{2,1,0:T(8,128)(2,1)}, bf16[2,256,512]{2,1,0:T(8,128)(2,1)S(1)}, u32[]{:S(2)}, u32[]{:S(2)}) collective-permute-start(bf16[2,256,512]{2,1,0:T(8,128)(2,1)} %collective-permute-done.9.refs_3_), channel_id=1, source_target_pairs={{0,24},{4,100},{8,0},{12,108},{16,8},{20,116},{24,16},{28,124},{32... | collective-permute-start | bytes 1572872 | tf_op jit(solution)/shard_map/ppermute | solution.py:285
  78.8 9.6 %collective-permute-start.19 = (bf16[2,272,512]{2,1,0:T(8,128)(2,1)S(1)}, bf16[2,272,512]{2,1,0:T(8,128)(2,1)S(1)}, u32[]{:S(2)}, u32[]{:S(2)}) collective-permute-start(bf16[2,272,512]{2,1,0:T(8,128)(2,1)S(1)} %get-tuple-element.51), channel_id=1, source_target_pairs={{0,24},{4,100},{8,0},{12,108},{16,8},{20,116},{24,16},{28,124},{32... | collective-permute-start | bytes 1671176 | tf_op jit(solution)/shard_map/ppermute | solution.py:285
  78.9 11.0 %collective-permute-start.14 = (bf16[2,272,512]{2,1,0:T(8,128)(2,1)S(1)}, bf16[2,272,512]{2,1,0:T(8,128)(2,1)S(1)}, u32[]{:S(2)}, u32[]{:S(2)}) collective-permute-start(bf16[2,272,512]{2,1,0:T(8,128)(2,1)S(1)} %get-tuple-element.46), channel_id=1, source_target_pairs={{0,8},{4,36},{8,16},{12,44},{16,24},{20,52},{24,0},{28,60},{32,40}... | collective-permute-start | bytes 1671176 | tf_op jit(solution)/shard_map/ppermute | solution.py:285
  80.9 14.8 %collective-permute-start.18 = (bf16[2,272,512]{2,1,0:T(8,128)(2,1)S(1)}, bf16[2,272,512]{2,1,0:T(8,128)(2,1)S(1)}, u32[]{:S(2)}, u32[]{:S(2)}) collective-permute-start(bf16[2,272,512]{2,1,0:T(8,128)(2,1)S(1)} %get-tuple-element.49), channel_id=1, source_target_pairs={{0,8},{4,36},{8,16},{12,44},{16,24},{20,52},{24,0},{28,60},{32,40}... | collective-permute-start | bytes 1671176 | tf_op jit(solution)/shard_map/ppermute | solution.py:285
  80.9 25.4 %collective-permute-start.16 = (bf16[2,272,512]{2,1,0:T(8,128)(2,1)S(1)}, bf16[2,272,512]{2,1,0:T(8,128)(2,1)S(1)}, u32[]{:S(2)}, u32[]{:S(2)}) collective-permute-start(bf16[2,272,512]{2,1,0:T(8,128)(2,1)S(1)} %get-tuple-element.47), channel_id=1, source_target_pairs={{0,24},{4,100},{8,0},{12,108},{16,8},{20,116},{24,16},{28,124},{32... | collective-permute-start | bytes 1671176 | tf_op jit(solution)/shard_map/ppermute | solution.py:285
  88.5 21.1 %copy-start.16 = (s32[8192]{0:T(1024)S(1)}, s32[8192]{0:T(1024)}, u32[]{:S(2)}) copy-start(s32[8192]{0:T(1024)} %param.26) | copy-start | bytes 98308
  88.6 11.9 %collective-permute-start.20 = (bf16[2,272,512]{2,1,0:T(8,128)(2,1)S(1)}, bf16[2,272,512]{2,1,0:T(8,128)(2,1)S(1)}, u32[]{:S(2)}, u32[]{:S(2)}) collective-permute-start(bf16[2,272,512]{2,1,0:T(8,128)(2,1)S(1)} %add_convert_fusion), channel_id=1, source_target_pairs={{0,24},{4,100},{8,0},{12,108},{16,8},{20,116},{24,16},{28,124},{32... | collective-permute-start | bytes 1671176 | tf_op jit(solution)/shard_map/ppermute | solution.py:285
  90.0 17.0 %collective-permute-start.15 = (bf16[2,272,512]{2,1,0:T(8,128)(2,1)S(1)}, bf16[2,272,512]{2,1,0:T(8,128)(2,1)S(1)}, u32[]{:S(2)}, u32[]{:S(2)}) collective-permute-start(bf16[2,272,512]{2,1,0:T(8,128)(2,1)S(1)} %add_convert_fusion.1), channel_id=1, source_target_pairs={{0,8},{4,36},{8,16},{12,44},{16,24},{20,52},{24,0},{28,60},{32,40}... | collective-permute-start | bytes 1671176 | tf_op jit(solution)/shard_map/ppermute | solution.py:285
  90.9 18.8 %collective-permute-start.23 = (bf16[2,256,512]{2,1,0:T(8,128)(2,1)S(1)}, bf16[2,256,512]{2,1,0:T(8,128)(2,1)S(1)}, u32[]{:S(2)}, u32[]{:S(2)}) collective-permute-start(bf16[2,256,512]{2,1,0:T(8,128)(2,1)S(1)} %local_kv.1.kv), channel_id=1, source_target_pairs={{0,4},{4,8},{8,12},{12,16},{16,20},{20,24},{24,28},{28,32},{32,36}... | collective-permute-start | bytes 1572872 | tf_op jit(solution)/shard_map/ppermute | solution.py:452
  100.5 13.3 %copy-start.7 = (bf16[512,2048]{1,0:T(8,128)(2,1)S(1)}, bf16[512,2048]{1,0:T(8,128)(2,1)}, u32[]{:S(2)}) copy-start(bf16[512,2048]{1,0:T(8,128)(2,1)} %weight.1) | copy-start | bytes 6291460
  100.5 13.3 %copy-start.18 = (f32[4]{0:T(128)S(1)}, f32[4]{0:T(128)}, u32[]{:S(2)}) copy-start(f32[4]{0:T(128)} %bias.1) | copy-start | bytes 52
  100.7 10.6 %collective-permute-start.21 = (bf16[272,512]{1,0:T(8,128)(2,1)S(1)}, bf16[272,512]{1,0:T(8,128)(2,1)S(1)}, u32[]{:S(2)}, u32[]{:S(2)}) collective-permute-start(bf16[272,512]{1,0:T(8,128)(2,1)S(1)} %get-tuple-element.62), channel_id=1, source_target_pairs={{0,32},{4,12},{8,40},{12,20},{16,48},{20,28},{24,56},{28,4},{32,64... | collective-permute-start | bytes 835592 | tf_op jit(solution)/shard_map/ppermute | solution.py:280
  100.8 13.0 %collective-permute-start.22 = (bf16[272,512]{1,0:T(8,128)(2,1)S(1)}, bf16[272,512]{1,0:T(8,128)(2,1)S(1)}, u32[]{:S(2)}, u32[]{:S(2)}) collective-permute-start(bf16[272,512]{1,0:T(8,128)(2,1)S(1)} %get-tuple-element.61), channel_id=1, source_target_pairs={{0,64},{4,20},{8,72},{12,28},{16,80},{20,4},{24,88},{28,12},{32,96... | collective-permute-start | bytes 835592 | tf_op jit(solution)/shard_map/ppermute | solution.py:280
  107.1 6.6 %collective-permute-start.17 = (bf16[272,512]{1,0:T(8,128)(2,1)S(1)}, bf16[272,512]{1,0:T(8,128)(2,1)S(1)}, u32[]{:S(2)}, u32[]{:S(2)}) collective-permute-start(bf16[272,512]{1,0:T(8,128)(2,1)S(1)} %fusion), channel_id=1, source_target_pairs={{0,96},{4,28},{8,104},{12,4},{16,112},{20,12},{24,120},{28,20},{32... | collective-permute-start | bytes 835592 | tf_op jit(solution)/shard_map/ppermute | solution.py:280
  116.6 9.6 %collective-permute-start.24 = (bf16[64,2048]{1,0:T(8,128)(2,1)S(1)}, bf16[64,2048]{1,0:T(8,128)(2,1)S(1)}, u32[]{:S(2)}, u32[]{:S(2)}) collective-permute-start(bf16[64,2048]{1,0:T(8,128)(2,1)S(1)} %get-tuple-element.56), channel_id=1, source_target_pairs={{0,1},{1,2},{2,3},{3,0},{4,5},{5,6},{6,7},{7,4},{8,9},{9,10},{10,1... | collective-permute-start | bytes 786440 | tf_op jit(solution)/shard_map/ppermute | solution.py:293
  118.1 12.4 %collective-permute-start.25 = (bf16[64,2048]{1,0:T(8,128)(2,1)S(1)}, bf16[64,2048]{1,0:T(8,128)(2,1)S(1)}, u32[]{:S(2)}, u32[]{:S(2)}) collective-permute-start(bf16[64,2048]{1,0:T(8,128)(2,1)S(1)} %get-tuple-element.57), channel_id=1, source_target_pairs={{0,3},{1,0},{2,1},{3,2},{4,7},{5,4},{6,5},{7,6},{8,11},{9,8},{10,9... | collective-permute-start | bytes 786440 | tf_op jit(solution)/shard_map/ppermute | solution.py:293
  119.9 12.2 %collective-permute-start.26 = (bf16[64,2048]{1,0:T(8,128)(2,1)S(1)}, bf16[64,2048]{1,0:T(8,128)(2,1)S(1)}, u32[]{:S(2)}, u32[]{:S(2)}) collective-permute-start(bf16[64,2048]{1,0:T(8,128)(2,1)S(1)} %get-tuple-element.58), channel_id=1, source_target_pairs={{0,2},{1,3},{2,0},{3,1},{4,6},{5,7},{6,4},{7,5},{8,10},{9,11},{10,... | collective-permute-start | bytes 786440 | tf_op jit(solution)/shard_map/ppermute | solution.py:293
  (1 other events, 0.7 us)

commit v3 on v2

--- a/solution.py
+++ b/solution.py
@@ -19,12 +19,14 @@
 BF16 = jnp.bfloat16
 
 
-def params(mib=40):
+def params(mib=24):
     return pltpu.CompilerParams(vmem_limit_bytes=mib * 2**20)
 
 
 def cost(us):
-    return pl.CostEstimate(flops=1, bytes_accessed=int(us * 3.69e6), transcendentals=0)
+    return pl.CostEstimate(
+        flops=int(us * 1.15e9), bytes_accessed=int(us * 3.69e6), transcendentals=int(us * 1e6)
+    )
 
 
 def unit_into(ref, rows, value):
@@ -42,14 +44,6 @@
         (piece * scale * gain[order[p]].astype(F32)).astype(BF16)
         for p, piece in enumerate(pieces)
     ]
-
-
-def project(order, normed, weight):
-    result = None
-    for p, value in enumerate(normed):
-        term = jnp.dot(value, weight[order[p]], preferred_element_type=F32)
-        result = term if result is None else result + term
-    return result
 
 
 def query_kernel(order, x0, x1, x2, x3, gain, weight, queries, x, w, x_sem, w_sem):
@@ -72,10 +66,25 @@
     unit_into(queries, slice(None), result)
 
 
-def kv_kernel(order, x0, x1, x2, x3, gain, key_weight, value_weight, kv):
+def kv_kernel(order, x0, x1, x2, x3, gain, key_weight, value_weight, kv, w, sem):
+    fetches = [
+        pltpu.make_async_copy(weight.at[order[p]], w.at[side, p], sem.at[side, p])
+        for side, weight in enumerate((key_weight, value_weight))
+        for p in range(4)
+    ]
+    for fetch in fetches:
+        fetch.start()
     normed = norm_pieces(order, (x0, x1, x2, x3), gain)
-    unit_into(kv.at[0], slice(None), project(order, normed, key_weight))
-    kv[1] = project(order, normed, value_weight).astype(BF16)
+    for side in range(2):
+        result = None
+        for p, value in enumerate(normed):
+            fetches[4 * side + p].wait()
+            term = jnp.dot(value, w[side, p], preferred_element_type=F32)
+            result = term if result is None else result + term
+        if side == 0:
+            unit_into(kv.at[0], slice(None), result)
+        else:
+            kv[1] = result.astype(BF16)
 
 
 def key_unit_kernel(raw, keys, x, sem):
@@ -114,7 +123,7 @@
             pltpu.SemaphoreType.DMA((blocks,)),
         ],
         compiler_params=params(),
-        cost_estimate=cost(6),
+        cost_estimate=cost(30),
         name="key_unit",
     )(raw)
 
@@ -169,19 +178,16 @@
     tile_row = lax.broadcasted_iota(jnp.int32, (16, HD), 0)
     cols = [slice(h * HD, (h + 1) * HD) for h in range(heads)]
     o[...] = jnp.zeros_like(o)
-    for load in loads:
-        load.wait()
-
-    def group(g, _):
+
+    def source(i, _):
+        pltpu.make_async_copy(parts[0].at[0], q.at[i], in_sem.at[i]).wait()
         for j, (k, v) in enumerate(sources):
-            base = ((first + g) * 2 + j) * 13
-
-            def step(p, _, j=j, k=k, v=v, base=base):
-                i = meta[base + 1 + p * 3] + 4 * g
-                half = meta[base + 2 + p * 3]
-                b = meta[base + 3 + p * 3]
+            base = ((first * 4 + i) * 2 + j) * 3
+
+            def slot(j=j, k=k, v=v, base=base):
+                half = meta[base + 1]
                 rows = pl.ds(pl.multiple_of(half * QB, QB), QB)
-                span = pl.ds(pl.multiple_of(b * MB, MB), MB)
+                span = pl.ds(pl.multiple_of(meta[base + 2] * MB, MB), MB)
                 scores = [
                     lax.dot_general(q[i, rows, c], k[span, c], NT, preferred_element_type=F32)
                     for c in cols
@@ -206,14 +212,17 @@
                         den = den + o[i, 2 * QB :, c].astype(F32)
                     o[i, rows, c] = num.astype(BF16)
                     o[i, 2 * QB :, c] = den.astype(BF16)
-                return 0
-
-            lax.fori_loop(0, meta[base], step, 0)
+
+            pl.when(meta[base] > 0)(slot)
+        for t in range(n):
+            pl.when(i // 2 == t)(
+                lambda t=t: pltpu.make_async_copy(
+                    o.at[i], outs[t].at[i - 2 * t], out_sem.at[i]
+                ).start()
+            )
         return 0
 
-    lax.fori_loop(0, n // 2, group, 0)
-    for store in stores:
-        store.start()
+    lax.fori_loop(0, 2 * n, source, 0)
     for store in stores:
         store.wait()
 
@@ -235,17 +244,17 @@
             pltpu.SemaphoreType.DMA((2 * n,)),
         ],
         compiler_params=params(),
-        cost_estimate=cost(3 * n),
+        cost_estimate=cost(15 * n),
         name="memory_attention",
     )(meta, sharp, *parts, *resident)
 
 
 def output_kernel(
-    order, bias, z, u, v, x1, x2, x3, local, weight, c0, c1, c2, c3, mixed, w, w_sem
+    order, bias, z, u, v, s, x1, x2, x3, local, weight, c0, c1, c2, c3, mixed, w, w_sem
 ):
     fetch = pltpu.make_async_copy(weight, w, w_sem)
     fetch.start()
-    total = z[0].astype(F32) + u[0].astype(F32) + v[0].astype(F32)
+    total = z[0].astype(F32) + u[0].astype(F32) + v[0].astype(F32) + s[0].astype(F32)
     total = total + x1[...].astype(F32) + x2[...].astype(F32) + x3[...].astype(F32)
     dens = total[2 * QB :, :]
     for h in range(total.shape[1] // HD):
@@ -308,22 +317,11 @@
     block = jnp.sum(jnp.where(hit, (ids % blocks_here)[:, None, :], 0), axis=-1).reshape(4, 4, 2)
     place = jnp.arange(16, dtype=jnp.int32)[None, None, :] // 8
     half = jnp.sum(jnp.where(hit, place, 0), axis=-1).reshape(4, 4, 2)
-    slot = jnp.arange(4, dtype=jnp.int32)
-    earlier = slot[:, None] > slot[None, :]
-    rank = jnp.sum(jnp.where(earlier[None, :, :, None], here[:, None], 0), axis=2)
-    chosen = (here[..., None] > 0) & (rank[..., None] == slot)
-    fields = jnp.stack([jnp.broadcast_to(slot[None, :, None], here.shape), half, block], axis=-1)
-    table = jnp.sum(jnp.where(chosen[..., None], fields[:, :, :, None, :], 0), axis=1)
-    count = jnp.sum(here, axis=1)[..., None]
-    return jnp.concatenate([count, table.reshape(4, 2, 12)], axis=-1).reshape(-1)
-
-
-def add(a, b):
-    return (a.astype(F32) + b.astype(F32)).astype(BF16)
-
-
-def add3(a, b, c):
-    return (a.astype(F32) + b.astype(F32) + c.astype(F32)).astype(BF16)
+    return jnp.stack([here, half, block], axis=-1).reshape(-1)
+
+
+def sum_of(*values):
+    return sum(v.astype(F32) for v in values).astype(BF16)
 
 
 def ordered(first, *later):
@@ -352,7 +350,7 @@
         out_shape=[jax.ShapeDtypeStruct(s.shape, s.dtype) for s in shapes],
         scratch_shapes=list(scratch),
         compiler_params=params(),
-        cost_estimate=cost(us),
+        cost_estimate=cost(5 * us),
         name=name,
     )(*values)
 
@@ -382,9 +380,12 @@
     x2 = along_tp(hidden_states, -1)
     x3 = along_tp(hidden_states, 2)
     k_own = key_unit(archive_address_vectors)
-    (x3,) = ordered(k_own, x3)
+    k_own, v_own = ordered(x1, k_own, archive_content_vectors)
+    k_sib = other_core(k_own)
+    v_sib = other_core(v_own)
     meta = make_meta(retrieval_assignments, index, k_own.shape[0] // MB)
     gain = entry_rescale_coefficients.reshape(4, 1, piece)
+    x3, meta, gain = lax.optimization_barrier((ordered(k_own, x3)[0], meta, gain))
 
     (queries,) = call(
         3,
@@ -405,16 +406,7 @@
     a1 = first_axis(queries, 1)
     a2 = first_axis(queries, -1)
     a3 = first_axis(queries, 2)
-    m1 = jnp.stack([queries, a1])
-    m2 = jnp.stack([a2, a3])
-    b1p = second_axis(m1, 1)
-    b2m = second_axis(m2, -1)
-    b1m = second_axis(m1, -1)
-    b2p = second_axis(m2, 1)
     x1, x2, x3 = ordered(queries, x1, x2, x3)
-    k_own, v_own = ordered(queries, k_own, archive_content_vectors)
-    k_sib = other_core(k_own)
-    v_sib = other_core(v_own)
     (kv,) = call(
         5,
         kv_kernel,
@@ -430,27 +422,43 @@
             content_projection_matrix.reshape(4, piece, width),
         ),
         (like((2, rows, width), BF16),),
-    )
-    resident = (k_own, v_own, k_sib, v_sib)
+        far=(5, 6),
+        scratch=[
+            pltpu.VMEM((2, 4, piece, width), BF16),
+            pltpu.SemaphoreType.DMA((2, 4)),
+        ],
+    )
+    m1 = jnp.stack([queries, a1])
+    a2, a3 = ordered(kv, a2, a3)
+    m2 = jnp.stack([a2, a3])
+    b1p = second_axis(m1, 1)
+    b2m = second_axis(m2, -1)
+    b1m = second_axis(m1, -1)
+    b2p = second_axis(m2, 1)
+
+    resident = tuple(
+        pltpu.with_memory_space_constraint(a, pltpu.VMEM) for a in (k_own, v_own, k_sib, v_sib)
+    )
     attend = lambda first, *parts: memory_attention(
         first, meta, reader_sharpness, parts, resident
     )
-    m1, m2 = ordered(kv, m1, m2)
     z1, z2 = attend(0, m1, m2)
-    b1p, b2m, kv = ordered(z1, b1p, b2m, kv)
+    b1p, b2m, b1m, b2p, kv = ordered(z1, b1p, b2m, b1m, b2p, kv)
     c1 = second_axis(b1p, 1)
     c2 = second_axis(b2m, -1)
+    count = lax.axis_size("mem")
+    before = lax.ppermute(kv, "mem", [(i, i + 1) for i in range(count - 1)])
     n1, n2, p1, p2 = attend(1, b1p, b2p, b1m, b2m)
+    u1 = second_axis(p1, 1)
     u2 = second_axis(p2, 1)
     v1 = second_axis(n1, -1)
-    c1, c2 = ordered(p1, c1, c2)
+    v2 = second_axis(n2, -1)
+    c1, c2, before = ordered(p1, c1, c2, before)
     f1, f2 = attend(3, c1, c2)
 
-    t1 = second_axis(f1, 1)
-    t2 = second_axis(f2, -1)
-    count = lax.axis_size("mem")
-    before = lax.ppermute(kv, "mem", [(i, i + 1) for i in range(count - 1)])
-    kv, queries = ordered(f1, kv, queries)
+    s1 = second_axis(f1, 2)
+    s2 = second_axis(f2, 2)
+    kv, queries, before = ordered(f1, kv, queries, before)
     (local_out,) = call(
         3,
         local_kernel,
@@ -459,11 +467,11 @@
         (document_labels.reshape(-1, QB), queries, kv, before),
         (like((rows, width), F32),),
     )
-    u1 = second_axis(add(p1, t1), 1)
-    v2 = second_axis(add(n2, t2), -1)
-    r2 = first_axis(add3(z2[0], u2[0], v2[0]), 1)
-    r3 = first_axis(add3(z2[1], u2[1], v2[1]), 2)
-    r1 = first_axis(add3(z1[1], u1[1], v1[1]), -1)
+    u1, u2, v1, v2, local_out = lax.optimization_barrier((u1, u2, v1, v2, local_out))
+    whole = lambda a, i: sum_of(z1[i], u1[i], v1[i], s1[i]) if a == 0 else sum_of(z2[i], u2[i], v2[i], s2[i])
+    r3 = first_axis(whole(1, 1), 2)
+    r2 = first_axis(whole(1, 0), 1)
+    r1 = first_axis(whole(0, 1), -1)
 
     chunk = like((rows // 4, 4 * piece), BF16)
     e0, d1, d2, d3 = call(
@@ -471,9 +479,9 @@
         output_kernel,
         "merge_output",
         (order, reader_mixing_bias),
-        ((z1,), (u1,), (v1,), r1, r2, r3, local_out, final_projection_matrix),
+        ((z1,), (u1,), (v1,), (s1,), r1, r2, r3, local_out, final_projection_matrix),
         (chunk,) * 4,
-        far=(7,),
+        far=(8,),
         scratch=[
             pltpu.VMEM((rows, width), BF16),
             pltpu.VMEM(final_projection_matrix.shape, BF16),

time: 133 us -> 118 us (0.89)
  Pallas kernels: 34.8 us -> 22.7 us
  local copies, waits for them, and re-layouts: 15.6 us -> 5.79 us
  waiting for transfers between devices: 34.6 us -> 40.2 us
  starting transfers between devices: 43.7 us -> 46.2 us
    pallas_call x3, Pallas kernels: 22.9 us -> 9.62 us  [memory_attention(): pl.pallas_call(functools.partial(memory_kernel, first), in_specs=[SMEM, S...]
    unnamed x45 -> x29, local copies, waits for them, and re-layouts: 13.9 us -> 4.3 us
    ppermute x12, waiting for transfers between devices: 13.3 us -> 22.9 us  [second_axis(): return lax.ppermute(value, 'mem', pairs)]
    ppermute x6, waiting for transfers between devices: 13.2 us -> 8.01 us  [along_tp(): return lax.ppermute(value, 'tp', [(i, (i + by) % 4) for i in range(4)])]
    ppermute x12, starting transfers between devices: 17.3 us -> 21.4 us  [second_axis(): return lax.ppermute(value, 'mem', pairs)]
  transfers between devices with their start and end apart: 27 -> 27, of which waited for: 12 -> 10; matrix products, arithmetic and copies ran while one was open for 4% -> 3% of each run, Pallas kernels for 17% -> 17%
where the time goes in v3:
time: 118 us
  starting transfers between devices  46.2 us (39%)
  waiting for transfers between devices  40.2 us (34%)
  Pallas kernels  22.7 us (19%)
  local copies, waits for them, and re-layouts  5.79 us (5%)
  other arithmetic  2.72 us (2%)
    ppermute x12, waiting for transfers between devices, second_axis(): return lax.ppermute(value, 'mem', pairs)  22.9 us
    ppermute x12, starting transfers between devices, second_axis(): return lax.ppermute(value, 'mem', pairs)  21.4 us
    ppermute x6, starting transfers between devices, first_axis(): return lax.ppermute(value, 'mem', pairs)  13.1 us
    pallas_call x4, Pallas kernels, call(): pl.pallas_call(kernel, grid=(1,), in_specs=specs, out_specs=[whole(s) for...  9.91 us
    ppermute x6, starting transfers between devices, along_tp(): return lax.ppermute(value, 'tp', [(i, (i + by) % 4) for i in range(4)])  9.8 us
    pallas_call x3, Pallas kernels, memory_attention(): pl.pallas_call(functools.partial(memory_kernel, first), in_specs=[SMEM, S...  9.62 us
    ppermute x6, waiting for transfers between devices, first_axis(): return lax.ppermute(value, 'mem', pairs)  9.28 us
    ppermute x6, waiting for transfers between devices, along_tp(): return lax.ppermute(value, 'tp', [(i, (i + by) % 4) for i in range(4)])  8.01 us
  transfers between devices with their start and end apart: 27, of which 10 were waited for; matrix products, arithmetic and copies ran while one was open for 3% of the time, Pallas kernels for 17%

profile of v3, /device:TPU:0, one launch (start us, length us, event | category | flops | bytes accessed | tf_op | source)
XLA Modules:
  0.0 117.9 jit_solution(6739597958470950173)
XLA Ops:
  0.0 1.6 %collective-permute-start = (bf16[256,512]{1,0:T(8,128)(2,1)}, bf16[256,512]{1,0:T(8,128)(2,1)S(1)}, u32[]{:S(2)}, u32[]{:S(2)}) collective-permute-start(bf16[256,512]{1,0:T(8,128)(2,1)} %x0.3), channel_id=1, source_target_pairs={{0,1},{1,2},{2,3},{3,0},{4,5},{5,6},{6,7},{7,4},{8,9},{9,10},{10,1... | collective-permute-start | bytes 786440 | tf_op jit(solution)/shard_map/ppermute | solution.py:302
  1.6 2.7 %collective-permute-start.1 = (bf16[256,512]{1,0:T(8,128)(2,1)}, bf16[256,512]{1,0:T(8,128)(2,1)S(1)}, u32[]{:S(2)}, u32[]{:S(2)}) collective-permute-start(bf16[256,512]{1,0:T(8,128)(2,1)} %x0.3), channel_id=1, source_target_pairs={{0,2},{1,3},{2,0},{3,1},{4,6},{5,7},{6,4},{7,5},{8,10},{9,11},{10,... | collective-permute-start | bytes 786440 | tf_op jit(solution)/shard_map/ppermute | solution.py:302
  4.3 1.4 %collective-permute-start.2 = (bf16[256,512]{1,0:T(8,128)(2,1)}, bf16[256,512]{1,0:T(8,128)(2,1)S(1)}, u32[]{:S(2)}, u32[]{:S(2)}) collective-permute-start(bf16[256,512]{1,0:T(8,128)(2,1)} %x0.3), channel_id=1, source_target_pairs={{0,3},{1,0},{2,1},{3,2},{4,7},{5,4},{6,5},{7,6},{8,11},{9,8},{10,9... | collective-permute-start | bytes 786440 | tf_op jit(solution)/shard_map/ppermute | solution.py:302
  5.7 0.7 broadcast_add_fusion.1
  6.8 2.2 %copy-done = bf16[4096,512]{1,0:T(8,128)(2,1)S(1)} copy-done((bf16[4096,512]{1,0:T(8,128)(2,1)S(1)}, bf16[4096,512]{1,0:T(8,128)(2,1)}, u32[]{:S(2)}) %copy-start) | copy-done | bytes 4194328
  9.0 3.1 %key_unit.1.refs_2_.refs_4_ = bf16[4096,512]{1,0:T(8,128)(2,1)S(1)} custom-call(bf16[4096,512]{1,0:T(8,128)(2,1)S(1)} %copy-done), custom_call_target="tpu_custom_call" | custom-call | flops 34500001792 | bytes 110700000 | tf_op jit(solution)/shard_map/key_unit/pallas_call | solution.py:116
  12.2 2.0 %copy-done.2 = bf16[4096,512]{1,0:T(8,128)(2,1)} copy-done((bf16[4096,512]{1,0:T(8,128)(2,1)}, bf16[4096,512]{1,0:T(8,128)(2,1)S(1)}, u32[]{:S(2)}) %copy-start.2) | copy-done | bytes 4194328
  14.3 0.6 gather_fusion
  16.2 0.6 collective-permute-start.7
  16.8 2.3 %norm_query.1.queries = bf16[256,512]{1,0:T(8,128)(2,1)S(1)} custom-call(s32[4]{0:T(128)S(1)} %get-tuple-element.90.order, bf16[256,512]{1,0:T(8,128)(2,1)S(1)} %copy-done.8, bf16[256,512]{1,0:T(8,128)(2,1)S(1)} %collective-permute-done.x1, bf16[256,512]{1,0:T(8,128)(2,1)S(1)} %collective-permute-done.2.x2, bf16[256,512]{1,0:T(8,128)(2,1)S(1)} %collective-permute-done.1.x3, ...), custom_call_target="tpu_custom_call" | custom-call | flops 17250000896 | bytes 55350000 | tf_op jit(solution)/shard_map/norm_query/pallas_call | solution.py:345
  19.0 2.0 %collective-permute-start.3 = (bf16[256,512]{1,0:T(8,128)(2,1)S(1)}, bf16[256,512]{1,0:T(8,128)(2,1)S(1)}, u32[]{:S(2)}, u32[]{:S(2)}) collective-permute-start(bf16[256,512]{1,0:T(8,128)(2,1)S(1)} %norm_query.1.queries), channel_id=1, source_target_pairs={{0,32},{4,12},{8,40},{12,20},{16,48},{20,28},{24,56},{28,4},{32,64... | collective-permute-start | bytes 786440 | tf_op jit(solution)/shard_map/ppermute | solution.py:289
  21.0 2.2 %collective-permute-start.4 = (bf16[256,512]{1,0:T(8,128)(2,1)S(1)}, bf16[256,512]{1,0:T(8,128)(2,1)S(1)}, u32[]{:S(2)}, u32[]{:S(2)}) collective-permute-start(bf16[256,512]{1,0:T(8,128)(2,1)S(1)} %norm_query.1.queries), channel_id=1, source_target_pairs={{0,96},{4,28},{8,104},{12,4},{16,112},{20,12},{24,120},{28,20},{32... | collective-permute-start | bytes 786440 | tf_op jit(solution)/shard_map/ppermute | solution.py:289
  23.2 1.8 %collective-permute-start.5 = (bf16[256,512]{1,0:T(8,128)(2,1)S(1)}, bf16[256,512]{1,0:T(8,128)(2,1)S(1)}, u32[]{:S(2)}, u32[]{:S(2)}) collective-permute-start(bf16[256,512]{1,0:T(8,128)(2,1)S(1)} %norm_query.1.queries), channel_id=1, source_target_pairs={{0,64},{4,20},{8,72},{12,28},{16,80},{20,4},{24,88},{28,12},{32,96... | collective-permute-start | bytes 786440 | tf_op jit(solution)/shard_map/ppermute | solution.py:289
  25.0 3.2 %local_kv.1.kv = bf16[2,256,512]{2,1,0:T(8,128)(2,1)S(1)} custom-call(s32[4]{0:T(128)S(1)} %get-tuple-element.90.order, bf16[256,512]{1,0:T(8,128)(2,1)S(1)} %copy-done.8, bf16[256,512]{1,0:T(8,128)(2,1)S(1)} %collective-permute-done.x1, bf16[256,512]{1,0:T(8,128)(2,1)S(1)} %collective-permute-done.2.x2, bf16[256,512]{1,0:T(8,128)(2,1)S(1)} %collective-permute-done.1.x3, ...), custom_call_target="tpu_custom_call" | custom-call | flops 28750000128 | bytes 92250000 | tf_op jit(solution)/shard_map/local_kv/pallas_call | solution.py:345
  28.3 1.6 %collective-permute-start.8 = (bf16[2,256,512]{2,1,0:T(8,128)(2,1)S(1)}, bf16[2,256,512]{2,1,0:T(8,128)(2,1)S(1)}, u32[]{:S(2)}, u32[]{:S(2)}) collective-permute-start(bf16[2,256,512]{2,1,0:T(8,128)(2,1)S(1)} %pad_maximum_fusion.refs_0_), channel_id=1, source_target_pairs={{0,8},{4,36},{8,16},{12,44},{16,24},{20,52},{24,0},{28,60},{32,40}... | collective-permute-start | bytes 1572872 | tf_op jit(solution)/shard_map/ppermute | solution.py:294
  30.0 3.0 %collective-permute-start.10 = (bf16[2,256,512]{2,1,0:T(8,128)(2,1)S(1)}, bf16[2,256,512]{2,1,0:T(8,128)(2,1)S(1)}, u32[]{:S(2)}, u32[]{:S(2)}) collective-permute-start(bf16[2,256,512]{2,1,0:T(8,128)(2,1)S(1)} %pad_maximum_fusion.refs_0_), channel_id=1, source_target_pairs={{0,24},{4,100},{8,0},{12,108},{16,8},{20,116},{24,16},{28,124},{32... | collective-permute-start | bytes 1572872 | tf_op jit(solution)/shard_map/ppermute | solution.py:294
  33.0 2.6 %collective-permute-start.9 = (bf16[2,256,512]{2,1,0:T(8,128)(2,1)S(1)}, bf16[2,256,512]{2,1,0:T(8,128)(2,1)S(1)}, u32[]{:S(2)}, u32[]{:S(2)}) collective-permute-start(bf16[2,256,512]{2,1,0:T(8,128)(2,1)S(1)} %pad_maximum_fusion.1.refs_1_), channel_id=1, source_target_pairs={{0,24},{4,100},{8,0},{12,108},{16,8},{20,116},{24,16},{28,124},{32... | collective-permute-start | bytes 1572872 | tf_op jit(solution)/shard_map/ppermute | solution.py:294
  35.6 2.4 %memory_attention.3 = (bf16[2,272,512]{2,1,0:T(8,128)(2,1)S(1)}, bf16[2,272,512]{2,1,0:T(8,128)(2,1)S(1)}) custom-call(s32[96]{0:T(128)S(1)} %reshape.299.meta, f32[4]{0:T(128)S(1)} %copy-done.10, bf16[2,256,512]{2,1,0:T(8,128)(2,1)S(1)} %pad_maximum_fusion.refs_0_, bf16[2,256,512]{2,1,0:T(8,128)(2,1)S(1)} %pad_maximum_fusion.1.refs_1_, ...), custom_call_target="tpu_custom_call" | custom-call | flops 34500001792 | bytes 110700000 | tf_op jit(solution)/shard_map/memory_attention/pallas_call | solution.py:235
  38.1 0.7 collective-permute-done.8.refs_0_
  38.8 6.5 %collective-permute-done.9.refs_3_ = bf16[2,256,512]{2,1,0:T(8,128)(2,1)S(1)} collective-permute-done((bf16[2,256,512]{2,1,0:T(8,128)(2,1)S(1)}, bf16[2,256,512]{2,1,0:T(8,128)(2,1)S(1)}, u32[]{:S(2)}, u32[]{:S(2)}) %collective-permute-start.9) | collective-permute-done | bytes 524320 | tf_op jit(solution)/shard_map/ppermute | solution.py:294
  45.3 0.7 collective-permute-done.11.refs_1_
  46.0 0.3 collective-permute-start.16
  46.3 2.9 %collective-permute-start.17 = (bf16[2,256,512]{2,1,0:T(8,128)(2,1)S(1)}, bf16[2,256,512]{2,1,0:T(8,128)(2,1)S(1)}, u32[]{:S(2)}, u32[]{:S(2)}) collective-permute-start(bf16[2,256,512]{2,1,0:T(8,128)(2,1)S(1)} %collective-permute-done.9.refs_3_), channel_id=1, source_target_pairs={{0,24},{4,100},{8,0},{12,108},{16,8},{20,116},{24,16},{28,124},{32... | collective-permute-start | bytes 1572872 | tf_op jit(solution)/shard_map/ppermute | solution.py:294
  49.2 1.3 %collective-permute-start.18 = (bf16[2,256,512]{2,1,0:T(8,128)(2,1)S(1)}, bf16[2,256,512]{2,1,0:T(8,128)(2,1)S(1)}, u32[]{:S(2)}, u32[]{:S(2)}) collective-permute-start(bf16[2,256,512]{2,1,0:T(8,128)(2,1)S(1)} %local_kv.1.kv), channel_id=1, source_target_pairs={{0,4},{4,8},{8,12},{12,16},{16,20},{20,24},{24,28},{28,32},{32,36}... | collective-permute-start | bytes 1572872 | tf_op jit(solution)/shard_map/ppermute | solution.py:450
  50.6 5.2 %memory_attention.4 = (bf16[2,272,512]{2,1,0:T(8,128)(2,1)S(1)}, bf16[2,272,512]{2,1,0:T(8,128)(2,1)S(1)}, bf16[2,272,512]{2,1,0:T(8,128)(2,1)S(1)}, bf16[2,272,512]{2,1,0:T(8,128)(2,1)S(1)}) custom-call(s32[96]{0:T(128)S(1)} %reshape.299.meta, f32[4]{0:T(128)S(1)} %copy-done.10, bf16[2,256,512]{2,1,0:T(8,128)(2,1)S(1)} %collective-permute-done.8.refs_0_, ...), custom_call_target="tpu_custom_call" | custom-call | flops 69000003584 | bytes 221400000 | tf_op jit(solution)/shard_map/memory_attention/pallas_call | solution.py:235
  55.8 1.1 collective-permute-start.12
  56.9 0.3 collective-permute-start.13
  57.3 3.1 %collective-permute-start.14 = (bf16[2,272,512]{2,1,0:T(8,128)(2,1)S(1)}, bf16[2,272,512]{2,1,0:T(8,128)(2,1)S(1)}, u32[]{:S(2)}, u32[]{:S(2)}) collective-permute-start(bf16[2,272,512]{2,1,0:T(8,128)(2,1)S(1)} %get-tuple-element.62), channel_id=1, source_target_pairs={{0,24},{4,100},{8,0},{12,108},{16,8},{20,116},{24,16},{28,124},{32... | collective-permute-start | bytes 1671176 | tf_op jit(solution)/shard_map/ppermute | solution.py:294
  60.4 1.0 collective-permute-start.15
  61.4 2.0 %memory_attention.5 = (bf16[2,272,512]{2,1,0:T(8,128)(2,1)S(1)}, bf16[2,272,512]{2,1,0:T(8,128)(2,1)S(1)}) custom-call(s32[96]{0:T(128)S(1)} %reshape.299.meta, f32[4]{0:T(128)S(1)} %copy-done.10, bf16[2,256,512]{2,1,0:T(8,128)(2,1)S(1)} %collective-permute-done.16.refs_0_, bf16[2,256,512]{2,1,0:T(8,128)(2,1)S(1)} %collective-permute-done.17.refs_1_, ...), custom_call_target="tpu_custom_call" | custom-call | flops 34500001792 | bytes 110700000 | tf_op jit(solution)/shard_map/memory_attention/pallas_call | solution.py:235
  63.4 4.8 %collective-permute-start.19 = (bf16[2,272,512]{2,1,0:T(8,128)(2,1)S(1)}, bf16[2,272,512]{2,1,0:T(8,128)(2,1)S(1)}, u32[]{:S(2)}, u32[]{:S(2)}) collective-permute-start(bf16[2,272,512]{2,1,0:T(8,128)(2,1)S(1)} %get-tuple-element.67), channel_id=1, source_target_pairs={{0,16},{4,68},{8,24},{12,76},{16,0},{20,84},{24,8},{28,92},{32,48}... | collective-permute-start | bytes 1671176 | tf_op jit(solution)/shard_map/ppermute | solution.py:294
  68.2 0.5 collective-permute-start.21
  68.8 1.7 %local_attention.1.local = f32[256,512]{1,0:T(8,128)S(1)} custom-call(s32[1]{0:T(128)} %bitcast.1.index, f32[4]{0:T(128)S(1)} %copy-done.10, s32[64,128]{1,0:T(8,128)S(1)} %bitcast.28, bf16[256,512]{1,0:T(8,128)(2,1)S(1)} %norm_query.1.queries, bf16[2,256,512]{2,1,0:T(8,128)(2,1)S(1)} %local_kv.1.kv, bf16[2,256,512]{2,1,0:T(8,128)(2,1)S(1)} %collective-permute-done.18.before), custom_call_target="tpu_custom_call" | custom-call | flops 17250000896 | bytes 55350000 | tf_op jit(solution)/shard_map/local_attention/pallas_call | solution.py:345
  70.4 3.5 %collective-permute-done.13 = bf16[2,272,512]{2,1,0:T(8,128)(2,1)S(1)} collective-permute-done((bf16[2,272,512]{2,1,0:T(8,128)(2,1)S(1)}, bf16[2,272,512]{2,1,0:T(8,128)(2,1)S(1)}, u32[]{:S(2)}, u32[]{:S(2)}) %collective-permute-start.13) | collective-permute-done | bytes 557088 | tf_op jit(solution)/shard_map/ppermute | solution.py:294
  74.0 11.4 %collective-permute-done.15 = bf16[2,272,512]{2,1,0:T(8,128)(2,1)S(1)} collective-permute-done((bf16[2,272,512]{2,1,0:T(8,128)(2,1)S(1)}, bf16[2,272,512]{2,1,0:T(8,128)(2,1)S(1)}, u32[]{:S(2)}, u32[]{:S(2)}) %collective-permute-start.15) | collective-permute-done | bytes 557088 | tf_op jit(solution)/shard_map/ppermute | solution.py:294
  85.5 5.6 %collective-permute-start.20 = (bf16[272,512]{1,0:T(8,128)(2,1)S(1)}, bf16[272,512]{1,0:T(8,128)(2,1)S(1)}, u32[]{:S(2)}, u32[]{:S(2)}) collective-permute-start(bf16[272,512]{1,0:T(8,128)(2,1)S(1)} %fusion), channel_id=1, source_target_pairs={{0,96},{4,28},{8,104},{12,4},{16,112},{20,12},{24,120},{28,20},{32... | collective-permute-start | bytes 835592 | tf_op jit(solution)/shard_map/ppermute | solution.py:289
  91.1 0.3 fusion.2
  91.5 1.5 %collective-permute-start.23 = (bf16[272,512]{1,0:T(8,128)(2,1)S(1)}, bf16[272,512]{1,0:T(8,128)(2,1)S(1)}, u32[]{:S(2)}, u32[]{:S(2)}) collective-permute-start(bf16[272,512]{1,0:T(8,128)(2,1)S(1)} %get-tuple-element.85), channel_id=1, source_target_pairs={{0,64},{4,20},{8,72},{12,28},{16,80},{20,4},{24,88},{28,12},{32,96... | collective-permute-start | bytes 835592 | tf_op jit(solution)/shard_map/ppermute | solution.py:289
  93.0 2.2 %collective-permute-done.20.x1 = bf16[272,512]{1,0:T(8,128)(2,1)S(1)} collective-permute-done((bf16[272,512]{1,0:T(8,128)(2,1)S(1)}, bf16[272,512]{1,0:T(8,128)(2,1)S(1)}, u32[]{:S(2)}, u32[]{:S(2)}) %collective-permute-start.20) | collective-permute-done | bytes 278560 | tf_op jit(solution)/shard_map/ppermute | solution.py:289
  95.2 7.0 %collective-permute-done.22.x2 = bf16[272,512]{1,0:T(8,128)(2,1)S(1)} collective-permute-done((bf16[272,512]{1,0:T(8,128)(2,1)S(1)}, bf16[272,512]{1,0:T(8,128)(2,1)S(1)}, u32[]{:S(2)}, u32[]{:S(2)}) %collective-permute-start.22) | collective-permute-done | bytes 278560 | tf_op jit(solution)/shard_map/ppermute | solution.py:289
  102.2 2.8 %merge_output.1 = (bf16[64,2048]{1,0:T(8,128)(2,1)S(1)}, bf16[64,2048]{1,0:T(8,128)(2,1)S(1)}, bf16[64,2048]{1,0:T(8,128)(2,1)S(1)}, bf16[64,2048]{1,0:T(8,128)(2,1)S(1)}) custom-call(s32[4]{0:T(128)S(1)} %get-tuple-element.90.order, f32[4]{0:T(128)S(1)} %copy-done.11, bf16[2,272,512]{2,1,0:T(8,128)(2,1)S(1)} %get-tuple-element.55.z, ...), custom_call_target="tpu_custom_call" | custom-call | flops 28750000128 | bytes 92250000 | tf_op jit(solution)/shard_map/merge_output/pallas_call | solution.py:345
  105.0 2.0 %collective-permute-start.26 = (bf16[64,2048]{1,0:T(8,128)(2,1)S(1)}, bf16[64,2048]{1,0:T(8,128)(2,1)S(1)}, u32[]{:S(2)}, u32[]{:S(2)}) collective-permute-start(bf16[64,2048]{1,0:T(8,128)(2,1)S(1)} %get-tuple-element.82), channel_id=1, source_target_pairs={{0,2},{1,3},{2,0},{3,1},{4,6},{5,7},{6,4},{7,5},{8,10},{9,11},{10,... | collective-permute-start | bytes 786440 | tf_op jit(solution)/shard_map/ppermute | solution.py:302
  107.0 1.5 %collective-permute-start.25 = (bf16[64,2048]{1,0:T(8,128)(2,1)S(1)}, bf16[64,2048]{1,0:T(8,128)(2,1)S(1)}, u32[]{:S(2)}, u32[]{:S(2)}) collective-permute-start(bf16[64,2048]{1,0:T(8,128)(2,1)S(1)} %get-tuple-element.81), channel_id=1, source_target_pairs={{0,3},{1,0},{2,1},{3,2},{4,7},{5,4},{6,5},{7,6},{8,11},{9,8},{10,9... | collective-permute-start | bytes 786440 | tf_op jit(solution)/shard_map/ppermute | solution.py:302
  108.5 0.6 collective-permute-start.24
  109.1 5.3 %collective-permute-done.26 = bf16[64,2048]{1,0:T(8,128)(2,1)S(1)} collective-permute-done((bf16[64,2048]{1,0:T(8,128)(2,1)S(1)}, bf16[64,2048]{1,0:T(8,128)(2,1)S(1)}, u32[]{:S(2)}, u32[]{:S(2)}) %collective-permute-start.26) | collective-permute-done | bytes 262176 | tf_op jit(solution)/shard_map/ppermute | solution.py:302
  114.4 1.8 %collective-permute-done.25 = bf16[64,2048]{1,0:T(8,128)(2,1)S(1)} collective-permute-done((bf16[64,2048]{1,0:T(8,128)(2,1)S(1)}, bf16[64,2048]{1,0:T(8,128)(2,1)S(1)}, u32[]{:S(2)}, u32[]{:S(2)}) %collective-permute-start.25) | collective-permute-done | bytes 262176 | tf_op jit(solution)/shard_map/ppermute | solution.py:302
  116.1 0.9 collective-permute-done.24
  117.1 0.8 add_convert_fusion.3
  (73 shorter events, 2.3 us)
Async XLA Ops:
  0.0 16.0 %collective-permute-start = (bf16[256,512]{1,0:T(8,128)(2,1)}, bf16[256,512]{1,0:T(8,128)(2,1)S(1)}, u32[]{:S(2)}, u32[]{:S(2)}) collective-permute-start(bf16[256,512]{1,0:T(8,128)(2,1)} %x0.3), channel_id=1, source_target_pairs={{0,1},{1,2},{2,3},{3,0},{4,5},{5,6},{6,7},{7,4},{8,9},{9,10},{10,1... | collective-permute-start | bytes 786440 | tf_op jit(solution)/shard_map/ppermute | solution.py:302
  1.6 14.6 %collective-permute-start.1 = (bf16[256,512]{1,0:T(8,128)(2,1)}, bf16[256,512]{1,0:T(8,128)(2,1)S(1)}, u32[]{:S(2)}, u32[]{:S(2)}) collective-permute-start(bf16[256,512]{1,0:T(8,128)(2,1)} %x0.3), channel_id=1, source_target_pairs={{0,2},{1,3},{2,0},{3,1},{4,6},{5,7},{6,4},{7,5},{8,10},{9,11},{10,... | collective-permute-start | bytes 786440 | tf_op jit(solution)/shard_map/ppermute | solution.py:302
  4.3 12.4 %collective-permute-start.2 = (bf16[256,512]{1,0:T(8,128)(2,1)}, bf16[256,512]{1,0:T(8,128)(2,1)S(1)}, u32[]{:S(2)}, u32[]{:S(2)}) collective-permute-start(bf16[256,512]{1,0:T(8,128)(2,1)} %x0.3), channel_id=1, source_target_pairs={{0,3},{1,0},{2,1},{3,2},{4,7},{5,4},{6,5},{7,6},{8,11},{9,8},{10,9... | collective-permute-start | bytes 786440 | tf_op jit(solution)/shard_map/ppermute | solution.py:302
  6.8 2.2 %copy-start = (bf16[4096,512]{1,0:T(8,128)(2,1)S(1)}, bf16[4096,512]{1,0:T(8,128)(2,1)}, u32[]{:S(2)}) copy-start(bf16[4096,512]{1,0:T(8,128)(2,1)} %raw.1) | copy-start | bytes 12582916
  9.0 5.1 %copy-start.12 = (s32[64,8]{0,1:T(8,128)S(1)}, s32[64,8]{0,1:T(8,128)}, u32[]{:S(2)}) copy-start(s32[64,8]{0,1:T(8,128)} %param.25) | copy-start | bytes 6148
  9.0 7.0 %copy-start.13 = (bf16[2048]{0:T(1024)(128)(2,1)S(1)}, bf16[2048]{0:T(1024)(128)(2,1)}, u32[]{:S(2)}) copy-start(bf16[2048]{0:T(1024)(128)(2,1)} %param.16) | copy-start | bytes 12292
  9.0 7.7 %copy-start.4 = (bf16[2048,512]{1,0:T(8,128)(2,1)S(1)}, bf16[2048,512]{1,0:T(8,128)(2,1)}, u32[]{:S(2)}) copy-start(bf16[2048,512]{1,0:T(8,128)(2,1)} %param.17) | copy-start | bytes 6291460
  9.0 7.7 %copy-start.8 = (bf16[256,512]{1,0:T(8,128)(2,1)S(1)}, bf16[256,512]{1,0:T(8,128)(2,1)}, u32[]{:S(2)}) copy-start(bf16[256,512]{1,0:T(8,128)(2,1)} %x0.3) | copy-start | bytes 786436
  12.1 2.0 %copy-start.2 = (bf16[4096,512]{1,0:T(8,128)(2,1)}, bf16[4096,512]{1,0:T(8,128)(2,1)S(1)}, u32[]{:S(2)}) copy-start(bf16[4096,512]{1,0:T(8,128)(2,1)S(1)} %key_unit.1.refs_2_.refs_4_) | copy-start | bytes 12582916
  16.0 19.6 %collective-permute-start.6 = (bf16[4096,512]{1,0:T(8,128)(2,1)}, bf16[4096,512]{1,0:T(8,128)(2,1)S(1)}, u32[]{:S(2)}, u32[]{:S(2)}) collective-permute-start(bf16[4096,512]{1,0:T(8,128)(2,1)} %copy-done.2), channel_id=1, source_target_pairs={{0,4},{4,0},{8,12},{12,8},{16,20},{20,16},{24,28},{28,24},{32,36},... | collective-permute-start | bytes 12582920 | tf_op jit(solution)/shard_map/ppermute | solution.py:298
  16.2 19.5 %collective-permute-start.7 = (bf16[4096,512]{1,0:T(8,128)(2,1)}, bf16[4096,512]{1,0:T(8,128)(2,1)S(1)}, u32[]{:S(2)}, u32[]{:S(2)}) collective-permute-start(bf16[4096,512]{1,0:T(8,128)(2,1)} %refs_3_.1), channel_id=1, source_target_pairs={{0,4},{4,0},{8,12},{12,8},{16,20},{20,16},{24,28},{28,24},{32,36},... | collective-permute-start | bytes 12582920 | tf_op jit(solution)/shard_map/ppermute | solution.py:298
  16.7 8.3 %copy-start.5 = (bf16[2048,512]{1,0:T(8,128)(2,1)S(1)}, bf16[2048,512]{1,0:T(8,128)(2,1)}, u32[]{:S(2)}) copy-start(bf16[2048,512]{1,0:T(8,128)(2,1)} %param.18) | copy-start | bytes 6291460
  16.7 8.3 %copy-start.6 = (bf16[2048,512]{1,0:T(8,128)(2,1)S(1)}, bf16[2048,512]{1,0:T(8,128)(2,1)}, u32[]{:S(2)}) copy-start(bf16[2048,512]{1,0:T(8,128)(2,1)} %param.19) | copy-start | bytes 6291460
  19.0 9.2 %collective-permute-start.3 = (bf16[256,512]{1,0:T(8,128)(2,1)S(1)}, bf16[256,512]{1,0:T(8,128)(2,1)S(1)}, u32[]{:S(2)}, u32[]{:S(2)}) collective-permute-start(bf16[256,512]{1,0:T(8,128)(2,1)S(1)} %norm_query.1.queries), channel_id=1, source_target_pairs={{0,32},{4,12},{8,40},{12,20},{16,48},{20,28},{24,56},{28,4},{32,64... | collective-permute-start | bytes 786440 | tf_op jit(solution)/shard_map/ppermute | solution.py:289
  21.0 8.9 %collective-permute-start.4 = (bf16[256,512]{1,0:T(8,128)(2,1)S(1)}, bf16[256,512]{1,0:T(8,128)(2,1)S(1)}, u32[]{:S(2)}, u32[]{:S(2)}) collective-permute-start(bf16[256,512]{1,0:T(8,128)(2,1)S(1)} %norm_query.1.queries), channel_id=1, source_target_pairs={{0,96},{4,28},{8,104},{12,4},{16,112},{20,12},{24,120},{28,20},{32... | collective-permute-start | bytes 786440 | tf_op jit(solution)/shard_map/ppermute | solution.py:289
  23.2 9.7 %collective-permute-start.5 = (bf16[256,512]{1,0:T(8,128)(2,1)S(1)}, bf16[256,512]{1,0:T(8,128)(2,1)S(1)}, u32[]{:S(2)}, u32[]{:S(2)}) collective-permute-start(bf16[256,512]{1,0:T(8,128)(2,1)S(1)} %norm_query.1.queries), channel_id=1, source_target_pairs={{0,64},{4,20},{8,72},{12,28},{16,80},{20,4},{24,88},{28,12},{32,96... | collective-permute-start | bytes 786440 | tf_op jit(solution)/shard_map/ppermute | solution.py:289
  25.0 10.6 %copy-start.1 = (bf16[4096,512]{1,0:T(8,128)(2,1)S(1)}, bf16[4096,512]{1,0:T(8,128)(2,1)}, u32[]{:S(2)}) copy-start(bf16[4096,512]{1,0:T(8,128)(2,1)} %refs_3_.1) | copy-start | bytes 12582916
  25.0 10.6 %copy-start.3 = (bf16[4096,512]{1,0:T(8,128)(2,1)S(1)}, bf16[4096,512]{1,0:T(8,128)(2,1)}, u32[]{:S(2)}) copy-start(bf16[4096,512]{1,0:T(8,128)(2,1)} %copy-done.2) | copy-start | bytes 12582916
  25.0 10.6 %copy-start.10 = (f32[4]{0:T(128)S(1)}, f32[4]{0:T(128)}, u32[]{:S(2)}) copy-start(f32[4]{0:T(128)} %sharp.7) | copy-start | bytes 52
  28.3 10.5 %collective-permute-start.8 = (bf16[2,256,512]{2,1,0:T(8,128)(2,1)S(1)}, bf16[2,256,512]{2,1,0:T(8,128)(2,1)S(1)}, u32[]{:S(2)}, u32[]{:S(2)}) collective-permute-start(bf16[2,256,512]{2,1,0:T(8,128)(2,1)S(1)} %pad_maximum_fusion.refs_0_), channel_id=1, source_target_pairs={{0,8},{4,36},{8,16},{12,44},{16,24},{20,52},{24,0},{28,60},{32,40}... | collective-permute-start | bytes 1572872 | tf_op jit(solution)/shard_map/ppermute | solution.py:294
  30.0 15.3 %collective-permute-start.10 = (bf16[2,256,512]{2,1,0:T(8,128)(2,1)S(1)}, bf16[2,256,512]{2,1,0:T(8,128)(2,1)S(1)}, u32[]{:S(2)}, u32[]{:S(2)}) collective-permute-start(bf16[2,256,512]{2,1,0:T(8,128)(2,1)S(1)} %pad_maximum_fusion.refs_0_), channel_id=1, source_target_pairs={{0,24},{4,100},{8,0},{12,108},{16,8},{20,116},{24,16},{28,124},{32... | collective-permute-start | bytes 1572872 | tf_op jit(solution)/shard_map/ppermute | solution.py:294
  33.0 12.3 %collective-permute-start.9 = (bf16[2,256,512]{2,1,0:T(8,128)(2,1)S(1)}, bf16[2,256,512]{2,1,0:T(8,128)(2,1)S(1)}, u32[]{:S(2)}, u32[]{:S(2)}) collective-permute-start(bf16[2,256,512]{2,1,0:T(8,128)(2,1)S(1)} %pad_maximum_fusion.1.refs_1_), channel_id=1, source_target_pairs={{0,24},{4,100},{8,0},{12,108},{16,8},{20,116},{24,16},{28,124},{32... | collective-permute-start | bytes 1572872 | tf_op jit(solution)/shard_map/ppermute | solution.py:294
  35.6 10.4 %collective-permute-start.11 = (bf16[2,256,512]{2,1,0:T(8,128)(2,1)S(1)}, bf16[2,256,512]{2,1,0:T(8,128)(2,1)S(1)}, u32[]{:S(2)}, u32[]{:S(2)}) collective-permute-start(bf16[2,256,512]{2,1,0:T(8,128)(2,1)S(1)} %pad_maximum_fusion.1.refs_1_), channel_id=1, source_target_pairs={{0,8},{4,36},{8,16},{12,44},{16,24},{20,52},{24,0},{28,60},{32,40}... | collective-permute-start | bytes 1572872 | tf_op jit(solution)/shard_map/ppermute | solution.py:294
  46.0 11.2 %collective-permute-start.16 = (bf16[2,256,512]{2,1,0:T(8,128)(2,1)S(1)}, bf16[2,256,512]{2,1,0:T(8,128)(2,1)S(1)}, u32[]{:S(2)}, u32[]{:S(2)}) collective-permute-start(bf16[2,256,512]{2,1,0:T(8,128)(2,1)S(1)} %collective-permute-done.8.refs_0_), channel_id=1, source_target_pairs={{0,8},{4,36},{8,16},{12,44},{16,24},{20,52},{24,0},{28,60},{32,40}... | collective-permute-start | bytes 1572872 | tf_op jit(solution)/shard_map/ppermute | solution.py:294
  46.3 14.0 %collective-permute-start.17 = (bf16[2,256,512]{2,1,0:T(8,128)(2,1)S(1)}, bf16[2,256,512]{2,1,0:T(8,128)(2,1)S(1)}, u32[]{:S(2)}, u32[]{:S(2)}) collective-permute-start(bf16[2,256,512]{2,1,0:T(8,128)(2,1)S(1)} %collective-permute-done.9.refs_3_), channel_id=1, source_target_pairs={{0,24},{4,100},{8,0},{12,108},{16,8},{20,116},{24,16},{28,124},{32... | collective-permute-start | bytes 1572872 | tf_op jit(solution)/shard_map/ppermute | solution.py:294
  49.2 12.2 %collective-permute-start.18 = (bf16[2,256,512]{2,1,0:T(8,128)(2,1)S(1)}, bf16[2,256,512]{2,1,0:T(8,128)(2,1)S(1)}, u32[]{:S(2)}, u32[]{:S(2)}) collective-permute-start(bf16[2,256,512]{2,1,0:T(8,128)(2,1)S(1)} %local_kv.1.kv), channel_id=1, source_target_pairs={{0,4},{4,8},{8,12},{12,16},{16,20},{20,24},{24,28},{28,32},{32,36}... | collective-permute-start | bytes 1572872 | tf_op jit(solution)/shard_map/ppermute | solution.py:450
  55.8 12.4 %collective-permute-start.12 = (bf16[2,272,512]{2,1,0:T(8,128)(2,1)S(1)}, bf16[2,272,512]{2,1,0:T(8,128)(2,1)S(1)}, u32[]{:S(2)}, u32[]{:S(2)}) collective-permute-start(bf16[2,272,512]{2,1,0:T(8,128)(2,1)S(1)} %get-tuple-element.60), channel_id=1, source_target_pairs={{0,8},{4,36},{8,16},{12,44},{16,24},{20,52},{24,0},{28,60},{32,40}... | collective-permute-start | bytes 1671176 | tf_op jit(solution)/shard_map/ppermute | solution.py:294
  56.9 17.0 %collective-permute-start.13 = (bf16[2,272,512]{2,1,0:T(8,128)(2,1)S(1)}, bf16[2,272,512]{2,1,0:T(8,128)(2,1)S(1)}, u32[]{:S(2)}, u32[]{:S(2)}) collective-permute-start(bf16[2,272,512]{2,1,0:T(8,128)(2,1)S(1)} %get-tuple-element.61), channel_id=1, source_target_pairs={{0,8},{4,36},{8,16},{12,44},{16,24},{20,52},{24,0},{28,60},{32,40}... | collective-permute-start | bytes 1671176 | tf_op jit(solution)/shard_map/ppermute | solution.py:294
  57.3 16.7 %collective-permute-start.14 = (bf16[2,272,512]{2,1,0:T(8,128)(2,1)S(1)}, bf16[2,272,512]{2,1,0:T(8,128)(2,1)S(1)}, u32[]{:S(2)}, u32[]{:S(2)}) collective-permute-start(bf16[2,272,512]{2,1,0:T(8,128)(2,1)S(1)} %get-tuple-element.62), channel_id=1, source_target_pairs={{0,24},{4,100},{8,0},{12,108},{16,8},{20,116},{24,16},{28,124},{32... | collective-permute-start | bytes 1671176 | tf_op jit(solution)/shard_map/ppermute | solution.py:294
  60.4 8.4 %copy-start.9 = (s32[8192]{0:T(1024)S(1)}, s32[8192]{0:T(1024)}, u32[]{:S(2)}) copy-start(s32[8192]{0:T(1024)} %param.26) | copy-start | bytes 98308
  60.4 25.0 %collective-permute-start.15 = (bf16[2,272,512]{2,1,0:T(8,128)(2,1)S(1)}, bf16[2,272,512]{2,1,0:T(8,128)(2,1)S(1)}, u32[]{:S(2)}, u32[]{:S(2)}) collective-permute-start(bf16[2,272,512]{2,1,0:T(8,128)(2,1)S(1)} %get-tuple-element.63), channel_id=1, source_target_pairs={{0,24},{4,100},{8,0},{12,108},{16,8},{20,116},{24,16},{28,124},{32... | collective-permute-start | bytes 1671176 | tf_op jit(solution)/shard_map/ppermute | solution.py:294
  63.4 22.0 %collective-permute-start.19 = (bf16[2,272,512]{2,1,0:T(8,128)(2,1)S(1)}, bf16[2,272,512]{2,1,0:T(8,128)(2,1)S(1)}, u32[]{:S(2)}, u32[]{:S(2)}) collective-permute-start(bf16[2,272,512]{2,1,0:T(8,128)(2,1)S(1)} %get-tuple-element.67), channel_id=1, source_target_pairs={{0,16},{4,68},{8,24},{12,76},{16,0},{20,84},{24,8},{28,92},{32,48}... | collective-permute-start | bytes 1671176 | tf_op jit(solution)/shard_map/ppermute | solution.py:294
  68.2 22.9 %collective-permute-start.21 = (bf16[2,272,512]{2,1,0:T(8,128)(2,1)S(1)}, bf16[2,272,512]{2,1,0:T(8,128)(2,1)S(1)}, u32[]{:S(2)}, u32[]{:S(2)}) collective-permute-start(bf16[2,272,512]{2,1,0:T(8,128)(2,1)S(1)} %get-tuple-element.77), channel_id=1, source_target_pairs={{0,16},{4,68},{8,24},{12,76},{16,0},{20,84},{24,8},{28,92},{32,48}... | collective-permute-start | bytes 1671176 | tf_op jit(solution)/shard_map/ppermute | solution.py:294
  68.7 33.5 %copy-start.7 = (bf16[512,2048]{1,0:T(8,128)(2,1)S(1)}, bf16[512,2048]{1,0:T(8,128)(2,1)}, u32[]{:S(2)}) copy-start(bf16[512,2048]{1,0:T(8,128)(2,1)} %weight.1) | copy-start | bytes 6291460
  68.7 33.5 %copy-start.11 = (f32[4]{0:T(128)S(1)}, f32[4]{0:T(128)}, u32[]{:S(2)}) copy-start(f32[4]{0:T(128)} %bias.1) | copy-start | bytes 52
  85.5 9.6 %collective-permute-start.20 = (bf16[272,512]{1,0:T(8,128)(2,1)S(1)}, bf16[272,512]{1,0:T(8,128)(2,1)S(1)}, u32[]{:S(2)}, u32[]{:S(2)}) collective-permute-start(bf16[272,512]{1,0:T(8,128)(2,1)S(1)} %fusion), channel_id=1, source_target_pairs={{0,96},{4,28},{8,104},{12,4},{16,112},{20,12},{24,120},{28,20},{32... | collective-permute-start | bytes 835592 | tf_op jit(solution)/shard_map/ppermute | solution.py:289
  91.4 10.8 %collective-permute-start.22 = (bf16[272,512]{1,0:T(8,128)(2,1)S(1)}, bf16[272,512]{1,0:T(8,128)(2,1)S(1)}, u32[]{:S(2)}, u32[]{:S(2)}) collective-permute-start(bf16[272,512]{1,0:T(8,128)(2,1)S(1)} %get-tuple-element.86), channel_id=1, source_target_pairs={{0,32},{4,12},{8,40},{12,20},{16,48},{20,28},{24,56},{28,4},{32,64... | collective-permute-start | bytes 835592 | tf_op jit(solution)/shard_map/ppermute | solution.py:289
  91.5 10.7 %collective-permute-start.23 = (bf16[272,512]{1,0:T(8,128)(2,1)S(1)}, bf16[272,512]{1,0:T(8,128)(2,1)S(1)}, u32[]{:S(2)}, u32[]{:S(2)}) collective-permute-start(bf16[272,512]{1,0:T(8,128)(2,1)S(1)} %get-tuple-element.85), channel_id=1, source_target_pairs={{0,64},{4,20},{8,72},{12,28},{16,80},{20,4},{24,88},{28,12},{32,96... | collective-permute-start | bytes 835592 | tf_op jit(solution)/shard_map/ppermute | solution.py:289
  105.0 9.3 %collective-permute-start.26 = (bf16[64,2048]{1,0:T(8,128)(2,1)S(1)}, bf16[64,2048]{1,0:T(8,128)(2,1)S(1)}, u32[]{:S(2)}, u32[]{:S(2)}) collective-permute-start(bf16[64,2048]{1,0:T(8,128)(2,1)S(1)} %get-tuple-element.82), channel_id=1, source_target_pairs={{0,2},{1,3},{2,0},{3,1},{4,6},{5,7},{6,4},{7,5},{8,10},{9,11},{10,... | collective-permute-start | bytes 786440 | tf_op jit(solution)/shard_map/ppermute | solution.py:302
  107.0 9.1 %collective-permute-start.25 = (bf16[64,2048]{1,0:T(8,128)(2,1)S(1)}, bf16[64,2048]{1,0:T(8,128)(2,1)S(1)}, u32[]{:S(2)}, u32[]{:S(2)}) collective-permute-start(bf16[64,2048]{1,0:T(8,128)(2,1)S(1)} %get-tuple-element.81), channel_id=1, source_target_pairs={{0,3},{1,0},{2,1},{3,2},{4,7},{5,4},{6,5},{7,6},{8,11},{9,8},{10,9... | collective-permute-start | bytes 786440 | tf_op jit(solution)/shard_map/ppermute | solution.py:302
  108.5 8.5 %collective-permute-start.24 = (bf16[64,2048]{1,0:T(8,128)(2,1)S(1)}, bf16[64,2048]{1,0:T(8,128)(2,1)S(1)}, u32[]{:S(2)}, u32[]{:S(2)}) collective-permute-start(bf16[64,2048]{1,0:T(8,128)(2,1)S(1)} %get-tuple-element.80), channel_id=1, source_target_pairs={{0,1},{1,2},{2,3},{3,0},{4,5},{5,6},{6,7},{7,4},{8,9},{9,10},{10,1... | collective-permute-start | bytes 786440 | tf_op jit(solution)/shard_map/ppermute | solution.py:302

commit v4 on v3

--- a/solution.py
+++ b/solution.py
@@ -160,15 +160,15 @@
 
 
 def memory_kernel(first, meta, sharp, *refs):
-    n = (len(refs) - 8) // 2
+    n = (len(refs) - 8) * 2 // 3
     parts, sources = refs[:n], (refs[n : n + 2], refs[n + 2 : n + 4])
-    outs, (q, o, in_sem, out_sem) = refs[n + 4 : 2 * n + 4], refs[2 * n + 4 :]
+    outs, (q, o, in_sem, out_sem) = refs[n + 4 : -4], refs[-4:]
     heads = q.shape[2] // HD
     loads = [
         pltpu.make_async_copy(parts[i // 2].at[i % 2], q.at[i], in_sem.at[i]) for i in range(2 * n)
     ]
     stores = [
-        pltpu.make_async_copy(o.at[i], outs[i // 2].at[i % 2], out_sem.at[i]) for i in range(2 * n)
+        pltpu.make_async_copy(o.at[i], outs[i // 4].at[i % 4], out_sem.at[i]) for i in range(2 * n)
     ]
     for load in loads:
         load.start()
@@ -214,10 +214,10 @@
                     o[i, 2 * QB :, c] = den.astype(BF16)
 
             pl.when(meta[base] > 0)(slot)
-        for t in range(n):
-            pl.when(i // 2 == t)(
+        for t in range(n // 2):
+            pl.when(i // 4 == t)(
                 lambda t=t: pltpu.make_async_copy(
-                    o.at[i], outs[t].at[i - 2 * t], out_sem.at[i]
+                    o.at[i], outs[t].at[i - 4 * t], out_sem.at[i]
                 ).start()
             )
         return 0
@@ -230,13 +230,13 @@
 def memory_attention(first, meta, sharp, parts, resident):
     width = parts[0].shape[2]
     n = len(parts)
-    shape = jax.ShapeDtypeStruct((2, 2 * QB + 16, width), BF16)
+    shape = jax.ShapeDtypeStruct((4, 2 * QB + 16, width), BF16)
     far = pl.BlockSpec(memory_space=pl.ANY)
     return pl.pallas_call(
         functools.partial(memory_kernel, first),
         in_specs=[SMEM, SMEM] + [far] * n + [VMEM] * 4,
-        out_specs=[far] * n,
-        out_shape=[shape] * n,
+        out_specs=[far] * (n // 2),
+        out_shape=[shape] * (n // 2),
         scratch_shapes=[
             pltpu.VMEM((2 * n, 2 * QB, width), BF16),
             pltpu.VMEM((2 * n, 2 * QB + 16, width), BF16),
@@ -442,23 +442,20 @@
     attend = lambda first, *parts: memory_attention(
         first, meta, reader_sharpness, parts, resident
     )
-    z1, z2 = attend(0, m1, m2)
-    b1p, b2m, b1m, b2p, kv = ordered(z1, b1p, b2m, b1m, b2p, kv)
+    (z,) = attend(0, m1, m2)
+    b1p, b2m, b1m, b2p, kv = ordered(z, b1p, b2m, b1m, b2p, kv)
     c1 = second_axis(b1p, 1)
     c2 = second_axis(b2m, -1)
     count = lax.axis_size("mem")
     before = lax.ppermute(kv, "mem", [(i, i + 1) for i in range(count - 1)])
-    n1, n2, p1, p2 = attend(1, b1p, b2p, b1m, b2m)
-    u1 = second_axis(p1, 1)
-    u2 = second_axis(p2, 1)
-    v1 = second_axis(n1, -1)
-    v2 = second_axis(n2, -1)
-    c1, c2, before = ordered(p1, c1, c2, before)
-    f1, f2 = attend(3, c1, c2)
-
-    s1 = second_axis(f1, 2)
-    s2 = second_axis(f2, 2)
-    kv, queries, before = ordered(f1, kv, queries, before)
+    n, p = attend(1, b1p, b2p, b1m, b2m)
+    u = second_axis(p, 1)
+    v = second_axis(n, -1)
+    c1, c2, before = ordered(p, c1, c2, before)
+    (f,) = attend(3, c1, c2)
+
+    s = second_axis(f, 2)
+    kv, queries, before = ordered(f, kv, queries, before)
     (local_out,) = call(
         3,
         local_kernel,
@@ -467,11 +464,10 @@
         (document_labels.reshape(-1, QB), queries, kv, before),
         (like((rows, width), F32),),
     )
-    u1, u2, v1, v2, local_out = lax.optimization_barrier((u1, u2, v1, v2, local_out))
-    whole = lambda a, i: sum_of(z1[i], u1[i], v1[i], s1[i]) if a == 0 else sum_of(z2[i], u2[i], v2[i], s2[i])
-    r3 = first_axis(whole(1, 1), 2)
-    r2 = first_axis(whole(1, 0), 1)
-    r1 = first_axis(whole(0, 1), -1)
+    u, v, local_out = lax.optimization_barrier((u, v, local_out))
+    r3 = first_axis(sum_of(z[3], u[3], v[3], s[3]), 2)
+    r2 = first_axis(sum_of(z[2], u[2], v[2], s[2]), 1)
+    r1 = first_axis(sum_of(z[1], u[1], v[1], s[1]), -1)
 
     chunk = like((rows // 4, 4 * piece), BF16)
     e0, d1, d2, d3 = call(
@@ -479,7 +475,7 @@
         output_kernel,
         "merge_output",
         (order, reader_mixing_bias),
-        ((z1,), (u1,), (v1,), (s1,), r1, r2, r3, local_out, final_projection_matrix),
+        ((z,), (u,), (v,), (s,), r1, r2, r3, local_out, final_projection_matrix),
         (chunk,) * 4,
         far=(8,),
         scratch=[

time: 118 us -> 121 us (1.025); the launches traced: 118 us -> 120 us
  waiting for transfers between devices: 40.2 us -> 48.3 us
  starting transfers between devices: 46.2 us -> 39.3 us
    ppermute x6, starting transfers between devices: 13.1 us -> 9.39 us  [first_axis(): return lax.ppermute(value, 'mem', pairs)]
    ppermute x6, waiting for transfers between devices: 9.28 us -> 12.7 us  [first_axis(): return lax.ppermute(value, 'mem', pairs)]
    ppermute x12 -> x9, waiting for transfers between devices: 22.9 us -> 26.1 us  [second_axis(): return lax.ppermute(value, 'mem', pairs)]
    ppermute x12 -> x9, starting transfers between devices: 21.4 us -> 18.7 us  [second_axis(): return lax.ppermute(value, 'mem', pairs)]
    ppermute x6, waiting for transfers between devices: 8.01 us -> 9.52 us  [along_tp(): return lax.ppermute(value, 'tp', [(i, (i + by) % 4) for i in range(4)])]
    unnamed x29 -> x27, local copies, waits for them, and re-layouts: 4.3 us -> 4.97 us
  transfers between devices with their start and end apart: 27 -> 24, of which waited for: 10 -> 11; matrix products, arithmetic and copies ran while one was open for 3% -> 3% of each run, Pallas kernels for 17% -> 17%
where the time goes in v4:
time: 121 us; the launch traced here: 120 us
  waiting for transfers between devices  48.3 us (40%)
  starting transfers between devices  39.3 us (32%)
  Pallas kernels  22.6 us (19%)
  local copies, waits for them, and re-layouts  6.46 us (5%)
  other arithmetic  2.76 us (2%)
    ppermute x9, waiting for transfers between devices, second_axis(): return lax.ppermute(value, 'mem', pairs)  26.1 us
    ppermute x9, starting transfers between devices, second_axis(): return lax.ppermute(value, 'mem', pairs)  18.7 us
    ppermute x6, waiting for transfers between devices, first_axis(): return lax.ppermute(value, 'mem', pairs)  12.7 us
    pallas_call x4, Pallas kernels, call(): pl.pallas_call(kernel, grid=(1,), in_specs=specs, out_specs=[whole(s) for...  9.94 us
    ppermute x6, waiting for transfers between devices, along_tp(): return lax.ppermute(value, 'tp', [(i, (i + by) % 4) for i in range(4)])  9.52 us
    pallas_call x3, Pallas kernels, memory_attention(): pl.pallas_call(functools.partial(memory_kernel, first), in_specs=[SMEM, S...  9.5 us
    ppermute x6, starting transfers between devices, first_axis(): return lax.ppermute(value, 'mem', pairs)  9.39 us
    ppermute x6, starting transfers between devices, along_tp(): return lax.ppermute(value, 'tp', [(i, (i + by) % 4) for i in range(4)])  9.23 us
  transfers between devices with their start and end apart: 24, of which 11 were waited for; matrix products, arithmetic and copies ran while one was open for 3% of the time, Pallas kernels for 17%

profile of v4, /device:TPU:0, one launch (start us, length us, event | category | flops | bytes accessed | tf_op | source)
XLA Modules:
  0.0 119.7 jit_solution(18193019289570409979)
XLA Ops:
  0.0 1.6 %collective-permute-start = (bf16[256,512]{1,0:T(8,128)(2,1)}, bf16[256,512]{1,0:T(8,128)(2,1)S(1)}, u32[]{:S(2)}, u32[]{:S(2)}) collective-permute-start(bf16[256,512]{1,0:T(8,128)(2,1)} %x0.3), channel_id=1, source_target_pairs={{0,1},{1,2},{2,3},{3,0},{4,5},{5,6},{6,7},{7,4},{8,9},{9,10},{10,1... | collective-permute-start | bytes 786440 | tf_op jit(solution)/shard_map/ppermute | solution.py:302
  1.6 2.7 %collective-permute-start.1 = (bf16[256,512]{1,0:T(8,128)(2,1)}, bf16[256,512]{1,0:T(8,128)(2,1)S(1)}, u32[]{:S(2)}, u32[]{:S(2)}) collective-permute-start(bf16[256,512]{1,0:T(8,128)(2,1)} %x0.3), channel_id=1, source_target_pairs={{0,2},{1,3},{2,0},{3,1},{4,6},{5,7},{6,4},{7,5},{8,10},{9,11},{10,... | collective-permute-start | bytes 786440 | tf_op jit(solution)/shard_map/ppermute | solution.py:302
  4.3 1.4 %collective-permute-start.2 = (bf16[256,512]{1,0:T(8,128)(2,1)}, bf16[256,512]{1,0:T(8,128)(2,1)S(1)}, u32[]{:S(2)}, u32[]{:S(2)}) collective-permute-start(bf16[256,512]{1,0:T(8,128)(2,1)} %x0.3), channel_id=1, source_target_pairs={{0,3},{1,0},{2,1},{3,2},{4,7},{5,4},{6,5},{7,6},{8,11},{9,8},{10,9... | collective-permute-start | bytes 786440 | tf_op jit(solution)/shard_map/ppermute | solution.py:302
  5.7 0.7 broadcast_add_fusion.1
  6.8 0.8 copy.22
  7.7 2.2 %copy-done = bf16[4096,512]{1,0:T(8,128)(2,1)S(1)} copy-done((bf16[4096,512]{1,0:T(8,128)(2,1)S(1)}, bf16[4096,512]{1,0:T(8,128)(2,1)}, u32[]{:S(2)}) %copy-start) | copy-done | bytes 4194328
  9.9 3.1 %key_unit.1.refs_2_.refs_4_ = bf16[4096,512]{1,0:T(8,128)(2,1)S(1)} custom-call(bf16[4096,512]{1,0:T(8,128)(2,1)S(1)} %copy-done), custom_call_target="tpu_custom_call" | custom-call | flops 34500001792 | bytes 110700000 | tf_op jit(solution)/shard_map/key_unit/pallas_call | solution.py:116
  13.0 2.0 %copy-done.2 = bf16[4096,512]{1,0:T(8,128)(2,1)} copy-done((bf16[4096,512]{1,0:T(8,128)(2,1)}, bf16[4096,512]{1,0:T(8,128)(2,1)S(1)}, u32[]{:S(2)}) %copy-start.2) | copy-done | bytes 4194328
  15.0 0.6 gather_fusion
  15.8 0.2 fusion.3
  16.1 0.2 compare_reduce_fusion
  16.8 0.6 collective-permute-start.7
  17.4 2.3 %norm_query.1.queries = bf16[256,512]{1,0:T(8,128)(2,1)S(1)} custom-call(s32[4]{0:T(128)S(1)} %get-tuple-element.75.order, bf16[256,512]{1,0:T(8,128)(2,1)S(1)} %copy-done.8, bf16[256,512]{1,0:T(8,128)(2,1)S(1)} %collective-permute-done.x1, bf16[256,512]{1,0:T(8,128)(2,1)S(1)} %collective-permute-done.2.x2, bf16[256,512]{1,0:T(8,128)(2,1)S(1)} %collective-permute-done.1.x3, ...), custom_call_target="tpu_custom_call" | custom-call | flops 17250000896 | bytes 55350000 | tf_op jit(solution)/shard_map/norm_query/pallas_call | solution.py:345
  19.7 4.1 %collective-permute-start.4 = (bf16[256,512]{1,0:T(8,128)(2,1)S(1)}, bf16[256,512]{1,0:T(8,128)(2,1)S(1)}, u32[]{:S(2)}, u32[]{:S(2)}) collective-permute-start(bf16[256,512]{1,0:T(8,128)(2,1)S(1)} %norm_query.1.queries), channel_id=1, source_target_pairs={{0,96},{4,28},{8,104},{12,4},{16,112},{20,12},{24,120},{28,20},{32... | collective-permute-start | bytes 786440 | tf_op jit(solution)/shard_map/ppermute | solution.py:289
  23.8 1.3 %collective-permute-start.3 = (bf16[256,512]{1,0:T(8,128)(2,1)S(1)}, bf16[256,512]{1,0:T(8,128)(2,1)S(1)}, u32[]{:S(2)}, u32[]{:S(2)}) collective-permute-start(bf16[256,512]{1,0:T(8,128)(2,1)S(1)} %norm_query.1.queries), channel_id=1, source_target_pairs={{0,32},{4,12},{8,40},{12,20},{16,48},{20,28},{24,56},{28,4},{32,64... | collective-permute-start | bytes 786440 | tf_op jit(solution)/shard_map/ppermute | solution.py:289
  25.1 3.2 %local_kv.1.kv = bf16[2,256,512]{2,1,0:T(8,128)(2,1)S(1)} custom-call(s32[4]{0:T(128)S(1)} %get-tuple-element.75.order, bf16[256,512]{1,0:T(8,128)(2,1)S(1)} %copy-done.8, bf16[256,512]{1,0:T(8,128)(2,1)S(1)} %collective-permute-done.x1, bf16[256,512]{1,0:T(8,128)(2,1)S(1)} %collective-permute-done.2.x2, bf16[256,512]{1,0:T(8,128)(2,1)S(1)} %collective-permute-done.1.x3, ...), custom_call_target="tpu_custom_call" | custom-call | flops 28750000128 | bytes 92250000 | tf_op jit(solution)/shard_map/local_kv/pallas_call | solution.py:345
  28.3 2.2 %collective-permute-done.4 = bf16[256,512]{1,0:T(8,128)(2,1)S(1)} collective-permute-done((bf16[256,512]{1,0:T(8,128)(2,1)S(1)}, bf16[256,512]{1,0:T(8,128)(2,1)S(1)}, u32[]{:S(2)}, u32[]{:S(2)}) %collective-permute-start.4) | collective-permute-done | bytes 262176 | tf_op jit(solution)/shard_map/ppermute | solution.py:289
  30.5 1.3 %collective-permute-done.5 = bf16[256,512]{1,0:T(8,128)(2,1)S(1)} collective-permute-done((bf16[256,512]{1,0:T(8,128)(2,1)S(1)}, bf16[256,512]{1,0:T(8,128)(2,1)S(1)}, u32[]{:S(2)}, u32[]{:S(2)}) %collective-permute-start.5) | collective-permute-done | bytes 262176 | tf_op jit(solution)/shard_map/ppermute | solution.py:289
  31.9 1.6 %collective-permute-start.11 = (bf16[2,256,512]{2,1,0:T(8,128)(2,1)S(1)}, bf16[2,256,512]{2,1,0:T(8,128)(2,1)S(1)}, u32[]{:S(2)}, u32[]{:S(2)}) collective-permute-start(bf16[2,256,512]{2,1,0:T(8,128)(2,1)S(1)} %pad_maximum_fusion.1.refs_1_), channel_id=1, source_target_pairs={{0,8},{4,36},{8,16},{12,44},{16,24},{20,52},{24,0},{28,60},{32,40}... | collective-permute-start | bytes 1572872 | tf_op jit(solution)/shard_map/ppermute | solution.py:294
  33.5 1.7 %collective-permute-start.9 = (bf16[2,256,512]{2,1,0:T(8,128)(2,1)S(1)}, bf16[2,256,512]{2,1,0:T(8,128)(2,1)S(1)}, u32[]{:S(2)}, u32[]{:S(2)}) collective-permute-start(bf16[2,256,512]{2,1,0:T(8,128)(2,1)S(1)} %pad_maximum_fusion.1.refs_1_), channel_id=1, source_target_pairs={{0,24},{4,100},{8,0},{12,108},{16,8},{20,116},{24,16},{28,124},{32... | collective-permute-start | bytes 1572872 | tf_op jit(solution)/shard_map/ppermute | solution.py:294
  35.2 2.1 %collective-permute-start.10 = (bf16[2,256,512]{2,1,0:T(8,128)(2,1)S(1)}, bf16[2,256,512]{2,1,0:T(8,128)(2,1)S(1)}, u32[]{:S(2)}, u32[]{:S(2)}) collective-permute-start(bf16[2,256,512]{2,1,0:T(8,128)(2,1)S(1)} %pad_maximum_fusion.refs_0_), channel_id=1, source_target_pairs={{0,24},{4,100},{8,0},{12,108},{16,8},{20,116},{24,16},{28,124},{32... | collective-permute-start | bytes 1572872 | tf_op jit(solution)/shard_map/ppermute | solution.py:294
  37.4 1.9 %memory_attention.3.z = bf16[4,272,512]{2,1,0:T(8,128)(2,1)S(1)} custom-call(s32[96]{0:T(128)S(1)} %reshape.299.meta, f32[4]{0:T(128)S(1)} %copy-done.10, bf16[2,256,512]{2,1,0:T(8,128)(2,1)S(1)} %pad_maximum_fusion.refs_0_, bf16[2,256,512]{2,1,0:T(8,128)(2,1)S(1)} %pad_maximum_fusion.1.refs_1_, bf16[4096,512]{1,0:T(8,128)(2,1)S(1)} %copy-done.3, ...), custom_call_target="tpu_custom_call" | custom-call | flops 34500001792 | bytes 110700000 | tf_op jit(solution)/shard_map/memory_attention/pallas_call | solution.py:235
  39.4 3.0 %collective-permute-done.11.refs_1_ = bf16[2,256,512]{2,1,0:T(8,128)(2,1)S(1)} collective-permute-done((bf16[2,256,512]{2,1,0:T(8,128)(2,1)S(1)}, bf16[2,256,512]{2,1,0:T(8,128)(2,1)S(1)}, u32[]{:S(2)}, u32[]{:S(2)}) %collective-permute-start.11) | collective-permute-done | bytes 524320 | tf_op jit(solution)/shard_map/ppermute | solution.py:294
  42.3 0.4 collective-permute-done.9.refs_3_
  42.7 5.6 %collective-permute-done.10.refs_2_ = bf16[2,256,512]{2,1,0:T(8,128)(2,1)S(1)} collective-permute-done((bf16[2,256,512]{2,1,0:T(8,128)(2,1)S(1)}, bf16[2,256,512]{2,1,0:T(8,128)(2,1)S(1)}, u32[]{:S(2)}, u32[]{:S(2)}) %collective-permute-start.10) | collective-permute-done | bytes 524320 | tf_op jit(solution)/shard_map/ppermute | solution.py:294
  48.3 1.6 %collective-permute-start.14 = (bf16[2,256,512]{2,1,0:T(8,128)(2,1)S(1)}, bf16[2,256,512]{2,1,0:T(8,128)(2,1)S(1)}, u32[]{:S(2)}, u32[]{:S(2)}) collective-permute-start(bf16[2,256,512]{2,1,0:T(8,128)(2,1)S(1)} %collective-permute-done.8.refs_0_), channel_id=1, source_target_pairs={{0,8},{4,36},{8,16},{12,44},{16,24},{20,52},{24,0},{28,60},{32,40}... | collective-permute-start | bytes 1572872 | tf_op jit(solution)/shard_map/ppermute | solution.py:294
  49.9 1.7 %collective-permute-start.15 = (bf16[2,256,512]{2,1,0:T(8,128)(2,1)S(1)}, bf16[2,256,512]{2,1,0:T(8,128)(2,1)S(1)}, u32[]{:S(2)}, u32[]{:S(2)}) collective-permute-start(bf16[2,256,512]{2,1,0:T(8,128)(2,1)S(1)} %collective-permute-done.9.refs_3_), channel_id=1, source_target_pairs={{0,24},{4,100},{8,0},{12,108},{16,8},{20,116},{24,16},{28,124},{32... | collective-permute-start | bytes 1572872 | tf_op jit(solution)/shard_map/ppermute | solution.py:294
  51.5 1.3 %collective-permute-start.16 = (bf16[2,256,512]{2,1,0:T(8,128)(2,1)S(1)}, bf16[2,256,512]{2,1,0:T(8,128)(2,1)S(1)}, u32[]{:S(2)}, u32[]{:S(2)}) collective-permute-start(bf16[2,256,512]{2,1,0:T(8,128)(2,1)S(1)} %local_kv.1.kv), channel_id=1, source_target_pairs={{0,4},{4,8},{8,12},{12,16},{16,20},{20,24},{24,28},{28,32},{32,36}... | collective-permute-start | bytes 1572872 | tf_op jit(solution)/shard_map/ppermute | solution.py:450
  52.9 4.7 %memory_attention.4 = (bf16[4,272,512]{2,1,0:T(8,128)(2,1)S(1)}, bf16[4,272,512]{2,1,0:T(8,128)(2,1)S(1)}) custom-call(s32[96]{0:T(128)S(1)} %reshape.299.meta, f32[4]{0:T(128)S(1)} %copy-done.10, bf16[2,256,512]{2,1,0:T(8,128)(2,1)S(1)} %collective-permute-done.8.refs_0_, bf16[2,256,512]{2,1,0:T(8,128)(2,1)S(1)} %collective-permute-done.11.refs_1_, ...), custom_call_target="tpu_custom_call" | custom-call | flops 69000003584 | bytes 221400000 | tf_op jit(solution)/shard_map/memory_attention/pallas_call | solution.py:235
  57.6 1.0 collective-permute-start.12
  58.6 2.3 %collective-permute-start.13 = (bf16[4,272,512]{2,1,0:T(8,128)(2,1)S(1)}, bf16[4,272,512]{2,1,0:T(8,128)(2,1)S(1)}, u32[]{:S(2)}, u32[]{:S(2)}) collective-permute-start(bf16[4,272,512]{2,1,0:T(8,128)(2,1)S(1)} %get-tuple-element.52), channel_id=1, source_target_pairs={{0,24},{4,100},{8,0},{12,108},{16,8},{20,116},{24,16},{28,124},{32... | collective-permute-start | bytes 3342344 | tf_op jit(solution)/shard_map/ppermute | solution.py:294
  60.9 2.8 %memory_attention.5 = bf16[4,272,512]{2,1,0:T(8,128)(2,1)S(1)} custom-call(s32[96]{0:T(128)S(1)} %reshape.299.meta, f32[4]{0:T(128)S(1)} %copy-done.10, bf16[2,256,512]{2,1,0:T(8,128)(2,1)S(1)} %collective-permute-done.14.refs_0_, bf16[2,256,512]{2,1,0:T(8,128)(2,1)S(1)} %collective-permute-done.15.refs_1_, bf16[4096,512]{1,0:T(8,128)(2,1)S(1)} %copy-done.3, ...), custom_call_target="tpu_custom_call" | custom-call | flops 34500001792 | bytes 110700000 | tf_op jit(solution)/shard_map/memory_attention/pallas_call | solution.py:235
  63.8 6.7 %collective-permute-start.17 = (bf16[4,272,512]{2,1,0:T(8,128)(2,1)S(1)}, bf16[4,272,512]{2,1,0:T(8,128)(2,1)S(1)}, u32[]{:S(2)}, u32[]{:S(2)}) collective-permute-start(bf16[4,272,512]{2,1,0:T(8,128)(2,1)S(1)} %memory_attention.5), channel_id=1, source_target_pairs={{0,16},{4,68},{8,24},{12,76},{16,0},{20,84},{24,8},{28,92},{32,48}... | collective-permute-start | bytes 3342344 | tf_op jit(solution)/shard_map/ppermute | solution.py:294
  70.5 1.7 %local_attention.1.local = f32[256,512]{1,0:T(8,128)S(1)} custom-call(s32[1]{0:T(128)} %bitcast.1.index, f32[4]{0:T(128)S(1)} %copy-done.10, s32[64,128]{1,0:T(8,128)S(1)} %bitcast.28, bf16[256,512]{1,0:T(8,128)(2,1)S(1)} %norm_query.1.queries, bf16[2,256,512]{2,1,0:T(8,128)(2,1)S(1)} %local_kv.1.kv, bf16[2,256,512]{2,1,0:T(8,128)(2,1)S(1)} %collective-permute-done.16.before), custom_call_target="tpu_custom_call" | custom-call | flops 17250000896 | bytes 55350000 | tf_op jit(solution)/shard_map/local_attention/pallas_call | solution.py:345
  72.2 4.1 %collective-permute-done.12.u = bf16[4,272,512]{2,1,0:T(8,128)(2,1)S(1)} collective-permute-done((bf16[4,272,512]{2,1,0:T(8,128)(2,1)S(1)}, bf16[4,272,512]{2,1,0:T(8,128)(2,1)S(1)}, u32[]{:S(2)}, u32[]{:S(2)}) %collective-permute-start.12) | collective-permute-done | bytes 1114144 | tf_op jit(solution)/shard_map/ppermute | solution.py:294
  76.3 9.6 %collective-permute-done.13.v = bf16[4,272,512]{2,1,0:T(8,128)(2,1)S(1)} collective-permute-done((bf16[4,272,512]{2,1,0:T(8,128)(2,1)S(1)}, bf16[4,272,512]{2,1,0:T(8,128)(2,1)S(1)}, u32[]{:S(2)}, u32[]{:S(2)}) %collective-permute-start.13) | collective-permute-done | bytes 1114144 | tf_op jit(solution)/shard_map/ppermute | solution.py:294
  85.9 3.4 %collective-permute-done.17.s = bf16[4,272,512]{2,1,0:T(8,128)(2,1)S(1)} collective-permute-done((bf16[4,272,512]{2,1,0:T(8,128)(2,1)S(1)}, bf16[4,272,512]{2,1,0:T(8,128)(2,1)S(1)}, u32[]{:S(2)}, u32[]{:S(2)}) %collective-permute-start.17) | collective-permute-done | bytes 1114144 | tf_op jit(solution)/shard_map/ppermute | solution.py:294
  89.3 0.5 fusion.2
  89.8 2.5 %collective-permute-start.18 = (bf16[272,512]{1,0:T(8,128)(2,1)S(1)}, bf16[272,512]{1,0:T(8,128)(2,1)S(1)}, u32[]{:S(2)}, u32[]{:S(2)}) collective-permute-start(bf16[272,512]{1,0:T(8,128)(2,1)S(1)} %get-tuple-element.71), channel_id=1, source_target_pairs={{0,96},{4,28},{8,104},{12,4},{16,112},{20,12},{24,120},{28,20},{32... | collective-permute-start | bytes 835592 | tf_op jit(solution)/shard_map/ppermute | solution.py:289
  92.3 1.5 %collective-permute-start.20 = (bf16[272,512]{1,0:T(8,128)(2,1)S(1)}, bf16[272,512]{1,0:T(8,128)(2,1)S(1)}, u32[]{:S(2)}, u32[]{:S(2)}) collective-permute-start(bf16[272,512]{1,0:T(8,128)(2,1)S(1)} %get-tuple-element.69), channel_id=1, source_target_pairs={{0,64},{4,20},{8,72},{12,28},{16,80},{20,4},{24,88},{28,12},{32,96... | collective-permute-start | bytes 835592 | tf_op jit(solution)/shard_map/ppermute | solution.py:289
  93.8 2.6 %collective-permute-done.18.x1 = bf16[272,512]{1,0:T(8,128)(2,1)S(1)} collective-permute-done((bf16[272,512]{1,0:T(8,128)(2,1)S(1)}, bf16[272,512]{1,0:T(8,128)(2,1)S(1)}, u32[]{:S(2)}, u32[]{:S(2)}) %collective-permute-start.18) | collective-permute-done | bytes 278560 | tf_op jit(solution)/shard_map/ppermute | solution.py:289
  96.4 6.6 %collective-permute-done.19.x2 = bf16[272,512]{1,0:T(8,128)(2,1)S(1)} collective-permute-done((bf16[272,512]{1,0:T(8,128)(2,1)S(1)}, bf16[272,512]{1,0:T(8,128)(2,1)S(1)}, u32[]{:S(2)}, u32[]{:S(2)}) %collective-permute-start.19) | collective-permute-done | bytes 278560 | tf_op jit(solution)/shard_map/ppermute | solution.py:289
  103.0 2.8 %merge_output.1 = (bf16[64,2048]{1,0:T(8,128)(2,1)S(1)}, bf16[64,2048]{1,0:T(8,128)(2,1)S(1)}, bf16[64,2048]{1,0:T(8,128)(2,1)S(1)}, bf16[64,2048]{1,0:T(8,128)(2,1)S(1)}) custom-call(s32[4]{0:T(128)S(1)} %get-tuple-element.75.order, f32[4]{0:T(128)S(1)} %copy-done.11, bf16[4,272,512]{2,1,0:T(8,128)(2,1)S(1)} %memory_attention.3.z, ...), custom_call_target="tpu_custom_call" | custom-call | flops 28750000128 | bytes 92250000 | tf_op jit(solution)/shard_map/merge_output/pallas_call | solution.py:345
  105.8 0.7 collective-permute-start.21
  106.5 2.6 %collective-permute-start.22 = (bf16[64,2048]{1,0:T(8,128)(2,1)S(1)}, bf16[64,2048]{1,0:T(8,128)(2,1)S(1)}, u32[]{:S(2)}, u32[]{:S(2)}) collective-permute-start(bf16[64,2048]{1,0:T(8,128)(2,1)S(1)} %get-tuple-element.65), channel_id=1, source_target_pairs={{0,3},{1,0},{2,1},{3,2},{4,7},{5,4},{6,5},{7,6},{8,11},{9,8},{10,9... | collective-permute-start | bytes 786440 | tf_op jit(solution)/shard_map/ppermute | solution.py:302
  109.1 0.2 collective-permute-start.23
  109.3 9.5 %collective-permute-done.21 = bf16[64,2048]{1,0:T(8,128)(2,1)S(1)} collective-permute-done((bf16[64,2048]{1,0:T(8,128)(2,1)S(1)}, bf16[64,2048]{1,0:T(8,128)(2,1)S(1)}, u32[]{:S(2)}, u32[]{:S(2)}) %collective-permute-start.21) | collective-permute-done | bytes 262176 | tf_op jit(solution)/shard_map/ppermute | solution.py:302
  118.8 0.8 add_convert_fusion.3
  (64 shorter events, 1.5 us)
Async XLA Ops:
  0.0 16.7 %collective-permute-start = (bf16[256,512]{1,0:T(8,128)(2,1)}, bf16[256,512]{1,0:T(8,128)(2,1)S(1)}, u32[]{:S(2)}, u32[]{:S(2)}) collective-permute-start(bf16[256,512]{1,0:T(8,128)(2,1)} %x0.3), channel_id=1, source_target_pairs={{0,1},{1,2},{2,3},{3,0},{4,5},{5,6},{6,7},{7,4},{8,9},{9,10},{10,1... | collective-permute-start | bytes 786440 | tf_op jit(solution)/shard_map/ppermute | solution.py:302
  1.6 15.2 %collective-permute-start.1 = (bf16[256,512]{1,0:T(8,128)(2,1)}, bf16[256,512]{1,0:T(8,128)(2,1)S(1)}, u32[]{:S(2)}, u32[]{:S(2)}) collective-permute-start(bf16[256,512]{1,0:T(8,128)(2,1)} %x0.3), channel_id=1, source_target_pairs={{0,2},{1,3},{2,0},{3,1},{4,6},{5,7},{6,4},{7,5},{8,10},{9,11},{10,... | collective-permute-start | bytes 786440 | tf_op jit(solution)/shard_map/ppermute | solution.py:302
  4.3 13.1 %collective-permute-start.2 = (bf16[256,512]{1,0:T(8,128)(2,1)}, bf16[256,512]{1,0:T(8,128)(2,1)S(1)}, u32[]{:S(2)}, u32[]{:S(2)}) collective-permute-start(bf16[256,512]{1,0:T(8,128)(2,1)} %x0.3), channel_id=1, source_target_pairs={{0,3},{1,0},{2,1},{3,2},{4,7},{5,4},{6,5},{7,6},{8,11},{9,8},{10,9... | collective-permute-start | bytes 786440 | tf_op jit(solution)/shard_map/ppermute | solution.py:302
  7.7 2.2 %copy-start = (bf16[4096,512]{1,0:T(8,128)(2,1)S(1)}, bf16[4096,512]{1,0:T(8,128)(2,1)}, u32[]{:S(2)}) copy-start(bf16[4096,512]{1,0:T(8,128)(2,1)} %raw.1) | copy-start | bytes 12582916
  9.9 6.8 %copy-start.12 = (bf16[2048]{0:T(1024)(128)(2,1)S(1)}, bf16[2048]{0:T(1024)(128)(2,1)}, u32[]{:S(2)}) copy-start(bf16[2048]{0:T(1024)(128)(2,1)} %param.16) | copy-start | bytes 12292
  9.9 7.5 %copy-start.4 = (bf16[2048,512]{1,0:T(8,128)(2,1)S(1)}, bf16[2048,512]{1,0:T(8,128)(2,1)}, u32[]{:S(2)}) copy-start(bf16[2048,512]{1,0:T(8,128)(2,1)} %param.17) | copy-start | bytes 6291460
  9.9 7.5 %copy-start.8 = (bf16[256,512]{1,0:T(8,128)(2,1)S(1)}, bf16[256,512]{1,0:T(8,128)(2,1)}, u32[]{:S(2)}) copy-start(bf16[256,512]{1,0:T(8,128)(2,1)} %x0.3) | copy-start | bytes 786436
  13.0 2.0 %copy-start.2 = (bf16[4096,512]{1,0:T(8,128)(2,1)}, bf16[4096,512]{1,0:T(8,128)(2,1)S(1)}, u32[]{:S(2)}) copy-start(bf16[4096,512]{1,0:T(8,128)(2,1)S(1)} %key_unit.1.refs_2_.refs_4_) | copy-start | bytes 12582916
  16.7 20.6 %collective-permute-start.6 = (bf16[4096,512]{1,0:T(8,128)(2,1)}, bf16[4096,512]{1,0:T(8,128)(2,1)S(1)}, u32[]{:S(2)}, u32[]{:S(2)}) collective-permute-start(bf16[4096,512]{1,0:T(8,128)(2,1)} %copy-done.2), channel_id=1, source_target_pairs={{0,4},{4,0},{8,12},{12,8},{16,20},{20,16},{24,28},{28,24},{32,36},... | collective-permute-start | bytes 12582920 | tf_op jit(solution)/shard_map/ppermute | solution.py:298
  16.8 20.5 %collective-permute-start.7 = (bf16[4096,512]{1,0:T(8,128)(2,1)}, bf16[4096,512]{1,0:T(8,128)(2,1)S(1)}, u32[]{:S(2)}, u32[]{:S(2)}) collective-permute-start(bf16[4096,512]{1,0:T(8,128)(2,1)} %refs_3_.1), channel_id=1, source_target_pairs={{0,4},{4,0},{8,12},{12,8},{16,20},{20,16},{24,28},{28,24},{32,36},... | collective-permute-start | bytes 12582920 | tf_op jit(solution)/shard_map/ppermute | solution.py:298
  17.4 7.7 %copy-start.5 = (bf16[2048,512]{1,0:T(8,128)(2,1)S(1)}, bf16[2048,512]{1,0:T(8,128)(2,1)}, u32[]{:S(2)}) copy-start(bf16[2048,512]{1,0:T(8,128)(2,1)} %param.18) | copy-start | bytes 6291460
  17.4 7.7 %copy-start.6 = (bf16[2048,512]{1,0:T(8,128)(2,1)S(1)}, bf16[2048,512]{1,0:T(8,128)(2,1)}, u32[]{:S(2)}) copy-start(bf16[2048,512]{1,0:T(8,128)(2,1)} %param.19) | copy-start | bytes 6291460
  19.7 10.8 %collective-permute-start.4 = (bf16[256,512]{1,0:T(8,128)(2,1)S(1)}, bf16[256,512]{1,0:T(8,128)(2,1)S(1)}, u32[]{:S(2)}, u32[]{:S(2)}) collective-permute-start(bf16[256,512]{1,0:T(8,128)(2,1)S(1)} %norm_query.1.queries), channel_id=1, source_target_pairs={{0,96},{4,28},{8,104},{12,4},{16,112},{20,12},{24,120},{28,20},{32... | collective-permute-start | bytes 786440 | tf_op jit(solution)/shard_map/ppermute | solution.py:289
  23.8 8.0 %collective-permute-start.5 = (bf16[256,512]{1,0:T(8,128)(2,1)S(1)}, bf16[256,512]{1,0:T(8,128)(2,1)S(1)}, u32[]{:S(2)}, u32[]{:S(2)}) collective-permute-start(bf16[256,512]{1,0:T(8,128)(2,1)S(1)} %norm_query.1.queries), channel_id=1, source_target_pairs={{0,64},{4,20},{8,72},{12,28},{16,80},{20,4},{24,88},{28,12},{32,96... | collective-permute-start | bytes 786440 | tf_op jit(solution)/shard_map/ppermute | solution.py:289
  23.8 11.3 %collective-permute-start.3 = (bf16[256,512]{1,0:T(8,128)(2,1)S(1)}, bf16[256,512]{1,0:T(8,128)(2,1)S(1)}, u32[]{:S(2)}, u32[]{:S(2)}) collective-permute-start(bf16[256,512]{1,0:T(8,128)(2,1)S(1)} %norm_query.1.queries), channel_id=1, source_target_pairs={{0,32},{4,12},{8,40},{12,20},{16,48},{20,28},{24,56},{28,4},{32,64... | collective-permute-start | bytes 786440 | tf_op jit(solution)/shard_map/ppermute | solution.py:289
  25.1 12.3 %copy-start.1 = (bf16[4096,512]{1,0:T(8,128)(2,1)S(1)}, bf16[4096,512]{1,0:T(8,128)(2,1)}, u32[]{:S(2)}) copy-start(bf16[4096,512]{1,0:T(8,128)(2,1)} %refs_3_.1) | copy-start | bytes 12582916
  25.1 12.3 %copy-start.3 = (bf16[4096,512]{1,0:T(8,128)(2,1)S(1)}, bf16[4096,512]{1,0:T(8,128)(2,1)}, u32[]{:S(2)}) copy-start(bf16[4096,512]{1,0:T(8,128)(2,1)} %copy-done.2) | copy-start | bytes 12582916
  28.3 9.1 %copy-start.10 = (f32[4]{0:T(128)S(1)}, f32[4]{0:T(128)}, u32[]{:S(2)}) copy-start(f32[4]{0:T(128)} %sharp.7) | copy-start | bytes 52
  31.9 10.5 %collective-permute-start.11 = (bf16[2,256,512]{2,1,0:T(8,128)(2,1)S(1)}, bf16[2,256,512]{2,1,0:T(8,128)(2,1)S(1)}, u32[]{:S(2)}, u32[]{:S(2)}) collective-permute-start(bf16[2,256,512]{2,1,0:T(8,128)(2,1)S(1)} %pad_maximum_fusion.1.refs_1_), channel_id=1, source_target_pairs={{0,8},{4,36},{8,16},{12,44},{16,24},{20,52},{24,0},{28,60},{32,40}... | collective-permute-start | bytes 1572872 | tf_op jit(solution)/shard_map/ppermute | solution.py:294
  33.5 9.2 %collective-permute-start.9 = (bf16[2,256,512]{2,1,0:T(8,128)(2,1)S(1)}, bf16[2,256,512]{2,1,0:T(8,128)(2,1)S(1)}, u32[]{:S(2)}, u32[]{:S(2)}) collective-permute-start(bf16[2,256,512]{2,1,0:T(8,128)(2,1)S(1)} %pad_maximum_fusion.1.refs_1_), channel_id=1, source_target_pairs={{0,24},{4,100},{8,0},{12,108},{16,8},{20,116},{24,16},{28,124},{32... | collective-permute-start | bytes 1572872 | tf_op jit(solution)/shard_map/ppermute | solution.py:294
  35.2 13.1 %collective-permute-start.10 = (bf16[2,256,512]{2,1,0:T(8,128)(2,1)S(1)}, bf16[2,256,512]{2,1,0:T(8,128)(2,1)S(1)}, u32[]{:S(2)}, u32[]{:S(2)}) collective-permute-start(bf16[2,256,512]{2,1,0:T(8,128)(2,1)S(1)} %pad_maximum_fusion.refs_0_), channel_id=1, source_target_pairs={{0,24},{4,100},{8,0},{12,108},{16,8},{20,116},{24,16},{28,124},{32... | collective-permute-start | bytes 1572872 | tf_op jit(solution)/shard_map/ppermute | solution.py:294
  37.4 10.9 %collective-permute-start.8 = (bf16[2,256,512]{2,1,0:T(8,128)(2,1)S(1)}, bf16[2,256,512]{2,1,0:T(8,128)(2,1)S(1)}, u32[]{:S(2)}, u32[]{:S(2)}) collective-permute-start(bf16[2,256,512]{2,1,0:T(8,128)(2,1)S(1)} %pad_maximum_fusion.refs_0_), channel_id=1, source_target_pairs={{0,8},{4,36},{8,16},{12,44},{16,24},{20,52},{24,0},{28,60},{32,40}... | collective-permute-start | bytes 1572872 | tf_op jit(solution)/shard_map/ppermute | solution.py:294
  48.3 12.6 %collective-permute-start.14 = (bf16[2,256,512]{2,1,0:T(8,128)(2,1)S(1)}, bf16[2,256,512]{2,1,0:T(8,128)(2,1)S(1)}, u32[]{:S(2)}, u32[]{:S(2)}) collective-permute-start(bf16[2,256,512]{2,1,0:T(8,128)(2,1)S(1)} %collective-permute-done.8.refs_0_), channel_id=1, source_target_pairs={{0,8},{4,36},{8,16},{12,44},{16,24},{20,52},{24,0},{28,60},{32,40}... | collective-permute-start | bytes 1572872 | tf_op jit(solution)/shard_map/ppermute | solution.py:294
  49.9 11.0 %collective-permute-start.15 = (bf16[2,256,512]{2,1,0:T(8,128)(2,1)S(1)}, bf16[2,256,512]{2,1,0:T(8,128)(2,1)S(1)}, u32[]{:S(2)}, u32[]{:S(2)}) collective-permute-start(bf16[2,256,512]{2,1,0:T(8,128)(2,1)S(1)} %collective-permute-done.9.refs_3_), channel_id=1, source_target_pairs={{0,24},{4,100},{8,0},{12,108},{16,8},{20,116},{24,16},{28,124},{32... | collective-permute-start | bytes 1572872 | tf_op jit(solution)/shard_map/ppermute | solution.py:294
  51.5 9.4 %collective-permute-start.16 = (bf16[2,256,512]{2,1,0:T(8,128)(2,1)S(1)}, bf16[2,256,512]{2,1,0:T(8,128)(2,1)S(1)}, u32[]{:S(2)}, u32[]{:S(2)}) collective-permute-start(bf16[2,256,512]{2,1,0:T(8,128)(2,1)S(1)} %local_kv.1.kv), channel_id=1, source_target_pairs={{0,4},{4,8},{8,12},{12,16},{16,20},{20,24},{24,28},{28,32},{32,36}... | collective-permute-start | bytes 1572872 | tf_op jit(solution)/shard_map/ppermute | solution.py:450
  57.6 18.7 %collective-permute-start.12 = (bf16[4,272,512]{2,1,0:T(8,128)(2,1)S(1)}, bf16[4,272,512]{2,1,0:T(8,128)(2,1)S(1)}, u32[]{:S(2)}, u32[]{:S(2)}) collective-permute-start(bf16[4,272,512]{2,1,0:T(8,128)(2,1)S(1)} %get-tuple-element.51), channel_id=1, source_target_pairs={{0,8},{4,36},{8,16},{12,44},{16,24},{20,52},{24,0},{28,60},{32,40}... | collective-permute-start | bytes 3342344 | tf_op jit(solution)/shard_map/ppermute | solution.py:294
  58.6 11.9 %copy-start.9 = (s32[8192]{0:T(1024)S(1)}, s32[8192]{0:T(1024)}, u32[]{:S(2)}) copy-start(s32[8192]{0:T(1024)} %param.26) | copy-start | bytes 98308
  58.6 27.3 %collective-permute-start.13 = (bf16[4,272,512]{2,1,0:T(8,128)(2,1)S(1)}, bf16[4,272,512]{2,1,0:T(8,128)(2,1)S(1)}, u32[]{:S(2)}, u32[]{:S(2)}) collective-permute-start(bf16[4,272,512]{2,1,0:T(8,128)(2,1)S(1)} %get-tuple-element.52), channel_id=1, source_target_pairs={{0,24},{4,100},{8,0},{12,108},{16,8},{20,116},{24,16},{28,124},{32... | collective-permute-start | bytes 3342344 | tf_op jit(solution)/shard_map/ppermute | solution.py:294
  63.8 25.5 %collective-permute-start.17 = (bf16[4,272,512]{2,1,0:T(8,128)(2,1)S(1)}, bf16[4,272,512]{2,1,0:T(8,128)(2,1)S(1)}, u32[]{:S(2)}, u32[]{:S(2)}) collective-permute-start(bf16[4,272,512]{2,1,0:T(8,128)(2,1)S(1)} %memory_attention.5), channel_id=1, source_target_pairs={{0,16},{4,68},{8,24},{12,76},{16,0},{20,84},{24,8},{28,92},{32,48}... | collective-permute-start | bytes 3342344 | tf_op jit(solution)/shard_map/ppermute | solution.py:294
  72.2 30.8 %copy-start.7 = (bf16[512,2048]{1,0:T(8,128)(2,1)S(1)}, bf16[512,2048]{1,0:T(8,128)(2,1)}, u32[]{:S(2)}) copy-start(bf16[512,2048]{1,0:T(8,128)(2,1)} %weight.1) | copy-start | bytes 6291460
  72.2 30.8 %copy-start.11 = (f32[4]{0:T(128)S(1)}, f32[4]{0:T(128)}, u32[]{:S(2)}) copy-start(f32[4]{0:T(128)} %bias.1) | copy-start | bytes 52
  89.8 6.6 %collective-permute-start.18 = (bf16[272,512]{1,0:T(8,128)(2,1)S(1)}, bf16[272,512]{1,0:T(8,128)(2,1)S(1)}, u32[]{:S(2)}, u32[]{:S(2)}) collective-permute-start(bf16[272,512]{1,0:T(8,128)(2,1)S(1)} %get-tuple-element.71), channel_id=1, source_target_pairs={{0,96},{4,28},{8,104},{12,4},{16,112},{20,12},{24,120},{28,20},{32... | collective-permute-start | bytes 835592 | tf_op jit(solution)/shard_map/ppermute | solution.py:289
  92.3 10.7 %collective-permute-start.19 = (bf16[272,512]{1,0:T(8,128)(2,1)S(1)}, bf16[272,512]{1,0:T(8,128)(2,1)S(1)}, u32[]{:S(2)}, u32[]{:S(2)}) collective-permute-start(bf16[272,512]{1,0:T(8,128)(2,1)S(1)} %get-tuple-element.70), channel_id=1, source_target_pairs={{0,32},{4,12},{8,40},{12,20},{16,48},{20,28},{24,56},{28,4},{32,64... | collective-permute-start | bytes 835592 | tf_op jit(solution)/shard_map/ppermute | solution.py:289
  92.3 10.7 %collective-permute-start.20 = (bf16[272,512]{1,0:T(8,128)(2,1)S(1)}, bf16[272,512]{1,0:T(8,128)(2,1)S(1)}, u32[]{:S(2)}, u32[]{:S(2)}) collective-permute-start(bf16[272,512]{1,0:T(8,128)(2,1)S(1)} %get-tuple-element.69), channel_id=1, source_target_pairs={{0,64},{4,20},{8,72},{12,28},{16,80},{20,4},{24,88},{28,12},{32,96... | collective-permute-start | bytes 835592 | tf_op jit(solution)/shard_map/ppermute | solution.py:289
  105.8 13.0 %collective-permute-start.21 = (bf16[64,2048]{1,0:T(8,128)(2,1)S(1)}, bf16[64,2048]{1,0:T(8,128)(2,1)S(1)}, u32[]{:S(2)}, u32[]{:S(2)}) collective-permute-start(bf16[64,2048]{1,0:T(8,128)(2,1)S(1)} %get-tuple-element.64), channel_id=1, source_target_pairs={{0,1},{1,2},{2,3},{3,0},{4,5},{5,6},{6,7},{7,4},{8,9},{9,10},{10,1... | collective-permute-start | bytes 786440 | tf_op jit(solution)/shard_map/ppermute | solution.py:302
  106.5 12.3 %collective-permute-start.22 = (bf16[64,2048]{1,0:T(8,128)(2,1)S(1)}, bf16[64,2048]{1,0:T(8,128)(2,1)S(1)}, u32[]{:S(2)}, u32[]{:S(2)}) collective-permute-start(bf16[64,2048]{1,0:T(8,128)(2,1)S(1)} %get-tuple-element.65), channel_id=1, source_target_pairs={{0,3},{1,0},{2,1},{3,2},{4,7},{5,4},{6,5},{7,6},{8,11},{9,8},{10,9... | collective-permute-start | bytes 786440 | tf_op jit(solution)/shard_map/ppermute | solution.py:302
  109.1 9.7 %collective-permute-start.23 = (bf16[64,2048]{1,0:T(8,128)(2,1)S(1)}, bf16[64,2048]{1,0:T(8,128)(2,1)S(1)}, u32[]{:S(2)}, u32[]{:S(2)}) collective-permute-start(bf16[64,2048]{1,0:T(8,128)(2,1)S(1)} %get-tuple-element.66), channel_id=1, source_target_pairs={{0,2},{1,3},{2,0},{3,1},{4,6},{5,7},{6,4},{7,5},{8,10},{9,11},{10,... | collective-permute-start | bytes 786440 | tf_op jit(solution)/shard_map/ppermute | solution.py:302
